TPU v7x, 32 devices: a whole 2x2x4 slice. The times are simulated.
32 devices in a mesh: group: 2 (over x), dp: 4 (over y, core), mp: 4 (over z).
Axes of the slice: x: 2, y: 2, z: 4, core: 2. Of those that a mesh axis runs over, the one named last changes fastest.
Arguments:
- query_passage_words: int32 [2, 12, 128], P('group'), may hold values from 0 to 16383, as said below
- difficult_distractors: int32 [12, 7], P('dp'), may hold values from 0 to 11
- vocabulary_vectors: bfloat16 [4096, 16384], P('dp'), may hold values from -6 to 6
- layer_weight_matrix: bfloat16 [4096, 4096], P('dp', 'mp'), may hold values from -0.09375 to 0.09375
- lowering_factor_matrix: bfloat16 [16, 4096], replicated, may hold values from -0.09375 to 0.09375
- raising_factor_matrix: bfloat16 [16, 4096], P(None, 'mp'), may hold values from -1.5 to 1.5
- logit_sharpness: float32 [1], replicated, may hold values from 10 to 500
Outputs:
- embeddings: bfloat16 [2, 12, 4096], P('group', 'dp', 'mp')
- losses: float32 [2, 12], P('group', 'dp')
- adapter_up_gradient: float32 [16, 4096], P(None, 'mp')
Inputs may be any that keep to these rules, and one draw needn't show every extreme that they name: `query_passage_words`: id 0 is padding and fills only the end of a text; every text has at least 16 real tokens, and the first text of each side has 128. A query shares about half of its token slots with its paired passage.
All inputs are finite; a program needn't handle non-finite values.
Results may differ from a plain program's by a relative error of at most 0.018.
Values may be sent and summed in bfloat16 or wider, within the bound.
No kernel may reach another device: no remote copies, remote signals or barrier semaphores. Data moves between devices by JAX's collectives and lax.ppermute only.
A program may use at most 192 MiB of HBM per device.

v0:
```python
import jax
import jax.numpy as jnp
from jax import lax
from jax.sharding import PartitionSpec as P


def body(
    query_passage_words,
    difficult_distractors,
    vocabulary_vectors,
    layer_weight_matrix,
    lowering_factor_matrix,
    raising_factor_matrix,
    logit_sharpness,
):
    group_index = lax.axis_index("group")
    shard_index = lax.axis_index("dp")
    part_index = lax.axis_index("mp")
    shard_count = lax.axis_size("dp")
    side_ids = query_passage_words[0]
    text_count = side_ids.shape[0]
    length = side_ids.shape[1]
    per_shard = text_count // shard_count
    own_ids = lax.dynamic_slice_in_dim(side_ids, shard_index * per_shard, per_shard, 0)
    columns = jnp.take(vocabulary_vectors, side_ids.reshape(-1), axis=1)
    inputs = lax.all_to_all(columns, "dp", split_axis=1, concat_axis=0, tiled=True)
    tokens = inputs.shape[1]
    feature_width = raising_factor_matrix.shape[1]
    wide_inputs = inputs.astype(jnp.float32)
    inverse = lax.rsqrt(jnp.mean(wide_inputs * wide_inputs, axis=0) + 1e-05)
    normed_state = (wide_inputs * inverse[None, :]).astype(jnp.bfloat16)
    linear_map = lax.dot_general(
        lax.all_gather(layer_weight_matrix, "dp", axis=0, tiled=True),
        normed_state,
        (((0,), (0,)), ((), ())),
        preferred_element_type=jnp.float32,
    )
    reduced_sum = jnp.dot(
        lowering_factor_matrix, normed_state, preferred_element_type=jnp.float32
    ).astype(jnp.bfloat16)
    linear_map = linear_map + lax.dot_general(
        raising_factor_matrix,
        reduced_sum,
        (((0,), (0,)), ((), ())),
        preferred_element_type=jnp.float32,
    )
    own_inputs = lax.dynamic_slice_in_dim(
        inputs, part_index * feature_width, feature_width, 0
    ).astype(jnp.float32)
    hidden_state = own_inputs + jax.nn.silu(linear_map)
    mask = (own_ids != 0).astype(jnp.float32)
    counts = jnp.sum(mask, axis=1)
    summed = jnp.einsum("dnl,nl->nd", hidden_state.reshape(feature_width, per_shard, length), mask)
    pooled = (summed / counts[:, None]).astype(jnp.bfloat16)
    gathered = lax.all_gather(pooled, ("group", "dp"), axis=0, tiled=True)
    part_scores = lax.dot_general(
        pooled, gathered, (((1,), (1,)), ((), ())), preferred_element_type=jnp.float32
    )
    gathered_wide = gathered.astype(jnp.float32)
    part_norms = jnp.sum(gathered_wide * gathered_wide, axis=1)
    dots, norms = lax.psum((part_scores, part_norms), "mp")
    rnorm_all = lax.rsqrt(norms + 1e-06)
    all_count = gathered.shape[0]
    half_count = all_count // 2
    own_rows = (
        group_index * half_count + shard_index * per_shard + jnp.arange(per_shard, dtype=jnp.int32)
    )
    rnorm_own = jnp.take(rnorm_all, own_rows)
    cosine = dots * rnorm_own[:, None] * rnorm_all[None, :]
    multiplier_factor = logit_sharpness[0]
    scores = multiplier_factor * cosine
    column_ids = jnp.arange(all_count, dtype=jnp.int32)
    keep = column_ids[None, :] != own_rows[:, None]
    pair = (own_rows + half_count) % all_count
    weight = (group_index == 0).astype(jnp.float32)
    neg_cols = half_count + difficult_distractors
    top = jnp.max(jnp.where(keep, scores, -jnp.inf), axis=1)
    safe_scores = jnp.where(keep, scores, top[:, None])
    expd = jnp.where(keep, jnp.exp(safe_scores - top[:, None]), 0.0)
    neg_exp = (
        jnp.exp(jnp.minimum(jnp.take_along_axis(scores, neg_cols, axis=1) - top[:, None], 0.0))
        * weight
    )
    total = jnp.sum(expd, axis=1) + jnp.sum(neg_exp, axis=1)
    pair_score = jnp.take_along_axis(scores, pair[:, None], axis=1)[:, 0]
    losses = top + jnp.log(total) - pair_score
    onehot = (column_ids[None, None, :] == neg_cols[:, :, None]).astype(jnp.float32)
    probs = (expd + jnp.einsum("rk,rkc->rc", neg_exp, onehot)) / total[:, None]
    target = (column_ids[None, :] == pair[:, None]).astype(jnp.float32)
    grad_scores = (probs - target) / all_count
    coeff = (grad_scores * rnorm_own[:, None] * rnorm_all[None, :]).astype(jnp.bfloat16)
    along = jnp.dot(coeff, gathered, preferred_element_type=jnp.float32)
    pooled_wide = pooled.astype(jnp.float32)
    radial = jnp.sum(grad_scores * cosine, axis=1) * rnorm_own * rnorm_own
    embedding_gradient = multiplier_factor * (along - radial[:, None] * pooled_wide)
    token_grad = jnp.einsum("nd,nl->dnl", embedding_gradient / counts[:, None], mask).reshape(
        feature_width, tokens
    )
    sigma = jax.nn.sigmoid(linear_map)
    local = (token_grad * sigma * (1.0 + linear_map * (1.0 - sigma))).astype(jnp.bfloat16)
    up_portion = lax.dot_general(
        reduced_sum, local, (((1,), (1,)), ((), ())), preferred_element_type=jnp.float32
    )
    adapter_up_gradient = lax.psum(up_portion, ("group", "dp"))
    embeddings = (pooled_wide * rnorm_own[:, None]).astype(jnp.bfloat16)[None]
    return (embeddings, losses[None], adapter_up_gradient)


def solution(mesh):
    in_specs = (
        P("group", None, None),
        P("dp", None),
        P("dp", None),
        P("dp", "mp"),
        P(),
        P(None, "mp"),
        P(),
    )
    out_specs = (P("group", "dp", "mp"), P("group", "dp"), P(None, "mp"))
    return jax.shard_map(body, mesh=mesh, in_specs=in_specs, out_specs=out_specs, check_vma=False)
```

profile of v0, /device:TPU:0, one launch (start us, length us, event | category | flops | bytes accessed | tf_op | source)
XLA Modules:
  0.0 224.3 jit_solution(7666498482478999840)
XLA Ops:
  7.2 0.7 all-gather.3.cloned.1.call-update
  7.9 41.2 %copy.16 = bf16[1024,16384]{0,1:T(8,128)(2,1)} copy(bf16[1024,16384]{1,0:T(8,128)(2,1)} %param.9) | data formatting | bytes 67108864 | tf_op args[2]
  49.2 31.4 %gather_fusion = bf16[1536,1024]{1,0:T(8,128)(2,1)S(1)} fusion(bf16[1024,16384]{0,1:T(8,128)(2,1)} %copy.16, s32[2048]{0:T(1024)S(1)} %pad_clamp_fusion), kind=kCustom, calls=%fused_computation | custom fusion | bytes 6297600 | tf_op jit(solution)/shard_map/jit(_take)/gather | solution.py:25
  80.6 1.9 broadcast_select_fusion
  82.6 7.5 %all-to-all-start = ((bf16[1024,4,384]{0,2,1:T(8,128)(2,1)}), bf16[1024,4,384]{0,2,1:T(8,128)(2,1)S(1)}, u32[]{:S(2)}, u32[]{:S(2)}) async-start(bf16[1024,4,384]{0,2,1:T(8,128)(2,1)} %broadcast_select_fusion), calls=%async_computation | async-start | bytes 6291456 | tf_op jit(solution)/shard_map/all_to_all | solution.py:26
  91.1 35.9 %all-to-all-done = bf16[1024,4,384]{0,2,1:T(8,128)(2,1)S(1)} async-done(((bf16[1024,4,384]{0,2,1:T(8,128)(2,1)}), bf16[1024,4,384]{0,2,1:T(8,128)(2,1)S(1)}, u32[]{:S(2)}, u32[]{:S(2)}) %all-to-all-start) | async-done | bytes 3145760 | tf_op jit(solution)/shard_map/all_to_all | solution.py:26
  127.1 0.4 copy.23
  127.5 0.7 multiply_reduce_fusion
  128.2 1.0 copy-done.1
  129.2 1.0 fusion.9
  130.2 6.9 %fusion.8 = f32[384,1024]{1,0:T(8,128)S(1)} fusion(bf16[4096,1024]{1,0:T(8,128)(2,1)} %all-gather.3.cloned.1.call-done, bf16[4096,384]{0,1:T(8,128)(2,1)} %bitcast.93, f32[384]{0:T(512)S(1)} %add_rsqrt_fusion), kind=kOutput, calls=%fused_computation.20 | convolution fusion | flops 3225944064 | bytes 13108736 | tf_op jit(solution)/shard_map/dot_general | solution.py:32
  137.1 1.8 fusion.5
  138.9 0.2 fusion.18
  139.2 8.1 %all-gather = bf16[8,3,1024]{2,1,0:T(4,128)(2,1)S(1)} all-gather(bf16[1,3,1024]{2,1,0:T(4,128)(2,1)S(1)} %fusion.42), channel_id=1, replica_groups=mesh['group'=2,'dp'=4,'mp'=4] {'group','dp'}, dimensions={0}, use_global_device_ids=true | all-gather | bytes 55296 | tf_op jit(solution)/shard_map/all_gather | solution.py:55
  147.6 12.8 %all-reduce = (f32[24]{0:T(128)S(1)}, f32[3,24]{1,0:T(4,128)S(1)}) all-reduce(f32[24]{0:T(128)S(1)} %multiply_reduce_fusion.1, f32[3,24]{1,0:T(4,128)S(1)} %fusion.30), channel_id=1, replica_groups=mesh['group'=2,'dp'=4,'mp'=4] {'mp'}, use_global_device_ids=true, to_apply=%region_3.4 | all-reduce | flops 96 | bytes 768 | tf_op jit(solution)/shard_map/psum | solution.py:61
  160.4 0.6 gather_fusion.1
  161.2 0.8 gather_fusion.2
  162.4 0.7 gather_fusion.3
  163.4 0.5 fusion.24
  164.5 0.6 fusion.1
  165.1 0.8 fusion.31
  166.0 0.7 fusion.15
  166.7 49.4 %all-reduce.3.cloned.1.call-done = f32[16,1024]{1,0:T(8,128)} async-done(((f32[16,1024]{1,0:T(8,128)}), f32[16,1024]{1,0:T(8,128)}) %all-reduce.3.cloned.1.call-update) | async-done | bytes 65552 | tf_op jit(solution)/shard_map/psum | solution.py:104
  216.0 1.5 copy.40
  (47 shorter events, 2.3 us)
Async XLA Ops:
  7.2 122.0 %copy-start = (bf16[16,4096]{1,0:T(8,128)(2,1)S(1)}, bf16[16,4096]{1,0:T(8,128)(2,1)}, u32[]{:S(2)}) copy-start(bf16[16,4096]{1,0:T(8,128)(2,1)} %param.11) | copy-start | bytes 393220
  7.2 123.0 %all-gather.3.cloned.1.call-start = ((), (), s32[]{:S(2)}) async-start(), calls=%async_computation.1 | async-start | bytes 10485760 | tf_op jit(solution)/shard_map/all_gather | solution.py:33
  7.9 41.2 %copy-start.2 = (s32[1,12,128]{2,0,1:T(1,128)S(1)}, s32[1,12,128]{2,0,1:T(1,128)}, u32[]{:S(2)}) copy-start(s32[1,12,128]{2,0,1:T(1,128)} %param.7) | copy-start | bytes 18436
  82.6 8.2 %copy-start.3 = (s32[3,7]{1,0:T(4,128)S(1)}, s32[3,7]{1,0:T(4,128)}, u32[]{:S(2)}) copy-start(s32[3,7]{1,0:T(4,128)} %param.8) | copy-start | bytes 256
  82.6 44.5 %all-to-all-start = ((bf16[1024,4,384]{0,2,1:T(8,128)(2,1)}), bf16[1024,4,384]{0,2,1:T(8,128)(2,1)S(1)}, u32[]{:S(2)}, u32[]{:S(2)}) async-start(bf16[1024,4,384]{0,2,1:T(8,128)(2,1)} %broadcast_select_fusion), calls=%async_computation | async-start | bytes 6291456 | tf_op jit(solution)/shard_map/all_to_all | solution.py:26
  90.1 125.9 %all-reduce.3.cloned.1.call-start = ((), (), s32[]{:S(2)}) async-start(), calls=%async_computation.2 | async-start | bytes 131072 | tf_op jit(solution)/shard_map/psum | solution.py:104
  127.5 1.7 copy-start.1
  130.2 6.9 %copy-start.4 = (bf16[16,1024]{1,0:T(8,128)(2,1)S(1)}, bf16[16,1024]{1,0:T(8,128)(2,1)}, u32[]{:S(2)}) copy-start(bf16[16,1024]{1,0:T(8,128)(2,1)} %param.12) | copy-start | bytes 98308
Sparse Core Ops, SparseCore 0:
  9.6 60.9 all-gather.2
  166.1 49.8 all-reduce.2
where the time goes:
time: 226 us; the launch traced here: 224 us
  waiting for transfers between devices  86 us (38%)
  local copies, waits for them, and re-layouts  77.9 us (34%)
  blocking collectives  20.9 us (9%)
  between operations  14.9 us (7%)
  matrix products  11.2 us (5%)
  starting transfers between devices  7.58 us (3%)
  other arithmetic  5.94 us (3%)
    psum x1, waiting for transfers between devices, body(): adapter_up_gradient = lax.psum(up_portion, ('group', 'dp'))  49.4 us
    unnamed x14, local copies, waits for them, and re-layouts  43.7 us
    all_to_all x1, waiting for transfers between devices, body(): lax.all_to_all(columns, 'dp', split_axis=1, concat_axis=0, tiled=True)  35.9 us
    gather x1, local copies, waits for them, and re-layouts, body(): columns = jnp.take(vocabulary_vectors, side_ids.reshape(-1), axis=1)  31.4 us
    psum x1, blocking collectives, body(): dots, norms = lax.psum((part_scores, part_norms), 'mp')  12.8 us
    all_gather x1, blocking collectives, body(): gathered = lax.all_gather(pooled, ('group', 'dp'), axis=0, tiled=True)  8.08 us
    all_to_all x1, starting transfers between devices, body(): lax.all_to_all(columns, 'dp', split_axis=1, concat_axis=0, tiled=True)  7.54 us
    dot_general x1, matrix products, body(): lax.dot_general(lax.all_gather(layer_weight_matrix, 'dp', axis=0, tiled=T...  6.89 us
  transfers between devices with their start and end apart: 3, of which 2 were waited for; matrix products, arithmetic and copies ran while one was open for 35% of the time, Pallas kernels for 0%

commit v1 on v0

--- a/solution.py
+++ b/solution.py
@@ -1,10 +1,14 @@
+import functools
+
 import jax
 import jax.numpy as jnp
 from jax import lax
+from jax.experimental import pallas as pl
+from jax.experimental.pallas import tpu as pltpu
 from jax.sharding import PartitionSpec as P
 
 
-def body(
+def general_body(
     query_passage_words,
     difficult_distractors,
     vocabulary_vectors,
@@ -106,6 +110,482 @@
     return (embeddings, losses[None], adapter_up_gradient)
 
 
+IDS_PER_BLOCK = 1024
+WINDOW = 128
+CHUNK = 256
+ROWS = 16
+LANES = 128
+NT = (((1,), (1,)), ((), ()))
+VMEM_BYTES = 60 * 1024 * 1024
+
+
+def mm(a, b, dims=(((1,), (0,)), ((), ()))):
+    return lax.dot_general(a, b, dims, preferred_element_type=jnp.float32)
+
+
+def split(x):
+    high = x.astype(jnp.bfloat16)
+    return high, (x - high.astype(jnp.float32)).astype(jnp.bfloat16)
+
+
+def iota(shape, dim):
+    return lax.broadcasted_iota(jnp.int32, shape, dim)
+
+
+def quarter_of(dp_index, cores=2):
+    return (dp_index % cores) * 2 + dp_index // cores
+
+
+def project_kernel(
+    ids_ref,
+    hard_ref,
+    vocab_ref,
+    weight_ref,
+    lower_ref,
+    out00,
+    out01,
+    out10,
+    out11,
+    member_ref,
+    held,
+    weight,
+    lower,
+    rows32,
+    values,
+    turned,
+    ranks,
+    squares,
+    residual,
+    bounds,
+    held_sems,
+    weight_sems,
+    lower_sem,
+):
+    texts, length = ids_ref.shape
+    tokens = texts * length
+    features, vocab = vocab_ref.shape
+    blocks = vocab // IDS_PER_BLOCK
+    chunks = tokens // CHUNK
+    per_shard, negatives = hard_ref.shape
+    width = weight.shape[2]
+    outs = (out00, out01, out10, out11)
+    shard = lax.axis_index("dp")
+    core, side_y = lax.rem(shard, 2), lax.div(shard, 2)
+
+    def vocab_copy(b):
+        return pltpu.make_async_copy(
+            vocab_ref.at[:, pl.ds(pl.multiple_of(b * IDS_PER_BLOCK, LANES), IDS_PER_BLOCK)],
+            held.at[b],
+            held_sems.at[b],
+        )
+
+    def weight_copy(i, j):
+        quarter = (core ^ i) * 2 + (side_y ^ j)
+        return pltpu.make_async_copy(
+            weight_ref.at[:, pl.ds(pl.multiple_of(quarter * width, LANES), width)],
+            weight.at[2 * i + j],
+            weight_sems.at[2 * i + j],
+        )
+
+    lower_copy = pltpu.make_async_copy(
+        lower_ref.at[:, pl.ds(pl.multiple_of(shard * features, LANES), features)], lower, lower_sem
+    )
+    vocab_copy(0).start()
+    lower_copy.start()
+    for i in range(2):
+        for j in range(2):
+            weight_copy(i, j).start()
+    for b in range(1, blocks):
+        vocab_copy(b).start()
+
+    ids = ids_ref[...]
+    valid = ids != 0
+    block_of = jnp.where(valid, ids // IDS_PER_BLOCK, blocks)
+    for b in range(blocks + 1):
+        bounds[b] = jnp.sum((block_of < b).astype(jnp.float32)).astype(jnp.int32)
+    block_rows = 8 * pl.cdiv(blocks + 1, 8)
+    block_id = iota((block_rows, length), 0)
+    below = jnp.zeros((block_rows, length), jnp.float32)
+    for text in range(texts):
+        below += jnp.where(block_of[text : text + 1] < block_id, 1.0, 0.0)
+    before = jnp.broadcast_to(jnp.sum(below, axis=1, keepdims=True), (block_rows, length))
+    earlier = jnp.where(iota((length, length), 0) < iota((length, length), 1), 1.0, 0.0).astype(
+        jnp.bfloat16
+    )
+    for text in range(texts):
+        here = jnp.where(block_of[text : text + 1] == block_id, 1.0, 0.0)
+        inside = mm(here.astype(jnp.bfloat16), earlier)
+        ranks[pl.ds(text, 1), :] = jnp.sum(here * (inside + before), axis=0, keepdims=True)
+        before += jnp.broadcast_to(jnp.sum(here, axis=1, keepdims=True), (block_rows, length))
+    text_of = iota((texts, length), 0)
+    carried = jnp.where(valid, ids * ROWS + text_of, 0).astype(jnp.float32)
+    rank = ranks[...]
+
+    def place(p, carry):
+        position = (iota((LANES, length), 0) + p * LANES).astype(jnp.float32)
+        total = jnp.zeros((LANES, length), jnp.float32)
+        for text in range(texts):
+            total += jnp.where(rank[text : text + 1] == position, carried[text : text + 1], 0.0)
+        found = jnp.sum(total, axis=1, keepdims=True).astype(jnp.int32)
+        start = pl.multiple_of(p * LANES, LANES)
+        values[pl.ds(start, LANES), :] = jnp.broadcast_to(found, (LANES, LANES))
+        real = (found // ROWS != 0) & (lax.rem(found, ROWS) == iota((LANES, LANES), 1))
+        member_ref[pl.ds(start, LANES), :] = jnp.where(real, 1.0, 0.0).astype(jnp.bfloat16)
+        return carry
+
+    lax.fori_loop(0, tokens // LANES, place, 0)
+    values[pl.ds(tokens, WINDOW), :] = jnp.zeros((WINDOW, LANES), jnp.int32)
+
+    def clear(p, carry):
+        rows32[pl.ds(pl.multiple_of(p * LANES, LANES), LANES), :] = jnp.zeros(
+            (LANES, features), jnp.float32
+        )
+        return carry
+
+    lax.fori_loop(0, (tokens + WINDOW) // LANES, clear, 0)
+    residual[...] = jnp.zeros_like(residual)
+    squares[...] = jnp.zeros_like(squares)
+    turned[...] = jnp.zeros_like(turned)
+    turned[0:per_shard, chunks : chunks + negatives] = hard_ref[...].astype(jnp.float32)
+    lower_copy.wait()
+    for i in range(2):
+        for j in range(2):
+            weight_copy(i, j).wait()
+
+    def project(k, carry):
+        start = pl.multiple_of(k * CHUNK, CHUNK)
+        x = rows32[pl.ds(start, CHUNK), :].astype(jnp.bfloat16)
+        for q in range(4):
+            outs[q][pl.ds(start, CHUNK), :] = mm(x, weight[q]).astype(jnp.bfloat16)
+        reduced = mm(lower[...], x, NT).astype(jnp.bfloat16)
+        place_at = pl.multiple_of(tokens + k * ROWS, ROWS)
+        for q in range(4):
+            outs[q][pl.ds(place_at, ROWS), :] = reduced
+        ones = jnp.ones((ROWS, features), jnp.bfloat16)
+        squares[pl.ds(k, 1), :] = mm(ones, x * x, NT)[0:1]
+        member = member_ref[pl.ds(start, CHUNK), :].astype(jnp.float32).T.astype(jnp.bfloat16)
+        residual[...] += mm(member[0:ROWS], x)
+        return carry
+
+    def zero(k, carry):
+        start = pl.multiple_of(k * CHUNK, CHUNK)
+        place_at = pl.multiple_of(tokens + k * ROWS, ROWS)
+        for q in range(4):
+            outs[q][pl.ds(start, CHUNK), :] = jnp.zeros((CHUNK, width), jnp.bfloat16)
+            outs[q][pl.ds(place_at, ROWS), :] = jnp.zeros((ROWS, width), jnp.bfloat16)
+        return carry
+
+    def take(b, done):
+        vocab_copy(b).wait()
+        first, last = bounds[b], bounds[b + 1]
+        aligned = (first // ROWS) * ROWS
+        windows = jnp.where(last > first, (last - aligned + WINDOW - 1) // WINDOW, 0)
+
+        def window(w, carry):
+            start = pl.multiple_of(aligned + w * WINDOW, ROWS)
+            wanted = values[pl.ds(start, WINDOW), :] // ROWS - b * IDS_PER_BLOCK
+            wanted = jnp.concatenate([wanted] * (IDS_PER_BLOCK // LANES), axis=1)
+            picked = jnp.where(wanted == iota((WINDOW, IDS_PER_BLOCK), 1), 1.0, 0.0)
+            picked = jnp.where(wanted + b * IDS_PER_BLOCK == 0, 0.0, picked).astype(jnp.bfloat16)
+            rows32[pl.ds(start, WINDOW), :] += mm(picked, held[b], NT)
+            return carry
+
+        lax.fori_loop(0, windows, window, 0)
+        full = last // CHUNK
+        lax.fori_loop(done, full, project, 0)
+        return full
+
+    done = lax.fori_loop(0, blocks, take, 0)
+    used = (bounds[blocks] + CHUNK - 1) // CHUNK
+    lax.fori_loop(done, used, project, 0)
+    lax.fori_loop(used, chunks, zero, 0)
+
+    hard = turned[...].T[0:ROWS]
+    lane = iota((ROWS, width), 1)
+    misc = jnp.concatenate([squares[...], jnp.zeros((ROWS - squares.shape[0], width), jnp.float32)])
+    for i in range(per_shard):
+        misc += jnp.where(lane == shard * per_shard + i, hard[:, i : i + 1], 0.0)
+    misc = misc.astype(jnp.bfloat16)
+    mine = lax.axis_index("mp") == shard
+    for i in range(2):
+        for j in range(2):
+            quarter = (core ^ i) * 2 + (side_y ^ j)
+            part = residual[:, pl.ds(pl.multiple_of(quarter * width, LANES), width)]
+            out = outs[2 * i + j]
+            out[pl.ds(tokens + chunks * ROWS, ROWS), :] = misc
+            out[pl.ds(tokens + (chunks + 1) * ROWS, ROWS), :] = jnp.where(mine, part, 0.0).astype(
+                jnp.bfloat16
+            )
+
+
+def pool_kernel(
+    ids_ref,
+    own_ref,
+    core_ref,
+    far_ref,
+    member_ref,
+    raise_ref,
+    pooled_ref,
+    slope_ref,
+    reduced_ref,
+    misc_ref,
+    raised,
+    model_width,
+):
+    texts, length = ids_ref.shape
+    tokens = texts * length
+    chunks = tokens // CHUNK
+    width = own_ref.shape[1]
+    quarter = quarter_of(lax.axis_index("dp"))
+
+    def summed(start, size):
+        rows = pl.ds(start, size)
+        return (
+            own_ref[rows, :].astype(jnp.float32)
+            + core_ref[rows, :].astype(jnp.float32)
+            + far_ref[rows, :].astype(jnp.float32)
+        )
+
+    misc = summed(tokens + chunks * ROWS, ROWS)
+    misc_ref[...] = misc
+    inverse = lax.rsqrt(misc / model_width + 1e-05)
+    raised[...] = jnp.zeros_like(raised)
+    raised[0:ROWS, :] = raise_ref[:, pl.ds(pl.multiple_of(quarter * width, LANES), width)]
+    total = jnp.zeros((ROWS, width), jnp.float32)
+    for k in range(chunks):
+        scale = inverse[k : k + 1]
+        reduced = (summed(tokens + k * ROWS, ROWS) * scale).astype(jnp.bfloat16)
+        reduced_ref[:, k * CHUNK : (k + 1) * CHUNK] = reduced
+        stacked = jnp.concatenate(
+            [reduced.astype(jnp.float32), jnp.broadcast_to(scale, (LANES - ROWS, CHUNK))]
+        )
+        turned = stacked.T
+        low = turned.astype(jnp.bfloat16)
+        linear = summed(k * CHUNK, CHUNK) * turned[:, ROWS : ROWS + 1] + mm(low, raised[...])
+        sigma = 1.0 / (1.0 + jnp.exp(-linear))
+        slope_ref[pl.ds(k * CHUNK, CHUNK), :] = sigma * (1.0 + linear * (1.0 - sigma))
+        member = member_ref[pl.ds(k * CHUNK, CHUNK), :].astype(jnp.float32).T
+        member = member[0:ROWS].astype(jnp.bfloat16)
+        high, rest = split(linear * sigma)
+        total += mm(member, high) + mm(member, rest)
+    total += summed(tokens + (chunks + 1) * ROWS, ROWS)
+    counts = jnp.sum((ids_ref[...] != 0).astype(jnp.float32), axis=1, keepdims=True)
+    pooled = total[0:texts] / counts
+    pooled_ref[...] = jnp.zeros_like(pooled_ref)
+    pooled_ref[0:texts, :] = pooled.astype(jnp.bfloat16)
+
+
+def score_kernel(
+    ids_ref,
+    pooled_ref,
+    misc_ref,
+    slope_ref,
+    reduced_ref,
+    member_ref,
+    sharp_ref,
+    embed_ref,
+    loss_ref,
+    up_ref,
+    shards,
+    parts,
+    negatives,
+):
+    texts, length = ids_ref.shape
+    tokens = texts * length
+    chunks = tokens // CHUNK
+    rows = 2 * ROWS
+    width = pooled_ref.shape[2]
+    per_shard = loss_ref.shape[1]
+    group, shard, part = lax.axis_index("group"), lax.axis_index("dp"), lax.axis_index("mp")
+    places = shards * parts
+
+    def both(place):
+        return jnp.concatenate([pooled_ref[place], pooled_ref[places + place]], axis=0)
+
+    dots = jnp.zeros((rows, rows), jnp.float32)
+    for place in range(places):
+        block = both(place)
+        dots += mm(block, block, NT)
+    down, across = iota((rows, rows), 0), iota((rows, rows), 1)
+    same = down == across
+    real = (lax.rem(down, ROWS) < texts) & (lax.rem(across, ROWS) < texts)
+    diagonal = jnp.where(same, dots, 0.0)
+    rnorm_row = lax.rsqrt(jnp.sum(diagonal, axis=0, keepdims=True) + 1e-06)
+    rnorm_col = lax.rsqrt(jnp.sum(diagonal, axis=1, keepdims=True) + 1e-06)
+    sharpness = sharp_ref[0]
+    cosine = dots * rnorm_col * rnorm_row
+    scores = sharpness * cosine
+    keep = real & ~same
+    top = jnp.max(jnp.where(keep, scores, -jnp.inf), axis=0, keepdims=True)
+    top = jnp.where(lax.rem(across[0:1], ROWS) < texts, top, 0.0)
+    powers = jnp.exp(jnp.where(real, jnp.minimum(scores - top, 0.0), 0.0))
+    hard = misc_ref[chunks : chunks + negatives, 0:rows].astype(jnp.int32) + ROWS
+    times = jnp.zeros((rows, rows), jnp.float32)
+    for k in range(negatives):
+        times += jnp.where(hard[k : k + 1] == down, 1.0, 0.0)
+    times = jnp.where(across < texts, times, 0.0)
+    weights = (jnp.where(keep, 1.0, 0.0) + jnp.where(real, times, 0.0)) * powers
+    total = jnp.sum(weights, axis=0, keepdims=True)
+    total = jnp.where(lax.rem(across[0:1], ROWS) < texts, total, 1.0)
+    pair = (down == lax.rem(across + ROWS, rows)) & real
+    pair_score = jnp.sum(jnp.where(pair, scores, 0.0), axis=0, keepdims=True)
+    losses = top + jnp.log(total) - pair_score
+    grad_scores = (weights / total - jnp.where(pair, 1.0, 0.0)) / (2 * texts)
+    coeff = (grad_scores * rnorm_col * rnorm_row).astype(jnp.bfloat16)
+    radial = jnp.sum(grad_scores * cosine, axis=0, keepdims=True) * rnorm_row * rnorm_row
+
+    first = shard * per_shard
+    loss_col = jnp.sum(jnp.where(same, losses, 0.0), axis=1, keepdims=True)
+    at = (iota((rows, LANES), 0) == group * ROWS + first + iota((rows, LANES), 1)) & (
+        iota((rows, LANES), 1) < per_shard
+    )
+    loss_ref[...] = jnp.sum(jnp.where(at, loss_col, 0.0), axis=0, keepdims=True)[:, 0:per_shard]
+
+    place = shard * parts + part
+    mine = both(place)
+    along = mm(coeff.astype(jnp.float32).T.astype(jnp.bfloat16), mine)
+    radial_col = jnp.sum(jnp.where(same, radial, 0.0), axis=1, keepdims=True)
+    grad = sharpness * (along - radial_col * mine.astype(jnp.float32))
+    grad = jnp.where(group == 0, grad[0:ROWS], grad[ROWS:rows])
+    counts = jnp.sum((ids_ref[...] != 0).astype(jnp.float32), axis=1, keepdims=True)
+    grad = grad[0:texts] / counts
+    grad = jnp.concatenate([grad, jnp.zeros((LANES - texts, width), jnp.float32)])
+    high, rest = split(grad)
+    update = jnp.zeros((ROWS, width), jnp.float32)
+    for k in range(chunks):
+        member = member_ref[pl.ds(k * CHUNK, CHUNK), :]
+        token_grad = mm(member, high) + mm(member, rest)
+        local = (token_grad * slope_ref[pl.ds(k * CHUNK, CHUNK), :]).astype(jnp.bfloat16)
+        update += mm(reduced_ref[:, k * CHUNK : (k + 1) * CHUNK], local)
+    up_ref[...] = update
+
+    rnorm_own = jnp.where(group == 0, rnorm_col[0:ROWS], rnorm_col[ROWS:rows])
+    chosen = iota((ROWS, ROWS), 1) == iota((ROWS, ROWS), 0) + first
+    chosen = jnp.where(chosen & (iota((ROWS, ROWS), 0) < per_shard), 1.0, 0.0).astype(jnp.bfloat16)
+    for quarter in range(shards):
+        holder = quarter_of(quarter, 2)
+        block = pooled_ref[group * places + holder * parts + part].astype(jnp.float32) * rnorm_own
+        picked = mm(chosen, block.astype(jnp.bfloat16)).astype(jnp.bfloat16)
+        embed_ref[0, :, quarter * width : (quarter + 1) * width] = picked[0:per_shard]
+
+
+def any_spec():
+    return pl.BlockSpec(memory_space=pl.ANY)
+
+
+def vmem_spec():
+    return pl.BlockSpec(memory_space=pltpu.VMEM)
+
+
+def smem_spec():
+    return pl.BlockSpec(memory_space=pltpu.SMEM)
+
+
+def split_body(
+    query_passage_words,
+    difficult_distractors,
+    vocabulary_vectors,
+    layer_weight_matrix,
+    lowering_factor_matrix,
+    raising_factor_matrix,
+    logit_sharpness,
+):
+    shards, parts = lax.axis_size("dp"), lax.axis_size("mp")
+    ids = query_passage_words[0]
+    texts, length = ids.shape
+    tokens = texts * length
+    chunks = tokens // CHUNK
+    features, vocab = vocabulary_vectors.shape
+    blocks = vocab // IDS_PER_BLOCK
+    per_shard, negatives = difficult_distractors.shape
+    rank = lowering_factor_matrix.shape[0]
+    part_width = layer_weight_matrix.shape[1]
+    width = part_width // shards
+    rows = tokens + (chunks + 2) * ROWS
+    params = pltpu.CompilerParams(vmem_limit_bytes=VMEM_BYTES)
+    half = jax.ShapeDtypeStruct((rows, width), jnp.bfloat16)
+    own0, own1, away0, away1, member = pl.pallas_call(
+        project_kernel,
+        out_shape=[half] * 4 + [jax.ShapeDtypeStruct((tokens, LANES), jnp.bfloat16)],
+        in_specs=[vmem_spec()] * 2 + [any_spec()] * 3,
+        out_specs=[vmem_spec()] * 5,
+        scratch_shapes=[
+            pltpu.VMEM((blocks, features, IDS_PER_BLOCK), jnp.bfloat16),
+            pltpu.VMEM((4, features, width), jnp.bfloat16),
+            pltpu.VMEM((rank, features), jnp.bfloat16),
+            pltpu.VMEM((tokens + WINDOW, features), jnp.float32),
+            pltpu.VMEM((tokens + WINDOW, LANES), jnp.int32),
+            pltpu.VMEM((LANES, LANES), jnp.float32),
+            pltpu.VMEM((texts, length), jnp.float32),
+            pltpu.VMEM((8, width), jnp.float32),
+            pltpu.VMEM((ROWS, features), jnp.float32),
+            pltpu.SMEM((blocks + 1,), jnp.int32),
+            pltpu.SemaphoreType.DMA((blocks,)),
+            pltpu.SemaphoreType.DMA((4,)),
+            pltpu.SemaphoreType.DMA,
+        ],
+        compiler_params=params,
+        name="project",
+    )(
+        ids,
+        difficult_distractors,
+        vocabulary_vectors,
+        layer_weight_matrix,
+        lowering_factor_matrix,
+    )
+    other_core = [(d, d ^ 1) for d in range(shards)]
+    other_y = [(d, d ^ 2) for d in range(shards)]
+    core1 = lax.ppermute(away1, "dp", other_core)
+    core0 = lax.ppermute(away0, "dp", other_core)
+    chip1 = (own1.astype(jnp.float32) + core1.astype(jnp.float32)).astype(jnp.bfloat16)
+    far = lax.ppermute(chip1, "dp", other_y)
+    pooled, slope, reduced, misc = pl.pallas_call(
+        functools.partial(pool_kernel, model_width=float(features * shards)),
+        out_shape=[
+            jax.ShapeDtypeStruct((ROWS, width), jnp.bfloat16),
+            jax.ShapeDtypeStruct((tokens, width), jnp.float32),
+            jax.ShapeDtypeStruct((ROWS, tokens), jnp.bfloat16),
+            jax.ShapeDtypeStruct((ROWS, width), jnp.float32),
+        ],
+        in_specs=[vmem_spec()] * 6,
+        out_specs=[vmem_spec()] * 4,
+        scratch_shapes=[pltpu.VMEM((LANES, width), jnp.bfloat16)],
+        compiler_params=params,
+        name="pool",
+    )(ids, own0, core0, far, member, raising_factor_matrix)
+    gathered = lax.all_gather(pooled, ("group", "dp", "mp"), axis=0)
+    embeddings, losses, update = pl.pallas_call(
+        functools.partial(score_kernel, shards=shards, parts=parts, negatives=negatives),
+        out_shape=[
+            jax.ShapeDtypeStruct((1, per_shard, part_width), jnp.bfloat16),
+            jax.ShapeDtypeStruct((1, per_shard), jnp.float32),
+            jax.ShapeDtypeStruct((ROWS, width), jnp.float32),
+        ],
+        in_specs=[vmem_spec()] * 6 + [smem_spec()],
+        out_specs=[vmem_spec()] * 3,
+        compiler_params=params,
+        name="score",
+    )(ids, gathered, misc, slope, reduced, member, logit_sharpness)
+    updates = lax.all_gather(update, ("group", "dp"), axis=0)
+    columns = [updates[quarter_of(q)] + updates[shards + quarter_of(q)] for q in range(shards)]
+    return (embeddings, losses, jnp.concatenate(columns, axis=1))
+
+
+def body(words, hard, vocabulary, weight, lowering, raising, sharpness):
+    shards, parts = lax.axis_size("dp"), lax.axis_size("mp")
+    texts, length = words.shape[1:]
+    features, vocab = vocabulary.shape
+    negatives = hard.shape[1]
+    square = shards == 4 and features == weight.shape[1] and parts == shards
+    small = texts <= ROWS - 2 and length == LANES and texts * length <= 2048
+    even = (texts * length) % CHUNK == 0 and vocab % IDS_PER_BLOCK == 0
+    fits = features * vocab <= 2**24 and features % (4 * LANES) == 0
+    spare = texts * length // CHUNK + negatives <= ROWS and lowering.shape[0] == ROWS
+    fast = square and small and even and fits and spare and lax.axis_size("group") == 2
+    chosen = split_body if fast else general_body
+    return chosen(words, hard, vocabulary, weight, lowering, raising, sharpness)
+
+
 def solution(mesh):
     in_specs = (
         P("group", None, None),

time: 226 us -> 153 us (0.68)
  local copies, waits for them, and re-layouts: 77.9 us -> 2.22 us
  waiting for transfers between devices: 86 us -> 20.7 us
  blocking collectives: 20.9 us -> 83.4 us
  Pallas kernels: 0 us -> 39.4 us
  between operations: 14.9 us -> 1.32 us
  matrix products: 11.2 us -> 0 us
  starting transfers between devices: 7.58 us -> 3.55 us
  other arithmetic: 5.94 us -> 2.06 us
    all_gather x1 -> x2, blocking collectives: 8.08 us -> 83.4 us  [the longest x1 75.1 us: split_body(): gathered = lax.all_gather(pooled, ('group', 'dp', 'mp'), axis=0)]
    psum x1 -> x0, waiting for transfers between devices: 49.4 us -> none  [body(): adapter_up_gradient = lax.psum(up_portion, ('group', 'dp'))]
    unnamed x14 -> x5, local copies, waits for them, and re-layouts: 43.7 us -> 2.22 us
    pallas_call x0 -> x3, Pallas kernels: none -> 39.4 us  [the longest x1 31.4 us: split_body(): pl.pallas_call(project_kernel, out_shape=[half] * 4 + [jax.ShapeDtypeStru...]
    all_to_all x1 -> x0, waiting for transfers between devices: 35.9 us -> none  [body(): lax.all_to_all(columns, 'dp', split_axis=1, concat_axis=0, tiled=True)]
    gather x6 -> x0, local copies, waits for them, and re-layouts: 33.7 us -> none  [the longest x1 31.4 us: body(): columns = jnp.take(vocabulary_vectors, side_ids.reshape(-1), axis=1)]
    ppermute x0 -> x3, waiting for transfers between devices: none -> 20.7 us  [the longest x1 18.6 us: split_body(): far = lax.ppermute(chip1, 'dp', other_y)]
    psum x1 -> x0, blocking collectives: 12.8 us -> none  [body(): dots, norms = lax.psum((part_scores, part_norms), 'mp')]
  transfers between devices with their start and end apart: 3 -> 3, of which waited for: 2 -> 2; matrix products, arithmetic and copies ran while one was open for 35% -> 1% of each run, Pallas kernels for 0% -> 0%
where the time goes in v1:
time: 153 us
  blocking collectives  83.4 us (55%)
  Pallas kernels  39.4 us (26%)
  waiting for transfers between devices  20.7 us (14%)
  starting transfers between devices  3.55 us (2%)
  local copies, waits for them, and re-layouts  2.22 us (1%)
  other arithmetic  2.06 us (1%)
    all_gather x1, blocking collectives, split_body(): gathered = lax.all_gather(pooled, ('group', 'dp', 'mp'), axis=0)  75.1 us
    pallas_call x1, Pallas kernels, split_body(): pl.pallas_call(project_kernel, out_shape=[half] * 4 + [jax.ShapeDtypeStru...  31.4 us
    ppermute x1, waiting for transfers between devices, split_body(): far = lax.ppermute(chip1, 'dp', other_y)  18.6 us
    all_gather x1, blocking collectives, split_body(): updates = lax.all_gather(update, ('group', 'dp'), axis=0)  8.39 us
    pallas_call x1, Pallas kernels, split_body(): pl.pallas_call(functools.partial(pool_kernel, model_width=float(features...  4.23 us
    pallas_call x1, Pallas kernels, split_body(): pl.pallas_call(functools.partial(score_kernel, shards=shards, parts=parts...  3.85 us
  transfers between devices with their start and end apart: 3, of which 2 were waited for; matrix products, arithmetic and copies ran while one was open for 1% of the time, Pallas kernels for 0%

profile of v1, /device:TPU:0, one launch (start us, length us, event | category | flops | bytes accessed | tf_op | source)
XLA Modules:
  0.0 152.8 jit_solution(2417470716835044720)
XLA Ops:
  0.6 1.3 copy.12
  1.9 31.4 %project.1 = (bf16[1664,256]{1,0:T(8,128)(2,1)}, bf16[1664,256]{1,0:T(8,128)(2,1)}, bf16[1664,256]{1,0:T(8,128)(2,1)}, bf16[1664,256]{1,0:T(8,128)(2,1)}, bf16[1536,128]{1,0:T(8,128)(2,1)}) custom-call(s32[12,128]{1,0:T(8,128)} %bitcast.5, s32[3,7]{1,0:T(4,128)} %hard_ref.1, bf16[1024,16384]{1,0:T(8,128)(2,1)} %vocab_ref.1, bf16[1024,1024]{1,0:T(8,128)(2,1)} %weight_ref.1, ...), custom_call_target="tpu_custom_call" | custom-call | tf_op jit(solution)/shard_map/project/pallas_call | solution.py:507
  33.3 0.5 collective-permute-start.1
  33.8 0.1 collective-permute-start
  33.9 2.1 %collective-permute-done.1 = bf16[1664,256]{1,0:T(8,128)(2,1)S(1)} collective-permute-done((bf16[1664,256]{1,0:T(8,128)(2,1)}, bf16[1664,256]{1,0:T(8,128)(2,1)S(1)}, u32[]{:S(2)}, u32[]{:S(2)}) %collective-permute-start.1) | collective-permute-done | bytes 852000 | tf_op jit(solution)/shard_map/ppermute | solution.py:538
  36.0 1.4 add_convert_fusion
  37.5 3.0 %collective-permute-start.2 = (bf16[1664,256]{1,0:T(8,128)(2,1)S(1)}, bf16[1664,256]{1,0:T(8,128)(2,1)S(1)}, u32[]{:S(2)}, u32[]{:S(2)}) collective-permute-start(bf16[1664,256]{1,0:T(8,128)(2,1)S(1)} %add_convert_fusion), channel_id=1, source_target_pairs={{0,8},{4,12},{8,0},{12,4},{1,9},{5,13},{9,1},{13,5},{2,10},{6,14},... | collective-permute-start | bytes 2555912 | tf_op jit(solution)/shard_map/ppermute | solution.py:541
  41.1 0.0 collective-permute-done.core_ref
  41.1 0.0 copy-start
  41.1 18.6 %collective-permute-done.2.far_ref = bf16[1664,256]{1,0:T(8,128)(2,1)S(1)} collective-permute-done((bf16[1664,256]{1,0:T(8,128)(2,1)S(1)}, bf16[1664,256]{1,0:T(8,128)(2,1)S(1)}, u32[]{:S(2)}, u32[]{:S(2)}) %collective-permute-start.2) | collective-permute-done | bytes 852000 | tf_op jit(solution)/shard_map/ppermute | solution.py:541
  59.7 0.0 copy-start.1
  59.7 0.0 copy-done
  59.7 0.9 copy-done.1
  60.6 4.2 %pool.1 = (bf16[16,256]{1,0:T(8,128)(2,1)}, f32[1536,256]{1,0:T(8,128)}, bf16[16,1536]{1,0:T(8,128)(2,1)}, f32[16,256]{1,0:T(8,128)}) custom-call(s32[12,128]{1,0:T(8,128)} %bitcast.6, bf16[1664,256]{1,0:T(8,128)(2,1)} %get-tuple-element.15.own_ref, bf16[1664,256]{1,0:T(8,128)(2,1)} %copy-done, bf16[1664,256]{1,0:T(8,128)(2,1)} %copy-done.1, ...), custom_call_target="tpu_custom_call" | custom-call | tf_op jit(solution)/shard_map/pool/pallas_call | solution.py:542
  64.8 75.1 %all-gather = bf16[512,256]{1,0:T(8,128)(2,1)} all-gather(bf16[16,256]{1,0:T(8,128)(2,1)} %get-tuple-element.20), channel_id=2, replica_groups=mesh['group'=2,'dp'=4,'mp'=4] {'group','dp','mp'}, dimensions={0}, use_global_device_ids=true | all-gather | bytes 270336 | tf_op jit(solution)/shard_map/all_gather | solution.py:556
  139.9 3.8 %score.1 = (bf16[1,3,1024]{2,1,0:T(4,128)(2,1)}, f32[1,3]{1,0:T(1,128)}, f32[16,256]{1,0:T(8,128)}) custom-call(s32[12,128]{1,0:T(8,128)} %bitcast.7, bf16[32,16,256]{2,1,0:T(8,128)(2,1)} %bitcast.4, f32[16,256]{1,0:T(8,128)} %get-tuple-element.21.misc_ref, f32[1536,256]{1,0:T(8,128)} %get-tuple-element.22.slope_ref, ...), custom_call_target="tpu_custom_call" | custom-call | tf_op jit(solution)/shard_map/score/pallas_call | solution.py:557
  143.7 8.4 %all-gather.1 = f32[128,256]{1,0:T(8,128)S(1)} all-gather(f32[16,256]{1,0:T(8,128)} %get-tuple-element.26), channel_id=3, replica_groups=mesh['group'=2,'dp'=4,'mp'=4] {'group','dp'}, dimensions={0}, use_global_device_ids=true | all-gather | bytes 147456 | tf_op jit(solution)/shard_map/all_gather | solution.py:569
  152.1 0.6 pad_maximum_fusion
  (1 shorter events, 0.0 us)
Async XLA Ops:
  33.3 2.7 %collective-permute-start.1 = (bf16[1664,256]{1,0:T(8,128)(2,1)}, bf16[1664,256]{1,0:T(8,128)(2,1)S(1)}, u32[]{:S(2)}, u32[]{:S(2)}) collective-permute-start(bf16[1664,256]{1,0:T(8,128)(2,1)} %get-tuple-element.18), channel_id=1, source_target_pairs={{0,4},{4,0},{8,12},{12,8},{1,5},{5,1},{9,13},{13,9},{2,6},{6,2},{1... | collective-permute-start | bytes 2555912 | tf_op jit(solution)/shard_map/ppermute | solution.py:538
  33.8 7.2 %collective-permute-start = (bf16[1664,256]{1,0:T(8,128)(2,1)}, bf16[1664,256]{1,0:T(8,128)(2,1)S(1)}, u32[]{:S(2)}, u32[]{:S(2)}) collective-permute-start(bf16[1664,256]{1,0:T(8,128)(2,1)} %get-tuple-element.16), channel_id=1, source_target_pairs={{0,4},{4,0},{8,12},{12,8},{1,5},{5,1},{9,13},{13,9},{2,6},{6,2},{1... | collective-permute-start | bytes 2555912 | tf_op jit(solution)/shard_map/ppermute | solution.py:539
  37.5 22.2 %collective-permute-start.2 = (bf16[1664,256]{1,0:T(8,128)(2,1)S(1)}, bf16[1664,256]{1,0:T(8,128)(2,1)S(1)}, u32[]{:S(2)}, u32[]{:S(2)}) collective-permute-start(bf16[1664,256]{1,0:T(8,128)(2,1)S(1)} %add_convert_fusion), channel_id=1, source_target_pairs={{0,8},{4,12},{8,0},{12,4},{1,9},{5,13},{9,1},{13,5},{2,10},{6,14},... | collective-permute-start | bytes 2555912 | tf_op jit(solution)/shard_map/ppermute | solution.py:541
  41.1 18.6 %copy-start = (bf16[1664,256]{1,0:T(8,128)(2,1)}, bf16[1664,256]{1,0:T(8,128)(2,1)S(1)}, u32[]{:S(2)}) copy-start(bf16[1664,256]{1,0:T(8,128)(2,1)S(1)} %collective-permute-done.core_ref) | copy-start | bytes 2555908
  59.7 0.9 copy-start.1

commit v2 on v1

--- a/solution.py
+++ b/solution.py
@@ -110,10 +110,11 @@
     return (embeddings, losses[None], adapter_up_gradient)
 
 
-IDS_PER_BLOCK = 1024
-WINDOW = 128
-CHUNK = 256
-ROWS = 16
+BLOCK_BITS, WINDOW_BITS, CHUNK_BITS, ROW_BITS = 10, 7, 8, 4
+IDS_PER_BLOCK = 1 << BLOCK_BITS
+WINDOW = 1 << WINDOW_BITS
+CHUNK = 1 << CHUNK_BITS
+ROWS = 1 << ROW_BITS
 LANES = 128
 NT = (((1,), (1,)), ((), ()))
 VMEM_BYTES = 60 * 1024 * 1024
@@ -150,16 +151,18 @@
     held,
     weight,
     lower,
-    rows32,
+    gathered,
     values,
     turned,
     ranks,
     squares,
     residual,
+    counted,
     bounds,
     held_sems,
     weight_sems,
     lower_sem,
+    bounds_sem,
 ):
     texts, length = ids_ref.shape
     tokens = texts * length
@@ -200,15 +203,16 @@
 
     ids = ids_ref[...]
     valid = ids != 0
-    block_of = jnp.where(valid, ids // IDS_PER_BLOCK, blocks)
-    for b in range(blocks + 1):
-        bounds[b] = jnp.sum((block_of < b).astype(jnp.float32)).astype(jnp.int32)
-    block_rows = 8 * pl.cdiv(blocks + 1, 8)
+    block_of = jnp.where(valid, lax.shift_right_logical(ids, BLOCK_BITS), blocks)
+    block_rows = counted.shape[0]
     block_id = iota((block_rows, length), 0)
     below = jnp.zeros((block_rows, length), jnp.float32)
     for text in range(texts):
         below += jnp.where(block_of[text : text + 1] < block_id, 1.0, 0.0)
     before = jnp.broadcast_to(jnp.sum(below, axis=1, keepdims=True), (block_rows, length))
+    counted[...] = before.astype(jnp.int32)
+    bounds_copy = pltpu.make_async_copy(counted, bounds, bounds_sem)
+    bounds_copy.start()
     earlier = jnp.where(iota((length, length), 0) < iota((length, length), 1), 1.0, 0.0).astype(
         jnp.bfloat16
     )
@@ -218,7 +222,7 @@
         ranks[pl.ds(text, 1), :] = jnp.sum(here * (inside + before), axis=0, keepdims=True)
         before += jnp.broadcast_to(jnp.sum(here, axis=1, keepdims=True), (block_rows, length))
     text_of = iota((texts, length), 0)
-    carried = jnp.where(valid, ids * ROWS + text_of, 0).astype(jnp.float32)
+    carried = jnp.where(valid, lax.shift_left(ids, ROW_BITS) + text_of, 0).astype(jnp.float32)
     rank = ranks[...]
 
     def place(p, carry):
@@ -226,23 +230,19 @@
         total = jnp.zeros((LANES, length), jnp.float32)
         for text in range(texts):
             total += jnp.where(rank[text : text + 1] == position, carried[text : text + 1], 0.0)
-        found = jnp.sum(total, axis=1, keepdims=True).astype(jnp.int32)
+        found = jnp.broadcast_to(jnp.sum(total, axis=1, keepdims=True), (LANES, LANES))
+        found = found.astype(jnp.int32)
+        token = lax.shift_right_logical(found, ROW_BITS)
         start = pl.multiple_of(p * LANES, LANES)
-        values[pl.ds(start, LANES), :] = jnp.broadcast_to(found, (LANES, LANES))
-        real = (found // ROWS != 0) & (lax.rem(found, ROWS) == iota((LANES, LANES), 1))
+        values[pl.ds(start, LANES), :] = jnp.where(token == 0, -vocab, token)
+        real = (token != 0) & ((found & (ROWS - 1)) == iota((LANES, LANES), 1))
         member_ref[pl.ds(start, LANES), :] = jnp.where(real, 1.0, 0.0).astype(jnp.bfloat16)
+        gathered[pl.ds(start, LANES), :] = jnp.zeros((LANES, features), jnp.bfloat16)
         return carry
 
     lax.fori_loop(0, tokens // LANES, place, 0)
-    values[pl.ds(tokens, WINDOW), :] = jnp.zeros((WINDOW, LANES), jnp.int32)
-
-    def clear(p, carry):
-        rows32[pl.ds(pl.multiple_of(p * LANES, LANES), LANES), :] = jnp.zeros(
-            (LANES, features), jnp.float32
-        )
-        return carry
-
-    lax.fori_loop(0, (tokens + WINDOW) // LANES, clear, 0)
+    values[pl.ds(tokens, WINDOW), :] = jnp.full((WINDOW, LANES), -vocab, jnp.int32)
+    gathered[pl.ds(tokens, WINDOW), :] = jnp.zeros((WINDOW, features), jnp.bfloat16)
     residual[...] = jnp.zeros_like(residual)
     squares[...] = jnp.zeros_like(squares)
     turned[...] = jnp.zeros_like(turned)
@@ -254,7 +254,7 @@
 
     def project(k, carry):
         start = pl.multiple_of(k * CHUNK, CHUNK)
-        x = rows32[pl.ds(start, CHUNK), :].astype(jnp.bfloat16)
+        x = gathered[pl.ds(start, CHUNK), :]
         for q in range(4):
             outs[q][pl.ds(start, CHUNK), :] = mm(x, weight[q]).astype(jnp.bfloat16)
         reduced = mm(lower[...], x, NT).astype(jnp.bfloat16)
@@ -277,26 +277,30 @@
 
     def take(b, done):
         vocab_copy(b).wait()
-        first, last = bounds[b], bounds[b + 1]
-        aligned = (first // ROWS) * ROWS
-        windows = jnp.where(last > first, (last - aligned + WINDOW - 1) // WINDOW, 0)
+        first, last = bounds[b, 0], bounds[b + 1, 0]
+        aligned = lax.shift_left(lax.shift_right_logical(first, ROW_BITS), ROW_BITS)
+        windows = lax.shift_right_logical(last - aligned + WINDOW - 1, WINDOW_BITS)
+        windows = jnp.where(last > first, windows, 0)
 
         def window(w, carry):
             start = pl.multiple_of(aligned + w * WINDOW, ROWS)
-            wanted = values[pl.ds(start, WINDOW), :] // ROWS - b * IDS_PER_BLOCK
-            wanted = jnp.concatenate([wanted] * (IDS_PER_BLOCK // LANES), axis=1)
-            picked = jnp.where(wanted == iota((WINDOW, IDS_PER_BLOCK), 1), 1.0, 0.0)
-            picked = jnp.where(wanted + b * IDS_PER_BLOCK == 0, 0.0, picked).astype(jnp.bfloat16)
-            rows32[pl.ds(start, WINDOW), :] += mm(picked, held[b], NT)
+            wanted = values[pl.ds(start, WINDOW), :] - (b * IDS_PER_BLOCK + iota((WINDOW, LANES), 1))
+            picked = [
+                jnp.where(wanted == j * LANES, 1.0, 0.0).astype(jnp.bfloat16)
+                for j in range(IDS_PER_BLOCK // LANES)
+            ]
+            found = mm(jnp.concatenate(picked, axis=1), held[b], NT)
+            gathered[pl.ds(start, WINDOW), :] += found.astype(jnp.bfloat16)
             return carry
 
         lax.fori_loop(0, windows, window, 0)
-        full = last // CHUNK
+        full = lax.shift_right_logical(last, CHUNK_BITS)
         lax.fori_loop(done, full, project, 0)
         return full
 
+    bounds_copy.wait()
     done = lax.fori_loop(0, blocks, take, 0)
-    used = (bounds[blocks] + CHUNK - 1) // CHUNK
+    used = lax.shift_right_logical(bounds[blocks, 0] + CHUNK - 1, CHUNK_BITS)
     lax.fori_loop(done, used, project, 0)
     lax.fori_loop(used, chunks, zero, 0)
 
@@ -375,9 +379,32 @@
     pooled_ref[0:texts, :] = pooled.astype(jnp.bfloat16)
 
 
+def pair_up(near, far, group):
+    first = jnp.where(group == 0, near, far)
+    return jnp.concatenate([first, jnp.where(group == 0, far, near)], axis=0)
+
+
+def dots_kernel(*refs, shards):
+    blocks, dots_ref = refs[:-1], refs[-1]
+    group = lax.axis_index("group")
+    dots = jnp.zeros(dots_ref.shape, jnp.float32)
+    pairs = [pair_up(blocks[o][...], blocks[o + shards][...], group) for o in range(shards)]
+    for o in (0, 2):
+        dots += mm(pairs[o], pairs[o], NT) + mm(pairs[o + 1], pairs[o + 1], NT)
+    dots_ref[...] = dots
+
+
 def score_kernel(
     ids_ref,
-    pooled_ref,
+    near0,
+    near1,
+    near2,
+    near3,
+    far0,
+    dots0,
+    dots1,
+    dots2,
+    dots3,
     misc_ref,
     slope_ref,
     reduced_ref,
@@ -386,26 +413,16 @@
     embed_ref,
     loss_ref,
     up_ref,
-    shards,
-    parts,
     negatives,
 ):
     texts, length = ids_ref.shape
     tokens = texts * length
     chunks = tokens // CHUNK
     rows = 2 * ROWS
-    width = pooled_ref.shape[2]
+    width = near0.shape[1]
     per_shard = loss_ref.shape[1]
-    group, shard, part = lax.axis_index("group"), lax.axis_index("dp"), lax.axis_index("mp")
-    places = shards * parts
-
-    def both(place):
-        return jnp.concatenate([pooled_ref[place], pooled_ref[places + place]], axis=0)
-
-    dots = jnp.zeros((rows, rows), jnp.float32)
-    for place in range(places):
-        block = both(place)
-        dots += mm(block, block, NT)
+    group, shard = lax.axis_index("group"), lax.axis_index("dp")
+    dots = (dots0[...] + dots1[...]) + (dots2[...] + dots3[...])
     down, across = iota((rows, rows), 0), iota((rows, rows), 1)
     same = down == across
     real = (lax.rem(down, ROWS) < texts) & (lax.rem(across, ROWS) < texts)
@@ -441,8 +458,7 @@
     )
     loss_ref[...] = jnp.sum(jnp.where(at, loss_col, 0.0), axis=0, keepdims=True)[:, 0:per_shard]
 
-    place = shard * parts + part
-    mine = both(place)
+    mine = pair_up(near0[...], far0[...], group)
     along = mm(coeff.astype(jnp.float32).T.astype(jnp.bfloat16), mine)
     radial_col = jnp.sum(jnp.where(same, radial, 0.0), axis=1, keepdims=True)
     grad = sharpness * (along - radial_col * mine.astype(jnp.float32))
@@ -462,11 +478,11 @@
     rnorm_own = jnp.where(group == 0, rnorm_col[0:ROWS], rnorm_col[ROWS:rows])
     chosen = iota((ROWS, ROWS), 1) == iota((ROWS, ROWS), 0) + first
     chosen = jnp.where(chosen & (iota((ROWS, ROWS), 0) < per_shard), 1.0, 0.0).astype(jnp.bfloat16)
-    for quarter in range(shards):
-        holder = quarter_of(quarter, 2)
-        block = pooled_ref[group * places + holder * parts + part].astype(jnp.float32) * rnorm_own
+    for o, near in enumerate((near0, near1, near2, near3)):
+        block = near[...].astype(jnp.float32) * rnorm_own
         picked = mm(chosen, block.astype(jnp.bfloat16)).astype(jnp.bfloat16)
-        embed_ref[0, :, quarter * width : (quarter + 1) * width] = picked[0:per_shard]
+        at = pl.multiple_of(quarter_of(shard ^ o) * width, LANES)
+        embed_ref[0, :, pl.ds(at, width)] = picked[0:per_shard]
 
 
 def any_spec():
@@ -479,6 +495,11 @@
 
 def smem_spec():
     return pl.BlockSpec(memory_space=pltpu.SMEM)
+
+
+def exchange(x, axes, size):
+    steps = [[(i, i ^ o) for i in range(size)] for o in range(1, size)]
+    return [x] + [lax.ppermute(x, axes, step) for step in steps]
 
 
 def split_body(
@@ -497,6 +518,7 @@
     chunks = tokens // CHUNK
     features, vocab = vocabulary_vectors.shape
     blocks = vocab // IDS_PER_BLOCK
+    block_rows = 8 * pl.cdiv(blocks + 1, 8)
     per_shard, negatives = difficult_distractors.shape
     rank = lowering_factor_matrix.shape[0]
     part_width = layer_weight_matrix.shape[1]
@@ -513,15 +535,17 @@
             pltpu.VMEM((blocks, features, IDS_PER_BLOCK), jnp.bfloat16),
             pltpu.VMEM((4, features, width), jnp.bfloat16),
             pltpu.VMEM((rank, features), jnp.bfloat16),
-            pltpu.VMEM((tokens + WINDOW, features), jnp.float32),
+            pltpu.VMEM((tokens + WINDOW, features), jnp.bfloat16),
             pltpu.VMEM((tokens + WINDOW, LANES), jnp.int32),
             pltpu.VMEM((LANES, LANES), jnp.float32),
             pltpu.VMEM((texts, length), jnp.float32),
             pltpu.VMEM((8, width), jnp.float32),
             pltpu.VMEM((ROWS, features), jnp.float32),
-            pltpu.SMEM((blocks + 1,), jnp.int32),
+            pltpu.VMEM((block_rows, length), jnp.int32),
+            pltpu.SMEM((block_rows, length), jnp.int32),
             pltpu.SemaphoreType.DMA((blocks,)),
             pltpu.SemaphoreType.DMA((4,)),
+            pltpu.SemaphoreType.DMA,
             pltpu.SemaphoreType.DMA,
         ],
         compiler_params=params,
@@ -553,21 +577,32 @@
         compiler_params=params,
         name="pool",
     )(ids, own0, core0, far, member, raising_factor_matrix)
-    gathered = lax.all_gather(pooled, ("group", "dp", "mp"), axis=0)
+    blocks8 = exchange(pooled, ("group", "dp"), 2 * shards)
+    dots = pl.pallas_call(
+        functools.partial(dots_kernel, shards=shards),
+        out_shape=jax.ShapeDtypeStruct((2 * ROWS, 2 * ROWS), jnp.float32),
+        in_specs=[vmem_spec()] * 8,
+        out_specs=vmem_spec(),
+        compiler_params=params,
+        name="dots",
+    )(*blocks8)
+    dots4 = exchange(dots, "mp", parts)
     embeddings, losses, update = pl.pallas_call(
-        functools.partial(score_kernel, shards=shards, parts=parts, negatives=negatives),
+        functools.partial(score_kernel, negatives=negatives),
         out_shape=[
             jax.ShapeDtypeStruct((1, per_shard, part_width), jnp.bfloat16),
             jax.ShapeDtypeStruct((1, per_shard), jnp.float32),
             jax.ShapeDtypeStruct((ROWS, width), jnp.float32),
         ],
-        in_specs=[vmem_spec()] * 6 + [smem_spec()],
+        in_specs=[vmem_spec()] * 14 + [smem_spec()],
         out_specs=[vmem_spec()] * 3,
         compiler_params=params,
         name="score",
-    )(ids, gathered, misc, slope, reduced, member, logit_sharpness)
-    updates = lax.all_gather(update, ("group", "dp"), axis=0)
-    columns = [updates[quarter_of(q)] + updates[shards + quarter_of(q)] for q in range(shards)]
+    )(ids, *blocks8[:5], *dots4, misc, slope, reduced, member, logit_sharpness)
+    updates = exchange(update, ("group", "dp"), 2 * shards)
+    sums = [updates[o] + updates[o + shards] for o in range(shards)]
+    shard = lax.axis_index("dp")
+    columns = [lax.select_n(shard ^ quarter_of(q), *sums) for q in range(shards)]
     return (embeddings, losses, jnp.concatenate(columns, axis=1))
 
 

time: 153 us -> 102 us (0.67)
  blocking collectives: 83.4 us -> 0 us
  starting transfers between devices: 3.55 us -> 21.1 us
  waiting for transfers between devices: 20.7 us -> 32.1 us
    all_gather x2 -> x0, blocking collectives: 83.4 us -> none  [the longest x1 75.1 us: split_body(): gathered = lax.all_gather(pooled, ('group', 'dp', 'mp'), axis=0)]
    ppermute x0 -> x17, starting transfers between devices: none -> 17.5 us  [exchange(): return [x] + [lax.ppermute(x, axes, step) for step in steps]]
    ppermute x0 -> x17, waiting for transfers between devices: none -> 10.7 us  [exchange(): return [x] + [lax.ppermute(x, axes, step) for step in steps]]
    pallas_call x1 -> x2, Pallas kernels: 3.85 us -> 5.28 us  [the longest x1 3.73 us: split_body(): pl.pallas_call(functools.partial(score_kernel, negatives=negatives), out_...]
    unnamed x5 -> x25, local copies, waits for them, and re-layouts: 2.22 us -> 3.4 us
  transfers between devices with their start and end apart: 3 -> 20, of which waited for: 2 -> 10; matrix products, arithmetic and copies ran while one was open for 1% -> 1% of each run, Pallas kernels for 0% -> 0%
where the time goes in v2:
time: 102 us; the launch traced here: 101 us
  Pallas kernels  40.6 us (40%)
  waiting for transfers between devices  32.1 us (31%)
  starting transfers between devices  21.1 us (21%)
  local copies, waits for them, and re-layouts  3.4 us (3%)
  other arithmetic  2.79 us (3%)
  between operations  1.4 us (1%)
    pallas_call x1, Pallas kernels, split_body(): pl.pallas_call(project_kernel, out_shape=[half] * 4 + [jax.ShapeDtypeStru...  31 us
    ppermute x1, waiting for transfers between devices, split_body(): far = lax.ppermute(chip1, 'dp', other_y)  19.2 us
    ppermute x17, starting transfers between devices, exchange(): return [x] + [lax.ppermute(x, axes, step) for step in steps]  17.5 us
    ppermute x17, waiting for transfers between devices, exchange(): return [x] + [lax.ppermute(x, axes, step) for step in steps]  10.7 us
    pallas_call x1, Pallas kernels, split_body(): pl.pallas_call(functools.partial(pool_kernel, model_width=float(features...  4.25 us
    pallas_call x1, Pallas kernels, split_body(): pl.pallas_call(functools.partial(score_kernel, negatives=negatives), out_...  3.73 us
    unnamed x25, local copies, waits for them, and re-layouts  3.4 us
    ppermute x1, starting transfers between devices, split_body(): far = lax.ppermute(chip1, 'dp', other_y)  2.95 us
  transfers between devices with their start and end apart: 20, of which 10 were waited for; matrix products, arithmetic and copies ran while one was open for 1% of the time, Pallas kernels for 0%

profile of v2, /device:TPU:0, one launch (start us, length us, event | category | flops | bytes accessed | tf_op | source)
XLA Modules:
  0.0 101.3 jit_solution(18017044312992879202)
XLA Ops:
  0.6 1.3 %copy.12 = s32[1,12,128]{2,1,0:T(8,128)} copy(s32[1,12,128]{2,0,1:T(1,128)} %param.7) | data formatting | bytes 12288
  1.9 31.0 %project.1 = (bf16[1664,256]{1,0:T(8,128)(2,1)}, bf16[1664,256]{1,0:T(8,128)(2,1)}, bf16[1664,256]{1,0:T(8,128)(2,1)}, bf16[1664,256]{1,0:T(8,128)(2,1)}, bf16[1536,128]{1,0:T(8,128)(2,1)}) custom-call(s32[12,128]{1,0:T(8,128)} %bitcast.3, s32[3,7]{1,0:T(4,128)} %hard_ref.1, bf16[1024,16384]{1,0:T(8,128)(2,1)} %vocab_ref.1, bf16[1024,1024]{1,0:T(8,128)(2,1)} %weight_ref.1, ...), custom_call_target="tpu_custom_call" | custom-call | tf_op jit(solution)/shard_map/project/pallas_call | solution.py:529
  33.6 2.1 %collective-permute-done.1 = bf16[1664,256]{1,0:T(8,128)(2,1)S(1)} collective-permute-done((bf16[1664,256]{1,0:T(8,128)(2,1)}, bf16[1664,256]{1,0:T(8,128)(2,1)S(1)}, u32[]{:S(2)}, u32[]{:S(2)}) %collective-permute-start.1) | collective-permute-done | bytes 852000 | tf_op jit(solution)/shard_map/ppermute | solution.py:562
  35.7 1.4 %add_convert_fusion = bf16[1664,256]{1,0:T(8,128)(2,1)S(1)} fusion(bf16[1664,256]{1,0:T(8,128)(2,1)S(1)} %collective-permute-done.1, bf16[1664,256]{1,0:T(8,128)(2,1)} %get-tuple-element.17), kind=kLoop, calls=%fused_computation | loop fusion | flops 1703936 | bytes 2555904 | tf_op jit(solution)/shard_map/convert_element_type | solution.py:564
  37.1 3.0 %collective-permute-start.2 = (bf16[1664,256]{1,0:T(8,128)(2,1)S(1)}, bf16[1664,256]{1,0:T(8,128)(2,1)S(1)}, u32[]{:S(2)}, u32[]{:S(2)}) collective-permute-start(bf16[1664,256]{1,0:T(8,128)(2,1)S(1)} %add_convert_fusion), channel_id=1, source_target_pairs={{0,8},{4,12},{8,0},{12,4},{1,9},{5,13},{9,1},{13,5},{2,10},{6,14},... | collective-permute-start | bytes 2555912 | tf_op jit(solution)/shard_map/ppermute | solution.py:565
  40.1 19.2 %collective-permute-done.2.far_ref = bf16[1664,256]{1,0:T(8,128)(2,1)S(1)} collective-permute-done((bf16[1664,256]{1,0:T(8,128)(2,1)S(1)}, bf16[1664,256]{1,0:T(8,128)(2,1)S(1)}, u32[]{:S(2)}, u32[]{:S(2)}) %collective-permute-start.2) | collective-permute-done | bytes 852000 | tf_op jit(solution)/shard_map/ppermute | solution.py:565
  59.3 0.9 copy-done.1
  60.2 4.2 %pool.1 = (bf16[16,256]{1,0:T(8,128)(2,1)}, f32[1536,256]{1,0:T(8,128)}, bf16[16,1536]{1,0:T(8,128)(2,1)}, f32[16,256]{1,0:T(8,128)}) custom-call(s32[12,128]{1,0:T(8,128)} %bitcast.4, bf16[1664,256]{1,0:T(8,128)(2,1)} %get-tuple-element.15.own_ref, bf16[1664,256]{1,0:T(8,128)(2,1)} %copy-done, bf16[1664,256]{1,0:T(8,128)(2,1)} %copy-done.1, ...), custom_call_target="tpu_custom_call" | custom-call | tf_op jit(solution)/shard_map/pool/pallas_call | solution.py:566
  64.5 1.8 %collective-permute-start.4 = (bf16[16,256]{1,0:T(8,128)(2,1)}, bf16[16,256]{1,0:T(8,128)(2,1)S(1)}, u32[]{:S(2)}, u32[]{:S(2)}) collective-permute-start(bf16[16,256]{1,0:T(8,128)(2,1)} %get-tuple-element.20.refs_0_.near0), channel_id=1, source_target_pairs={{0,8},{4,12},{8,0},{12,4},{16,24},{20,28},{24,16},{28,20},{1,9},{5... | collective-permute-start | bytes 24584 | tf_op jit(solution)/shard_map/ppermute | solution.py:502
  66.4 1.7 %collective-permute-start.6 = (bf16[16,256]{1,0:T(8,128)(2,1)}, bf16[16,256]{1,0:T(8,128)(2,1)S(1)}, u32[]{:S(2)}, u32[]{:S(2)}) collective-permute-start(bf16[16,256]{1,0:T(8,128)(2,1)} %get-tuple-element.20.refs_0_.near0), channel_id=1, source_target_pairs={{0,16},{4,20},{8,24},{12,28},{16,0},{20,4},{24,8},{28,12},{1,17},{... | collective-permute-start | bytes 24584 | tf_op jit(solution)/shard_map/ppermute | solution.py:502
  68.1 2.6 %collective-permute-start.8 = (bf16[16,256]{1,0:T(8,128)(2,1)}, bf16[16,256]{1,0:T(8,128)(2,1)S(1)}, u32[]{:S(2)}, u32[]{:S(2)}) collective-permute-start(bf16[16,256]{1,0:T(8,128)(2,1)} %get-tuple-element.20.refs_0_.near0), channel_id=1, source_target_pairs={{0,24},{4,28},{8,16},{12,20},{16,8},{20,12},{24,0},{28,4},{1,25},{... | collective-permute-start | bytes 24584 | tf_op jit(solution)/shard_map/ppermute | solution.py:502
  71.3 1.6 %collective-permute-done.8.refs_6_ = bf16[16,256]{1,0:T(8,128)(2,1)S(1)} collective-permute-done((bf16[16,256]{1,0:T(8,128)(2,1)}, bf16[16,256]{1,0:T(8,128)(2,1)S(1)}, u32[]{:S(2)}, u32[]{:S(2)}) %collective-permute-start.8) | collective-permute-done | bytes 8224 | tf_op jit(solution)/shard_map/ppermute | solution.py:502
  72.9 2.0 %collective-permute-done.9.refs_7_ = bf16[16,256]{1,0:T(8,128)(2,1)S(1)} collective-permute-done((bf16[16,256]{1,0:T(8,128)(2,1)}, bf16[16,256]{1,0:T(8,128)(2,1)S(1)}, u32[]{:S(2)}, u32[]{:S(2)}) %collective-permute-start.9) | collective-permute-done | bytes 8224 | tf_op jit(solution)/shard_map/ppermute | solution.py:502
  75.5 1.6 %dots.1.dots0 = f32[32,32]{1,0:T(8,128)} custom-call(bf16[16,256]{1,0:T(8,128)(2,1)} %get-tuple-element.20.refs_0_.near0, bf16[16,256]{1,0:T(8,128)(2,1)} %copy-done.2, bf16[16,256]{1,0:T(8,128)(2,1)} %copy-done.3, bf16[16,256]{1,0:T(8,128)(2,1)} %copy-done.4, bf16[16,256]{1,0:T(8,128)(2,1)} %copy-done.5, bf16[16,256]{1,0:T(8,128)(2,1)} %copy-done.9, ...), custom_call_target="tpu_custom_call" | custom-call | tf_op jit(solution)/shard_map/dots/pallas_call | solution.py:581
  77.1 1.6 %collective-permute-start.10 = (f32[32,32]{1,0:T(8,128)}, f32[32,32]{1,0:T(8,128)S(1)}, u32[]{:S(2)}, u32[]{:S(2)}) collective-permute-start(f32[32,32]{1,0:T(8,128)} %dots.1.dots0), channel_id=1, source_target_pairs={{0,1},{1,0},{2,3},{3,2},{4,5},{5,4},{6,7},{7,6},{8,9},{9,8},{10,11... | collective-permute-start | bytes 12296 | tf_op jit(solution)/shard_map/ppermute | solution.py:502
  78.6 2.6 %collective-permute-start.11 = (f32[32,32]{1,0:T(8,128)}, f32[32,32]{1,0:T(8,128)S(1)}, u32[]{:S(2)}, u32[]{:S(2)}) collective-permute-start(f32[32,32]{1,0:T(8,128)} %dots.1.dots0), channel_id=1, source_target_pairs={{0,2},{1,3},{2,0},{3,1},{4,6},{5,7},{6,4},{7,5},{8,10},{9,11},{10,... | collective-permute-start | bytes 12296 | tf_op jit(solution)/shard_map/ppermute | solution.py:502
  82.1 1.4 %collective-permute-done.11.dots2 = f32[32,32]{1,0:T(8,128)S(1)} collective-permute-done((f32[32,32]{1,0:T(8,128)}, f32[32,32]{1,0:T(8,128)S(1)}, u32[]{:S(2)}, u32[]{:S(2)}) %collective-permute-start.11) | collective-permute-done | bytes 4128 | tf_op jit(solution)/shard_map/ppermute | solution.py:502
  83.5 3.4 %collective-permute-done.12.dots3 = f32[32,32]{1,0:T(8,128)S(1)} collective-permute-done((f32[32,32]{1,0:T(8,128)}, f32[32,32]{1,0:T(8,128)S(1)}, u32[]{:S(2)}, u32[]{:S(2)}) %collective-permute-start.12) | collective-permute-done | bytes 4128 | tf_op jit(solution)/shard_map/ppermute | solution.py:502
  87.6 3.7 %score.1 = (bf16[1,3,1024]{2,1,0:T(4,128)(2,1)}, f32[1,3]{1,0:T(1,128)}, f32[16,256]{1,0:T(8,128)}) custom-call(s32[12,128]{1,0:T(8,128)} %bitcast.5, bf16[16,256]{1,0:T(8,128)(2,1)} %get-tuple-element.20.refs_0_.near0, bf16[16,256]{1,0:T(8,128)(2,1)} %copy-done.2, bf16[16,256]{1,0:T(8,128)(2,1)} %copy-done.3, bf16[16,256]{1,0:T(8,128)(2,1)} %copy-done.4, ...), custom_call_target="tpu_custom_call" | custom-call | tf_op jit(solution)/shard_map/score/pallas_call | solution.py:590
  91.8 1.6 %collective-permute-start.15 = (f32[16,256]{1,0:T(8,128)}, f32[16,256]{1,0:T(8,128)S(1)}, u32[]{:S(2)}, u32[]{:S(2)}) collective-permute-start(f32[16,256]{1,0:T(8,128)} %get-tuple-element.26), channel_id=1, source_target_pairs={{0,20},{4,16},{8,28},{12,24},{16,4},{20,0},{24,12},{28,8},{1,21},{... | collective-permute-start | bytes 49160 | tf_op jit(solution)/shard_map/ppermute | solution.py:502
  93.9 1.5 %collective-permute-start.17 = (f32[16,256]{1,0:T(8,128)}, f32[16,256]{1,0:T(8,128)S(1)}, u32[]{:S(2)}, u32[]{:S(2)}) collective-permute-start(f32[16,256]{1,0:T(8,128)} %get-tuple-element.26), channel_id=1, source_target_pairs={{0,24},{4,28},{8,16},{12,20},{16,8},{20,12},{24,0},{28,4},{1,25},{... | collective-permute-start | bytes 49160 | tf_op jit(solution)/shard_map/ppermute | solution.py:502
  95.6 2.5 %collective-permute-start.19 = (f32[16,256]{1,0:T(8,128)}, f32[16,256]{1,0:T(8,128)S(1)}, u32[]{:S(2)}, u32[]{:S(2)}) collective-permute-start(f32[16,256]{1,0:T(8,128)} %get-tuple-element.26), channel_id=1, source_target_pairs={{0,28},{4,24},{8,20},{12,16},{16,12},{20,8},{24,4},{28,0},{1,29},{... | collective-permute-start | bytes 49160 | tf_op jit(solution)/shard_map/ppermute | solution.py:502
  99.0 0.9 collective-permute-done.19
  99.9 0.7 select_select_fusion.3
  (49 shorter events, 5.5 us)
Async XLA Ops:
  33.0 2.7 %collective-permute-start.1 = (bf16[1664,256]{1,0:T(8,128)(2,1)}, bf16[1664,256]{1,0:T(8,128)(2,1)S(1)}, u32[]{:S(2)}, u32[]{:S(2)}) collective-permute-start(bf16[1664,256]{1,0:T(8,128)(2,1)} %get-tuple-element.18), channel_id=1, source_target_pairs={{0,4},{4,0},{8,12},{12,8},{1,5},{5,1},{9,13},{13,9},{2,6},{6,2},{1... | collective-permute-start | bytes 2555912 | tf_op jit(solution)/shard_map/ppermute | solution.py:562
  33.5 6.6 %collective-permute-start = (bf16[1664,256]{1,0:T(8,128)(2,1)}, bf16[1664,256]{1,0:T(8,128)(2,1)S(1)}, u32[]{:S(2)}, u32[]{:S(2)}) collective-permute-start(bf16[1664,256]{1,0:T(8,128)(2,1)} %get-tuple-element.16), channel_id=1, source_target_pairs={{0,4},{4,0},{8,12},{12,8},{1,5},{5,1},{9,13},{13,9},{2,6},{6,2},{1... | collective-permute-start | bytes 2555912 | tf_op jit(solution)/shard_map/ppermute | solution.py:563
  37.1 22.2 %collective-permute-start.2 = (bf16[1664,256]{1,0:T(8,128)(2,1)S(1)}, bf16[1664,256]{1,0:T(8,128)(2,1)S(1)}, u32[]{:S(2)}, u32[]{:S(2)}) collective-permute-start(bf16[1664,256]{1,0:T(8,128)(2,1)S(1)} %add_convert_fusion), channel_id=1, source_target_pairs={{0,8},{4,12},{8,0},{12,4},{1,9},{5,13},{9,1},{13,5},{2,10},{6,14},... | collective-permute-start | bytes 2555912 | tf_op jit(solution)/shard_map/ppermute | solution.py:565
  40.1 19.2 %copy-start = (bf16[1664,256]{1,0:T(8,128)(2,1)}, bf16[1664,256]{1,0:T(8,128)(2,1)S(1)}, u32[]{:S(2)}) copy-start(bf16[1664,256]{1,0:T(8,128)(2,1)S(1)} %collective-permute-done.core_ref) | copy-start | bytes 2555908
  64.5 3.6 %collective-permute-start.3 = (bf16[16,256]{1,0:T(8,128)(2,1)}, bf16[16,256]{1,0:T(8,128)(2,1)S(1)}, u32[]{:S(2)}, u32[]{:S(2)}) collective-permute-start(bf16[16,256]{1,0:T(8,128)(2,1)} %get-tuple-element.20.refs_0_.near0), channel_id=1, source_target_pairs={{0,4},{4,0},{8,12},{12,8},{16,20},{20,16},{24,28},{28,24},{1,5},{5... | collective-permute-start | bytes 24584 | tf_op jit(solution)/shard_map/ppermute | solution.py:502
  64.5 6.2 %collective-permute-start.4 = (bf16[16,256]{1,0:T(8,128)(2,1)}, bf16[16,256]{1,0:T(8,128)(2,1)S(1)}, u32[]{:S(2)}, u32[]{:S(2)}) collective-permute-start(bf16[16,256]{1,0:T(8,128)(2,1)} %get-tuple-element.20.refs_0_.near0), channel_id=1, source_target_pairs={{0,8},{4,12},{8,0},{12,4},{16,24},{20,28},{24,16},{28,20},{1,9},{5... | collective-permute-start | bytes 24584 | tf_op jit(solution)/shard_map/ppermute | solution.py:502
  66.3 4.6 %collective-permute-start.5 = (bf16[16,256]{1,0:T(8,128)(2,1)}, bf16[16,256]{1,0:T(8,128)(2,1)S(1)}, u32[]{:S(2)}, u32[]{:S(2)}) collective-permute-start(bf16[16,256]{1,0:T(8,128)(2,1)} %get-tuple-element.20.refs_0_.near0), channel_id=1, source_target_pairs={{0,12},{4,8},{8,4},{12,0},{16,28},{20,24},{24,20},{28,16},{1,13},{... | collective-permute-start | bytes 24584 | tf_op jit(solution)/shard_map/ppermute | solution.py:502
  66.4 4.5 %collective-permute-start.6 = (bf16[16,256]{1,0:T(8,128)(2,1)}, bf16[16,256]{1,0:T(8,128)(2,1)S(1)}, u32[]{:S(2)}, u32[]{:S(2)}) collective-permute-start(bf16[16,256]{1,0:T(8,128)(2,1)} %get-tuple-element.20.refs_0_.near0), channel_id=1, source_target_pairs={{0,16},{4,20},{8,24},{12,28},{16,0},{20,4},{24,8},{28,12},{1,17},{... | collective-permute-start | bytes 24584 | tf_op jit(solution)/shard_map/ppermute | solution.py:502
  68.0 3.3 %collective-permute-start.7 = (bf16[16,256]{1,0:T(8,128)(2,1)}, bf16[16,256]{1,0:T(8,128)(2,1)S(1)}, u32[]{:S(2)}, u32[]{:S(2)}) collective-permute-start(bf16[16,256]{1,0:T(8,128)(2,1)} %get-tuple-element.20.refs_0_.near0), channel_id=1, source_target_pairs={{0,20},{4,16},{8,28},{12,24},{16,4},{20,0},{24,12},{28,8},{1,21},{... | collective-permute-start | bytes 24584 | tf_op jit(solution)/shard_map/ppermute | solution.py:502
  68.1 6.8 %copy-start.2 = (bf16[16,256]{1,0:T(8,128)(2,1)}, bf16[16,256]{1,0:T(8,128)(2,1)S(1)}, u32[]{:S(2)}) copy-start(bf16[16,256]{1,0:T(8,128)(2,1)S(1)} %collective-permute-done.3.refs_1_.near1) | copy-start | bytes 24580
  68.1 4.8 %collective-permute-start.8 = (bf16[16,256]{1,0:T(8,128)(2,1)}, bf16[16,256]{1,0:T(8,128)(2,1)S(1)}, u32[]{:S(2)}, u32[]{:S(2)}) collective-permute-start(bf16[16,256]{1,0:T(8,128)(2,1)} %get-tuple-element.20.refs_0_.near0), channel_id=1, source_target_pairs={{0,24},{4,28},{8,16},{12,20},{16,8},{20,12},{24,0},{28,4},{1,25},{... | collective-permute-start | bytes 24584 | tf_op jit(solution)/shard_map/ppermute | solution.py:502
  70.7 4.2 %copy-start.3 = (bf16[16,256]{1,0:T(8,128)(2,1)}, bf16[16,256]{1,0:T(8,128)(2,1)S(1)}, u32[]{:S(2)}) copy-start(bf16[16,256]{1,0:T(8,128)(2,1)S(1)} %collective-permute-done.4.refs_2_.near2) | copy-start | bytes 24580
  70.7 4.2 %collective-permute-start.9 = (bf16[16,256]{1,0:T(8,128)(2,1)}, bf16[16,256]{1,0:T(8,128)(2,1)S(1)}, u32[]{:S(2)}, u32[]{:S(2)}) collective-permute-start(bf16[16,256]{1,0:T(8,128)(2,1)} %get-tuple-element.20.refs_0_.near0), channel_id=1, source_target_pairs={{0,28},{4,24},{8,20},{12,16},{16,12},{20,8},{24,4},{28,0},{1,29},{... | collective-permute-start | bytes 24584 | tf_op jit(solution)/shard_map/ppermute | solution.py:502
  77.1 5.0 %collective-permute-start.10 = (f32[32,32]{1,0:T(8,128)}, f32[32,32]{1,0:T(8,128)S(1)}, u32[]{:S(2)}, u32[]{:S(2)}) collective-permute-start(f32[32,32]{1,0:T(8,128)} %dots.1.dots0), channel_id=1, source_target_pairs={{0,1},{1,0},{2,3},{3,2},{4,5},{5,4},{6,7},{7,6},{8,9},{9,8},{10,11... | collective-permute-start | bytes 12296 | tf_op jit(solution)/shard_map/ppermute | solution.py:502
  78.6 4.9 %collective-permute-start.11 = (f32[32,32]{1,0:T(8,128)}, f32[32,32]{1,0:T(8,128)S(1)}, u32[]{:S(2)}, u32[]{:S(2)}) collective-permute-start(f32[32,32]{1,0:T(8,128)} %dots.1.dots0), channel_id=1, source_target_pairs={{0,2},{1,3},{2,0},{3,1},{4,6},{5,7},{6,4},{7,5},{8,10},{9,11},{10,... | collective-permute-start | bytes 12296 | tf_op jit(solution)/shard_map/ppermute | solution.py:502
  81.2 5.7 %collective-permute-start.12 = (f32[32,32]{1,0:T(8,128)}, f32[32,32]{1,0:T(8,128)S(1)}, u32[]{:S(2)}, u32[]{:S(2)}) collective-permute-start(f32[32,32]{1,0:T(8,128)} %dots.1.dots0), channel_id=1, source_target_pairs={{0,3},{1,2},{2,1},{3,0},{4,7},{5,6},{6,5},{7,4},{8,11},{9,10},{10,... | collective-permute-start | bytes 12296 | tf_op jit(solution)/shard_map/ppermute | solution.py:502
  82.1 4.9 %copy-start.6 = (f32[32,32]{1,0:T(8,128)}, f32[32,32]{1,0:T(8,128)S(1)}, u32[]{:S(2)}) copy-start(f32[32,32]{1,0:T(8,128)S(1)} %collective-permute-done.10.dots1) | copy-start | bytes 12292
  91.3 4.2 %collective-permute-start.13 = (f32[16,256]{1,0:T(8,128)}, f32[16,256]{1,0:T(8,128)S(1)}, u32[]{:S(2)}, u32[]{:S(2)}) collective-permute-start(f32[16,256]{1,0:T(8,128)} %get-tuple-element.26), channel_id=1, source_target_pairs={{0,16},{4,20},{8,24},{12,28},{16,0},{20,4},{24,8},{28,12},{1,17},{... | collective-permute-start | bytes 49160 | tf_op jit(solution)/shard_map/ppermute | solution.py:502
  91.8 3.8 %collective-permute-start.14 = (f32[16,256]{1,0:T(8,128)}, f32[16,256]{1,0:T(8,128)S(1)}, u32[]{:S(2)}, u32[]{:S(2)}) collective-permute-start(f32[16,256]{1,0:T(8,128)} %get-tuple-element.26), channel_id=1, source_target_pairs={{0,4},{4,0},{8,12},{12,8},{16,20},{20,16},{24,28},{28,24},{1,5},{5... | collective-permute-start | bytes 49160 | tf_op jit(solution)/shard_map/ppermute | solution.py:502
  91.8 6.3 %collective-permute-start.15 = (f32[16,256]{1,0:T(8,128)}, f32[16,256]{1,0:T(8,128)S(1)}, u32[]{:S(2)}, u32[]{:S(2)}) collective-permute-start(f32[16,256]{1,0:T(8,128)} %get-tuple-element.26), channel_id=1, source_target_pairs={{0,20},{4,16},{8,28},{12,24},{16,4},{20,0},{24,12},{28,8},{1,21},{... | collective-permute-start | bytes 49160 | tf_op jit(solution)/shard_map/ppermute | solution.py:502
  93.4 4.7 %collective-permute-start.16 = (f32[16,256]{1,0:T(8,128)}, f32[16,256]{1,0:T(8,128)S(1)}, u32[]{:S(2)}, u32[]{:S(2)}) collective-permute-start(f32[16,256]{1,0:T(8,128)} %get-tuple-element.26), channel_id=1, source_target_pairs={{0,8},{4,12},{8,0},{12,4},{16,24},{20,28},{24,16},{28,20},{1,9},{5... | collective-permute-start | bytes 49160 | tf_op jit(solution)/shard_map/ppermute | solution.py:502
  93.9 4.9 %collective-permute-start.17 = (f32[16,256]{1,0:T(8,128)}, f32[16,256]{1,0:T(8,128)S(1)}, u32[]{:S(2)}, u32[]{:S(2)}) collective-permute-start(f32[16,256]{1,0:T(8,128)} %get-tuple-element.26), channel_id=1, source_target_pairs={{0,24},{4,28},{8,16},{12,20},{16,8},{20,12},{24,0},{28,4},{1,25},{... | collective-permute-start | bytes 49160 | tf_op jit(solution)/shard_map/ppermute | solution.py:502
  95.4 3.5 %collective-permute-start.18 = (f32[16,256]{1,0:T(8,128)}, f32[16,256]{1,0:T(8,128)S(1)}, u32[]{:S(2)}, u32[]{:S(2)}) collective-permute-start(f32[16,256]{1,0:T(8,128)} %get-tuple-element.26), channel_id=1, source_target_pairs={{0,12},{4,8},{8,4},{12,0},{16,28},{20,24},{24,20},{28,16},{1,13},{... | collective-permute-start | bytes 49160 | tf_op jit(solution)/shard_map/ppermute | solution.py:502
  95.6 4.3 %collective-permute-start.19 = (f32[16,256]{1,0:T(8,128)}, f32[16,256]{1,0:T(8,128)S(1)}, u32[]{:S(2)}, u32[]{:S(2)}) collective-permute-start(f32[16,256]{1,0:T(8,128)} %get-tuple-element.26), channel_id=1, source_target_pairs={{0,28},{4,24},{8,20},{12,16},{16,12},{20,8},{24,4},{28,0},{1,29},{... | collective-permute-start | bytes 49160 | tf_op jit(solution)/shard_map/ppermute | solution.py:502
  (8 other events, 19.2 us)

commit v3 on v2

--- a/solution.py
+++ b/solution.py
@@ -116,6 +116,7 @@
 CHUNK = 1 << CHUNK_BITS
 ROWS = 1 << ROW_BITS
 LANES = 128
+PIECES = 4
 NT = (((1,), (1,)), ((), ()))
 VMEM_BYTES = 60 * 1024 * 1024
 
@@ -175,11 +176,11 @@
     shard = lax.axis_index("dp")
     core, side_y = lax.rem(shard, 2), lax.div(shard, 2)
 
-    def vocab_copy(b):
+    def vocab_copy(b, piece):
+        rows = pl.ds(piece * (features // PIECES), features // PIECES)
+        columns = pl.ds(pl.multiple_of(b * IDS_PER_BLOCK, LANES), IDS_PER_BLOCK)
         return pltpu.make_async_copy(
-            vocab_ref.at[:, pl.ds(pl.multiple_of(b * IDS_PER_BLOCK, LANES), IDS_PER_BLOCK)],
-            held.at[b],
-            held_sems.at[b],
+            vocab_ref.at[rows, columns], held.at[b, rows], held_sems.at[b, piece]
         )
 
     def weight_copy(i, j):
@@ -193,13 +194,15 @@
     lower_copy = pltpu.make_async_copy(
         lower_ref.at[:, pl.ds(pl.multiple_of(shard * features, LANES), features)], lower, lower_sem
     )
-    vocab_copy(0).start()
+    for piece in range(PIECES):
+        vocab_copy(0, piece).start()
     lower_copy.start()
     for i in range(2):
         for j in range(2):
             weight_copy(i, j).start()
     for b in range(1, blocks):
-        vocab_copy(b).start()
+        for piece in range(PIECES):
+            vocab_copy(b, piece).start()
 
     ids = ids_ref[...]
     valid = ids != 0
@@ -276,7 +279,8 @@
         return carry
 
     def take(b, done):
-        vocab_copy(b).wait()
+        for piece in range(PIECES):
+            vocab_copy(b, piece).wait()
         first, last = bounds[b, 0], bounds[b + 1, 0]
         aligned = lax.shift_left(lax.shift_right_logical(first, ROW_BITS), ROW_BITS)
         windows = lax.shift_right_logical(last - aligned + WINDOW - 1, WINDOW_BITS)
@@ -375,36 +379,29 @@
     total += summed(tokens + (chunks + 1) * ROWS, ROWS)
     counts = jnp.sum((ids_ref[...] != 0).astype(jnp.float32), axis=1, keepdims=True)
     pooled = total[0:texts] / counts
-    pooled_ref[...] = jnp.zeros_like(pooled_ref)
-    pooled_ref[0:texts, :] = pooled.astype(jnp.bfloat16)
-
-
-def pair_up(near, far, group):
-    first = jnp.where(group == 0, near, far)
-    return jnp.concatenate([first, jnp.where(group == 0, far, near)], axis=0)
-
-
-def dots_kernel(*refs, shards):
-    blocks, dots_ref = refs[:-1], refs[-1]
-    group = lax.axis_index("group")
-    dots = jnp.zeros(dots_ref.shape, jnp.float32)
-    pairs = [pair_up(blocks[o][...], blocks[o + shards][...], group) for o in range(shards)]
-    for o in (0, 2):
-        dots += mm(pairs[o], pairs[o], NT) + mm(pairs[o + 1], pairs[o + 1], NT)
-    dots_ref[...] = dots
+    pooled = jnp.concatenate([pooled, jnp.zeros((ROWS - texts, width), jnp.float32)])
+    for to in range(pooled_ref.shape[0]):
+        pooled_ref[to] = pooled.astype(jnp.bfloat16)
+
+
+def both_sides(pooled_ref, shard, shards):
+    return jnp.concatenate([pooled_ref[shard], pooled_ref[shards + shard]], axis=0)
+
+
+def dots_kernel(pooled_ref, dots_ref, shards):
+    dots = jnp.zeros((2 * ROWS, 2 * ROWS), jnp.float32)
+    for shard in range(shards):
+        block = both_sides(pooled_ref, shard, shards)
+        dots += mm(block, block, NT)
+    wide = jnp.concatenate([dots, jnp.zeros((2 * ROWS, LANES - 2 * ROWS), jnp.float32)], axis=1)
+    for to in range(dots_ref.shape[0]):
+        dots_ref[to] = wide
 
 
 def score_kernel(
     ids_ref,
-    near0,
-    near1,
-    near2,
-    near3,
-    far0,
-    dots0,
-    dots1,
-    dots2,
-    dots3,
+    pooled_ref,
+    dots_ref,
     misc_ref,
     slope_ref,
     reduced_ref,
@@ -413,16 +410,20 @@
     embed_ref,
     loss_ref,
     up_ref,
+    shards,
     negatives,
 ):
     texts, length = ids_ref.shape
     tokens = texts * length
     chunks = tokens // CHUNK
     rows = 2 * ROWS
-    width = near0.shape[1]
+    width = pooled_ref.shape[2]
     per_shard = loss_ref.shape[1]
     group, shard = lax.axis_index("group"), lax.axis_index("dp")
-    dots = (dots0[...] + dots1[...]) + (dots2[...] + dots3[...])
+    dots = dots_ref[0]
+    for part in range(1, dots_ref.shape[0]):
+        dots += dots_ref[part]
+    dots = dots[:, 0:rows]
     down, across = iota((rows, rows), 0), iota((rows, rows), 1)
     same = down == across
     real = (lax.rem(down, ROWS) < texts) & (lax.rem(across, ROWS) < texts)
@@ -458,7 +459,7 @@
     )
     loss_ref[...] = jnp.sum(jnp.where(at, loss_col, 0.0), axis=0, keepdims=True)[:, 0:per_shard]
 
-    mine = pair_up(near0[...], far0[...], group)
+    mine = both_sides(pooled_ref, shard, shards)
     along = mm(coeff.astype(jnp.float32).T.astype(jnp.bfloat16), mine)
     radial_col = jnp.sum(jnp.where(same, radial, 0.0), axis=1, keepdims=True)
     grad = sharpness * (along - radial_col * mine.astype(jnp.float32))
@@ -473,16 +474,16 @@
         token_grad = mm(member, high) + mm(member, rest)
         local = (token_grad * slope_ref[pl.ds(k * CHUNK, CHUNK), :]).astype(jnp.bfloat16)
         update += mm(reduced_ref[:, k * CHUNK : (k + 1) * CHUNK], local)
-    up_ref[...] = update
+    for to in range(up_ref.shape[0]):
+        up_ref[to] = update
 
     rnorm_own = jnp.where(group == 0, rnorm_col[0:ROWS], rnorm_col[ROWS:rows])
     chosen = iota((ROWS, ROWS), 1) == iota((ROWS, ROWS), 0) + first
     chosen = jnp.where(chosen & (iota((ROWS, ROWS), 0) < per_shard), 1.0, 0.0).astype(jnp.bfloat16)
-    for o, near in enumerate((near0, near1, near2, near3)):
-        block = near[...].astype(jnp.float32) * rnorm_own
+    for quarter in range(shards):
+        block = pooled_ref[group * shards + quarter_of(quarter)].astype(jnp.float32) * rnorm_own
         picked = mm(chosen, block.astype(jnp.bfloat16)).astype(jnp.bfloat16)
-        at = pl.multiple_of(quarter_of(shard ^ o) * width, LANES)
-        embed_ref[0, :, pl.ds(at, width)] = picked[0:per_shard]
+        embed_ref[0, :, quarter * width : (quarter + 1) * width] = picked[0:per_shard]
 
 
 def any_spec():
@@ -495,11 +496,6 @@
 
 def smem_spec():
     return pl.BlockSpec(memory_space=pltpu.SMEM)
-
-
-def exchange(x, axes, size):
-    steps = [[(i, i ^ o) for i in range(size)] for o in range(1, size)]
-    return [x] + [lax.ppermute(x, axes, step) for step in steps]
 
 
 def split_body(
@@ -543,7 +539,7 @@
             pltpu.VMEM((ROWS, features), jnp.float32),
             pltpu.VMEM((block_rows, length), jnp.int32),
             pltpu.SMEM((block_rows, length), jnp.int32),
-            pltpu.SemaphoreType.DMA((blocks,)),
+            pltpu.SemaphoreType.DMA((blocks, PIECES)),
             pltpu.SemaphoreType.DMA((4,)),
             pltpu.SemaphoreType.DMA,
             pltpu.SemaphoreType.DMA,
@@ -566,7 +562,7 @@
     pooled, slope, reduced, misc = pl.pallas_call(
         functools.partial(pool_kernel, model_width=float(features * shards)),
         out_shape=[
-            jax.ShapeDtypeStruct((ROWS, width), jnp.bfloat16),
+            jax.ShapeDtypeStruct((2 * shards, ROWS, width), jnp.bfloat16),
             jax.ShapeDtypeStruct((tokens, width), jnp.float32),
             jax.ShapeDtypeStruct((ROWS, tokens), jnp.bfloat16),
             jax.ShapeDtypeStruct((ROWS, width), jnp.float32),
@@ -577,32 +573,31 @@
         compiler_params=params,
         name="pool",
     )(ids, own0, core0, far, member, raising_factor_matrix)
-    blocks8 = exchange(pooled, ("group", "dp"), 2 * shards)
+    sides = ("group", "dp")
+    pooled = lax.all_to_all(pooled, sides, 0, 0)
     dots = pl.pallas_call(
         functools.partial(dots_kernel, shards=shards),
-        out_shape=jax.ShapeDtypeStruct((2 * ROWS, 2 * ROWS), jnp.float32),
-        in_specs=[vmem_spec()] * 8,
+        out_shape=jax.ShapeDtypeStruct((parts, 2 * ROWS, LANES), jnp.float32),
+        in_specs=[vmem_spec()],
         out_specs=vmem_spec(),
         compiler_params=params,
         name="dots",
-    )(*blocks8)
-    dots4 = exchange(dots, "mp", parts)
+    )(pooled)
+    dots = lax.all_to_all(dots, "mp", 0, 0)
     embeddings, losses, update = pl.pallas_call(
-        functools.partial(score_kernel, negatives=negatives),
+        functools.partial(score_kernel, shards=shards, negatives=negatives),
         out_shape=[
             jax.ShapeDtypeStruct((1, per_shard, part_width), jnp.bfloat16),
             jax.ShapeDtypeStruct((1, per_shard), jnp.float32),
-            jax.ShapeDtypeStruct((ROWS, width), jnp.float32),
+            jax.ShapeDtypeStruct((2 * shards, ROWS, width), jnp.float32),
         ],
-        in_specs=[vmem_spec()] * 14 + [smem_spec()],
+        in_specs=[vmem_spec()] * 7 + [smem_spec()],
         out_specs=[vmem_spec()] * 3,
         compiler_params=params,
         name="score",
-    )(ids, *blocks8[:5], *dots4, misc, slope, reduced, member, logit_sharpness)
-    updates = exchange(update, ("group", "dp"), 2 * shards)
-    sums = [updates[o] + updates[o + shards] for o in range(shards)]
-    shard = lax.axis_index("dp")
-    columns = [lax.select_n(shard ^ quarter_of(q), *sums) for q in range(shards)]
+    )(ids, pooled, dots, misc, slope, reduced, member, logit_sharpness)
+    update = lax.all_to_all(update, sides, 0, 0)
+    columns = [update[quarter_of(q)] + update[shards + quarter_of(q)] for q in range(shards)]
     return (embeddings, losses, jnp.concatenate(columns, axis=1))
 
 

time: 102 us -> 102 us (level)
  blocking collectives: 0 us -> 18.3 us
  starting transfers between devices: 21.1 us -> 8.42 us
  waiting for transfers between devices: 32.1 us -> 26.5 us
  Pallas kernels: 40.6 us -> 41.7 us
    all_to_all x0 -> x2, blocking collectives: none -> 18.3 us  [the longest x1 9.81 us: split_body(): pooled = lax.all_to_all(pooled, sides, 0, 0)]
    ppermute x17 -> x0, starting transfers between devices: 17.5 us -> none  [exchange(): return [x] + [lax.ppermute(x, axes, step) for step in steps]]
    ppermute x17 -> x0, waiting for transfers between devices: 10.7 us -> none  [exchange(): return [x] + [lax.ppermute(x, axes, step) for step in steps]]
    all_to_all x0 -> x1, waiting for transfers between devices: none -> 5.09 us  [split_body(): dots = lax.all_to_all(dots, 'mp', 0, 0)]
    all_to_all x0 -> x1, starting transfers between devices: none -> 4.87 us  [split_body(): dots = lax.all_to_all(dots, 'mp', 0, 0)]
    unnamed x25 -> x7, local copies, waits for them, and re-layouts: 3.4 us -> 2.84 us
  transfers between devices with their start and end apart: 20 -> 4, of which waited for: 10 -> 3; matrix products, arithmetic and copies ran while one was open for 1% -> 1% of each run, Pallas kernels for 0% -> 0%
where the time goes in v3:
time: 102 us; the launch traced here: 101 us
  Pallas kernels  41.7 us (41%)
  waiting for transfers between devices  26.5 us (26%)
  blocking collectives  18.3 us (18%)
  starting transfers between devices  8.42 us (8%)
  local copies, waits for them, and re-layouts  2.84 us (3%)
  other arithmetic  2.06 us (2%)
  between operations  1.3 us (1%)
    pallas_call x1, Pallas kernels, split_body(): pl.pallas_call(project_kernel, out_shape=[half] * 4 + [jax.ShapeDtypeStru...  32 us
    ppermute x1, waiting for transfers between devices, split_body(): far = lax.ppermute(chip1, 'dp', other_y)  19.2 us
    all_to_all x1, blocking collectives, split_body(): pooled = lax.all_to_all(pooled, sides, 0, 0)  9.81 us
    all_to_all x1, blocking collectives, split_body(): update = lax.all_to_all(update, sides, 0, 0)  8.45 us
    all_to_all x1, waiting for transfers between devices, split_body(): dots = lax.all_to_all(dots, 'mp', 0, 0)  5.09 us
    all_to_all x1, starting transfers between devices, split_body(): dots = lax.all_to_all(dots, 'mp', 0, 0)  4.87 us
    pallas_call x1, Pallas kernels, split_body(): pl.pallas_call(functools.partial(pool_kernel, model_width=float(features...  4.26 us
    pallas_call x1, Pallas kernels, split_body(): pl.pallas_call(functools.partial(score_kernel, shards=shards, negatives=n...  3.77 us
  transfers between devices with their start and end apart: 4, of which 3 were waited for; matrix products, arithmetic and copies ran while one was open for 1% of the time, Pallas kernels for 0%

profile of v3, /device:TPU:0, one launch (start us, length us, event | category | flops | bytes accessed | tf_op | source)
XLA Modules:
  0.0 101.1 jit_solution(7758575447903785063)
XLA Ops:
  0.6 1.3 %copy.12 = s32[1,12,128]{2,1,0:T(8,128)} copy(s32[1,12,128]{2,0,1:T(1,128)} %param.7) | data formatting | bytes 12288
  1.9 32.0 %project.1 = (bf16[1664,256]{1,0:T(8,128)(2,1)}, bf16[1664,256]{1,0:T(8,128)(2,1)}, bf16[1664,256]{1,0:T(8,128)(2,1)}, bf16[1664,256]{1,0:T(8,128)(2,1)}, bf16[1536,128]{1,0:T(8,128)(2,1)}) custom-call(s32[12,128]{1,0:T(8,128)} %bitcast.11, s32[3,7]{1,0:T(4,128)} %hard_ref.1, bf16[1024,16384]{1,0:T(8,128)(2,1)} %vocab_ref.1, bf16[1024,1024]{1,0:T(8,128)(2,1)} %weight_ref.1, ...), custom_call_target="tpu_custom_call" | custom-call | tf_op jit(solution)/shard_map/project/pallas_call | solution.py:525
  34.0 0.5 collective-permute-start.1
  34.5 0.1 collective-permute-start
  34.5 2.1 %collective-permute-done.1 = bf16[1664,256]{1,0:T(8,128)(2,1)S(1)} collective-permute-done((bf16[1664,256]{1,0:T(8,128)(2,1)}, bf16[1664,256]{1,0:T(8,128)(2,1)S(1)}, u32[]{:S(2)}, u32[]{:S(2)}) %collective-permute-start.1) | collective-permute-done | bytes 852000 | tf_op jit(solution)/shard_map/ppermute | solution.py:558
  36.7 1.4 %add_convert_fusion = bf16[1664,256]{1,0:T(8,128)(2,1)S(1)} fusion(bf16[1664,256]{1,0:T(8,128)(2,1)S(1)} %collective-permute-done.1, bf16[1664,256]{1,0:T(8,128)(2,1)} %get-tuple-element.17), kind=kLoop, calls=%fused_computation | loop fusion | flops 1703936 | bytes 2555904 | tf_op jit(solution)/shard_map/convert_element_type | solution.py:560
  38.1 3.0 %collective-permute-start.2 = (bf16[1664,256]{1,0:T(8,128)(2,1)S(1)}, bf16[1664,256]{1,0:T(8,128)(2,1)S(1)}, u32[]{:S(2)}, u32[]{:S(2)}) collective-permute-start(bf16[1664,256]{1,0:T(8,128)(2,1)S(1)} %add_convert_fusion), channel_id=1, source_target_pairs={{0,8},{4,12},{8,0},{12,4},{1,9},{5,13},{9,1},{13,5},{2,10},{6,14},... | collective-permute-start | bytes 2555912 | tf_op jit(solution)/shard_map/ppermute | solution.py:561
  41.1 0.0 collective-permute-done.core_ref
  41.1 0.0 copy-start
  41.1 19.2 %collective-permute-done.2.far_ref = bf16[1664,256]{1,0:T(8,128)(2,1)S(1)} collective-permute-done((bf16[1664,256]{1,0:T(8,128)(2,1)S(1)}, bf16[1664,256]{1,0:T(8,128)(2,1)S(1)}, u32[]{:S(2)}, u32[]{:S(2)}) %collective-permute-start.2) | collective-permute-done | bytes 852000 | tf_op jit(solution)/shard_map/ppermute | solution.py:561
  60.3 0.0 copy-start.1
  60.3 0.0 copy-done
  60.3 0.9 copy-done.1
  61.2 4.3 %pool.1 = (bf16[8,16,256]{2,1,0:T(8,128)(2,1)}, f32[1536,256]{1,0:T(8,128)}, bf16[16,1536]{1,0:T(8,128)(2,1)}, f32[16,256]{1,0:T(8,128)}) custom-call(s32[12,128]{1,0:T(8,128)} %bitcast.12, bf16[1664,256]{1,0:T(8,128)(2,1)} %get-tuple-element.15.own_ref, bf16[1664,256]{1,0:T(8,128)(2,1)} %copy-done, bf16[1664,256]{1,0:T(8,128)(2,1)} %copy-done.1, ...), custom_call_target="tpu_custom_call" | custom-call | tf_op jit(solution)/shard_map/pool/pallas_call | solution.py:562
  65.5 9.8 %all_to_all.15.pooled_ref = bf16[8,16,256]{2,1,0:T(8,128)(2,1)} all-to-all(bf16[8,16,256]{2,1,0:T(8,128)(2,1)} %get-tuple-element.20), channel_id=1, replica_groups=mesh['group'=2,'dp'=4,'mp'=4] {'group','dp'}, dimensions={0} | all-to-all | bytes 131072 | tf_op jit(solution)/shard_map/all_to_all | solution.py:577
  75.3 1.6 %dots.1 = f32[4,32,128]{2,1,0:T(8,128)} custom-call(bf16[8,16,256]{2,1,0:T(8,128)(2,1)} %all_to_all.15.pooled_ref), custom_call_target="tpu_custom_call" | custom-call | tf_op jit(solution)/shard_map/dots/pallas_call | solution.py:578
  76.9 4.9 %all-to-all-start.1 = ((f32[4,32,128]{2,1,0:T(8,128)}), f32[4,32,128]{2,1,0:T(8,128)S(1)}, u32[]{:S(2)}, u32[]{:S(2)}) async-start(f32[4,32,128]{2,1,0:T(8,128)} %dots.1), calls=%async_computation.1 | async-start | bytes 131072 | tf_op jit(solution)/shard_map/all_to_all | solution.py:586
  82.5 5.1 %all-to-all-done.1.dots_ref = f32[4,32,128]{2,1,0:T(8,128)S(1)} async-done(((f32[4,32,128]{2,1,0:T(8,128)}), f32[4,32,128]{2,1,0:T(8,128)S(1)}, u32[]{:S(2)}, u32[]{:S(2)}) %all-to-all-start.1) | async-done | bytes 65568 | tf_op jit(solution)/shard_map/all_to_all | solution.py:586
  87.5 0.0 copy-start.2
  87.5 0.6 copy-done.2
  88.2 3.8 %score.1 = (bf16[1,3,1024]{2,1,0:T(4,128)(2,1)}, f32[1,3]{1,0:T(1,128)}, f32[8,16,256]{2,1,0:T(8,128)}) custom-call(s32[12,128]{1,0:T(8,128)} %bitcast.13, bf16[8,16,256]{2,1,0:T(8,128)(2,1)} %all_to_all.15.pooled_ref, f32[4,32,128]{2,1,0:T(8,128)} %copy-done.2, f32[16,256]{1,0:T(8,128)} %get-tuple-element.21.misc_ref, ...), custom_call_target="tpu_custom_call" | custom-call | tf_op jit(solution)/shard_map/score/pallas_call | solution.py:587
  91.9 8.5 %all_to_all.16 = f32[8,16,256]{2,1,0:T(8,128)S(1)} all-to-all(f32[8,16,256]{2,1,0:T(8,128)} %get-tuple-element.26), channel_id=1, replica_groups=mesh['group'=2,'dp'=4,'mp'=4] {'group','dp'}, dimensions={0} | all-to-all | bytes 262144 | tf_op jit(solution)/shard_map/all_to_all | solution.py:599
  100.4 0.6 pad_maximum_fusion
  (1 shorter events, 0.0 us)
Async XLA Ops:
  34.0 2.7 %collective-permute-start.1 = (bf16[1664,256]{1,0:T(8,128)(2,1)}, bf16[1664,256]{1,0:T(8,128)(2,1)S(1)}, u32[]{:S(2)}, u32[]{:S(2)}) collective-permute-start(bf16[1664,256]{1,0:T(8,128)(2,1)} %get-tuple-element.18), channel_id=1, source_target_pairs={{0,4},{4,0},{8,12},{12,8},{1,5},{5,1},{9,13},{13,9},{2,6},{6,2},{1... | collective-permute-start | bytes 2555912 | tf_op jit(solution)/shard_map/ppermute | solution.py:558
  34.5 6.6 %collective-permute-start = (bf16[1664,256]{1,0:T(8,128)(2,1)}, bf16[1664,256]{1,0:T(8,128)(2,1)S(1)}, u32[]{:S(2)}, u32[]{:S(2)}) collective-permute-start(bf16[1664,256]{1,0:T(8,128)(2,1)} %get-tuple-element.16), channel_id=1, source_target_pairs={{0,4},{4,0},{8,12},{12,8},{1,5},{5,1},{9,13},{13,9},{2,6},{6,2},{1... | collective-permute-start | bytes 2555912 | tf_op jit(solution)/shard_map/ppermute | solution.py:559
  38.1 22.2 %collective-permute-start.2 = (bf16[1664,256]{1,0:T(8,128)(2,1)S(1)}, bf16[1664,256]{1,0:T(8,128)(2,1)S(1)}, u32[]{:S(2)}, u32[]{:S(2)}) collective-permute-start(bf16[1664,256]{1,0:T(8,128)(2,1)S(1)} %add_convert_fusion), channel_id=1, source_target_pairs={{0,8},{4,12},{8,0},{12,4},{1,9},{5,13},{9,1},{13,5},{2,10},{6,14},... | collective-permute-start | bytes 2555912 | tf_op jit(solution)/shard_map/ppermute | solution.py:561
  41.1 19.2 %copy-start = (bf16[1664,256]{1,0:T(8,128)(2,1)}, bf16[1664,256]{1,0:T(8,128)(2,1)S(1)}, u32[]{:S(2)}) copy-start(bf16[1664,256]{1,0:T(8,128)(2,1)S(1)} %collective-permute-done.core_ref) | copy-start | bytes 2555908
  60.3 0.9 copy-start.1
  76.9 10.6 %all-to-all-start.1 = ((f32[4,32,128]{2,1,0:T(8,128)}), f32[4,32,128]{2,1,0:T(8,128)S(1)}, u32[]{:S(2)}, u32[]{:S(2)}) async-start(f32[4,32,128]{2,1,0:T(8,128)} %dots.1), calls=%async_computation.1 | async-start | bytes 131072 | tf_op jit(solution)/shard_map/all_to_all | solution.py:586
  87.5 0.6 copy-start.2

commit v4 on v3

--- a/solution.py
+++ b/solution.py
@@ -116,7 +116,7 @@
 CHUNK = 1 << CHUNK_BITS
 ROWS = 1 << ROW_BITS
 LANES = 128
-PIECES = 4
+PIECES = 1
 NT = (((1,), (1,)), ((), ()))
 VMEM_BYTES = 60 * 1024 * 1024
 
@@ -151,6 +151,7 @@
     member_ref,
     held,
     weight,
+    lower_rows,
     lower,
     gathered,
     values,
@@ -192,7 +193,7 @@
         )
 
     lower_copy = pltpu.make_async_copy(
-        lower_ref.at[:, pl.ds(pl.multiple_of(shard * features, LANES), features)], lower, lower_sem
+        lower_ref.at[:, pl.ds(pl.multiple_of(shard * features, LANES), features)], lower_rows, lower_sem
     )
     for piece in range(PIECES):
         vocab_copy(0, piece).start()
@@ -237,20 +238,23 @@
         found = found.astype(jnp.int32)
         token = lax.shift_right_logical(found, ROW_BITS)
         start = pl.multiple_of(p * LANES, LANES)
-        values[pl.ds(start, LANES), :] = jnp.where(token == 0, -vocab, token)
+        values[pl.ds(start, LANES), :] = jnp.where(token == 0, -vocab, token).astype(jnp.float32)
         real = (token != 0) & ((found & (ROWS - 1)) == iota((LANES, LANES), 1))
         member_ref[pl.ds(start, LANES), :] = jnp.where(real, 1.0, 0.0).astype(jnp.bfloat16)
         gathered[pl.ds(start, LANES), :] = jnp.zeros((LANES, features), jnp.bfloat16)
         return carry
 
     lax.fori_loop(0, tokens // LANES, place, 0)
-    values[pl.ds(tokens, WINDOW), :] = jnp.full((WINDOW, LANES), -vocab, jnp.int32)
+    values[pl.ds(tokens, WINDOW), :] = jnp.full((WINDOW, LANES), -vocab, jnp.float32)
     gathered[pl.ds(tokens, WINDOW), :] = jnp.zeros((WINDOW, features), jnp.bfloat16)
     residual[...] = jnp.zeros_like(residual)
     squares[...] = jnp.zeros_like(squares)
     turned[...] = jnp.zeros_like(turned)
     turned[0:per_shard, chunks : chunks + negatives] = hard_ref[...].astype(jnp.float32)
     lower_copy.wait()
+    padded = jnp.zeros((LANES - ROWS, features), jnp.float32)
+    padded = jnp.concatenate([lower_rows[...].astype(jnp.float32), padded])
+    lower[...] = padded.T.astype(jnp.bfloat16)
     for i in range(2):
         for j in range(2):
             weight_copy(i, j).wait()
@@ -260,12 +264,12 @@
         x = gathered[pl.ds(start, CHUNK), :]
         for q in range(4):
             outs[q][pl.ds(start, CHUNK), :] = mm(x, weight[q]).astype(jnp.bfloat16)
-        reduced = mm(lower[...], x, NT).astype(jnp.bfloat16)
+        squared = mm(x * x, jnp.ones((features, LANES), jnp.bfloat16))
+        both = jnp.where(iota((CHUNK, LANES), 1) < ROWS, mm(x, lower[...]), squared).T
         place_at = pl.multiple_of(tokens + k * ROWS, ROWS)
         for q in range(4):
-            outs[q][pl.ds(place_at, ROWS), :] = reduced
-        ones = jnp.ones((ROWS, features), jnp.bfloat16)
-        squares[pl.ds(k, 1), :] = mm(ones, x * x, NT)[0:1]
+            outs[q][pl.ds(place_at, ROWS), :] = both[0:ROWS].astype(jnp.bfloat16)
+        squares[pl.ds(k, 1), :] = both[ROWS : ROWS + 1]
         member = member_ref[pl.ds(start, CHUNK), :].astype(jnp.float32).T.astype(jnp.bfloat16)
         residual[...] += mm(member[0:ROWS], x)
         return carry
@@ -288,13 +292,14 @@
 
         def window(w, carry):
             start = pl.multiple_of(aligned + w * WINDOW, ROWS)
-            wanted = values[pl.ds(start, WINDOW), :] - (b * IDS_PER_BLOCK + iota((WINDOW, LANES), 1))
+            wanted = values[pl.ds(start, WINDOW), :].T.astype(jnp.int32)
+            wanted -= b * IDS_PER_BLOCK + iota((LANES, WINDOW), 0)
             picked = [
                 jnp.where(wanted == j * LANES, 1.0, 0.0).astype(jnp.bfloat16)
                 for j in range(IDS_PER_BLOCK // LANES)
             ]
-            found = mm(jnp.concatenate(picked, axis=1), held[b], NT)
-            gathered[pl.ds(start, WINDOW), :] += found.astype(jnp.bfloat16)
+            found = mm(held[b], jnp.concatenate(picked, axis=0))
+            gathered[pl.ds(start, WINDOW), :] += found.T.astype(jnp.bfloat16)
             return carry
 
         lax.fori_loop(0, windows, window, 0)
@@ -531,8 +536,9 @@
             pltpu.VMEM((blocks, features, IDS_PER_BLOCK), jnp.bfloat16),
             pltpu.VMEM((4, features, width), jnp.bfloat16),
             pltpu.VMEM((rank, features), jnp.bfloat16),
+            pltpu.VMEM((features, LANES), jnp.bfloat16),
             pltpu.VMEM((tokens + WINDOW, features), jnp.bfloat16),
-            pltpu.VMEM((tokens + WINDOW, LANES), jnp.int32),
+            pltpu.VMEM((tokens + WINDOW, LANES), jnp.float32),
             pltpu.VMEM((LANES, LANES), jnp.float32),
             pltpu.VMEM((texts, length), jnp.float32),
             pltpu.VMEM((8, width), jnp.float32),

time: 102 us -> 101 us (level); the launches traced: 101 us -> 101 us
  no operation moved by 1% of the time
where the time goes in v4:
time: 101 us
  Pallas kernels  42.6 us (42%)
  waiting for transfers between devices  26.5 us (26%)
  blocking collectives  17.3 us (17%)
  starting transfers between devices  8.64 us (9%)
  local copies, waits for them, and re-layouts  2.84 us (3%)
  other arithmetic  2.06 us (2%)
  between operations  1.3 us (1%)
    pallas_call x1, Pallas kernels, split_body(): pl.pallas_call(project_kernel, out_shape=[half] * 4 + [jax.ShapeDtypeStru...  32.9 us
    ppermute x1, waiting for transfers between devices, split_body(): far = lax.ppermute(chip1, 'dp', other_y)  19.2 us
    all_to_all x1, blocking collectives, split_body(): pooled = lax.all_to_all(pooled, sides, 0, 0)  8.8 us
    all_to_all x1, blocking collectives, split_body(): update = lax.all_to_all(update, sides, 0, 0)  8.45 us
    all_to_all x1, waiting for transfers between devices, split_body(): dots = lax.all_to_all(dots, 'mp', 0, 0)  5.09 us
    all_to_all x1, starting transfers between devices, split_body(): dots = lax.all_to_all(dots, 'mp', 0, 0)  5.09 us
    pallas_call x1, Pallas kernels, split_body(): pl.pallas_call(functools.partial(pool_kernel, model_width=float(features...  4.26 us
    pallas_call x1, Pallas kernels, split_body(): pl.pallas_call(functools.partial(score_kernel, shards=shards, negatives=n...  3.77 us
  transfers between devices with their start and end apart: 4, of which 3 were waited for; matrix products, arithmetic and copies ran while one was open for 1% of the time, Pallas kernels for 0%

profile of v4, /device:TPU:0, one launch (start us, length us, event | category | flops | bytes accessed | tf_op | source)
XLA Modules:
  0.0 101.1 jit_solution(10124975218116123835)
XLA Ops:
  0.6 1.3 %copy.12 = s32[1,12,128]{2,1,0:T(8,128)} copy(s32[1,12,128]{2,0,1:T(1,128)} %param.7) | data formatting | bytes 12288
  1.9 32.9 %project.1 = (bf16[1664,256]{1,0:T(8,128)(2,1)}, bf16[1664,256]{1,0:T(8,128)(2,1)}, bf16[1664,256]{1,0:T(8,128)(2,1)}, bf16[1664,256]{1,0:T(8,128)(2,1)}, bf16[1536,128]{1,0:T(8,128)(2,1)}) custom-call(s32[12,128]{1,0:T(8,128)} %bitcast.11, s32[3,7]{1,0:T(4,128)} %hard_ref.1, bf16[1024,16384]{1,0:T(8,128)(2,1)} %vocab_ref.1, bf16[1024,1024]{1,0:T(8,128)(2,1)} %weight_ref.1, ...), custom_call_target="tpu_custom_call" | custom-call | tf_op jit(solution)/shard_map/project/pallas_call | solution.py:530
  34.8 0.5 collective-permute-start.1
  35.4 0.1 collective-permute-start
  35.4 2.1 %collective-permute-done.1 = bf16[1664,256]{1,0:T(8,128)(2,1)S(1)} collective-permute-done((bf16[1664,256]{1,0:T(8,128)(2,1)}, bf16[1664,256]{1,0:T(8,128)(2,1)S(1)}, u32[]{:S(2)}, u32[]{:S(2)}) %collective-permute-start.1) | collective-permute-done | bytes 852000 | tf_op jit(solution)/shard_map/ppermute | solution.py:564
  37.6 1.4 %add_convert_fusion = bf16[1664,256]{1,0:T(8,128)(2,1)S(1)} fusion(bf16[1664,256]{1,0:T(8,128)(2,1)S(1)} %collective-permute-done.1, bf16[1664,256]{1,0:T(8,128)(2,1)} %get-tuple-element.17), kind=kLoop, calls=%fused_computation | loop fusion | flops 1703936 | bytes 2555904 | tf_op jit(solution)/shard_map/convert_element_type | solution.py:566
  39.0 3.0 %collective-permute-start.2 = (bf16[1664,256]{1,0:T(8,128)(2,1)S(1)}, bf16[1664,256]{1,0:T(8,128)(2,1)S(1)}, u32[]{:S(2)}, u32[]{:S(2)}) collective-permute-start(bf16[1664,256]{1,0:T(8,128)(2,1)S(1)} %add_convert_fusion), channel_id=1, source_target_pairs={{0,8},{4,12},{8,0},{12,4},{1,9},{5,13},{9,1},{13,5},{2,10},{6,14},... | collective-permute-start | bytes 2555912 | tf_op jit(solution)/shard_map/ppermute | solution.py:567
  42.0 0.0 collective-permute-done.core_ref
  42.0 0.0 copy-start
  42.0 19.2 %collective-permute-done.2.far_ref = bf16[1664,256]{1,0:T(8,128)(2,1)S(1)} collective-permute-done((bf16[1664,256]{1,0:T(8,128)(2,1)S(1)}, bf16[1664,256]{1,0:T(8,128)(2,1)S(1)}, u32[]{:S(2)}, u32[]{:S(2)}) %collective-permute-start.2) | collective-permute-done | bytes 852000 | tf_op jit(solution)/shard_map/ppermute | solution.py:567
  61.2 0.0 copy-start.1
  61.2 0.0 copy-done
  61.2 0.9 copy-done.1
  62.1 4.3 %pool.1 = (bf16[8,16,256]{2,1,0:T(8,128)(2,1)}, f32[1536,256]{1,0:T(8,128)}, bf16[16,1536]{1,0:T(8,128)(2,1)}, f32[16,256]{1,0:T(8,128)}) custom-call(s32[12,128]{1,0:T(8,128)} %bitcast.12, bf16[1664,256]{1,0:T(8,128)(2,1)} %get-tuple-element.15.own_ref, bf16[1664,256]{1,0:T(8,128)(2,1)} %copy-done, bf16[1664,256]{1,0:T(8,128)(2,1)} %copy-done.1, ...), custom_call_target="tpu_custom_call" | custom-call | tf_op jit(solution)/shard_map/pool/pallas_call | solution.py:568
  66.4 8.8 %all_to_all.15.pooled_ref = bf16[8,16,256]{2,1,0:T(8,128)(2,1)} all-to-all(bf16[8,16,256]{2,1,0:T(8,128)(2,1)} %get-tuple-element.20), channel_id=1, replica_groups=mesh['group'=2,'dp'=4,'mp'=4] {'group','dp'}, dimensions={0} | all-to-all | bytes 131072 | tf_op jit(solution)/shard_map/all_to_all | solution.py:583
  75.2 1.6 %dots.1 = f32[4,32,128]{2,1,0:T(8,128)} custom-call(bf16[8,16,256]{2,1,0:T(8,128)(2,1)} %all_to_all.15.pooled_ref), custom_call_target="tpu_custom_call" | custom-call | tf_op jit(solution)/shard_map/dots/pallas_call | solution.py:584
  76.8 5.1 %all-to-all-start.1 = ((f32[4,32,128]{2,1,0:T(8,128)}), f32[4,32,128]{2,1,0:T(8,128)S(1)}, u32[]{:S(2)}, u32[]{:S(2)}) async-start(f32[4,32,128]{2,1,0:T(8,128)} %dots.1), calls=%async_computation.1 | async-start | bytes 131072 | tf_op jit(solution)/shard_map/all_to_all | solution.py:592
  82.5 5.1 %all-to-all-done.1.dots_ref = f32[4,32,128]{2,1,0:T(8,128)S(1)} async-done(((f32[4,32,128]{2,1,0:T(8,128)}), f32[4,32,128]{2,1,0:T(8,128)S(1)}, u32[]{:S(2)}, u32[]{:S(2)}) %all-to-all-start.1) | async-done | bytes 65568 | tf_op jit(solution)/shard_map/all_to_all | solution.py:592
  87.6 0.0 copy-start.2
  87.6 0.6 copy-done.2
  88.3 3.8 %score.1 = (bf16[1,3,1024]{2,1,0:T(4,128)(2,1)}, f32[1,3]{1,0:T(1,128)}, f32[8,16,256]{2,1,0:T(8,128)}) custom-call(s32[12,128]{1,0:T(8,128)} %bitcast.13, bf16[8,16,256]{2,1,0:T(8,128)(2,1)} %all_to_all.15.pooled_ref, f32[4,32,128]{2,1,0:T(8,128)} %copy-done.2, f32[16,256]{1,0:T(8,128)} %get-tuple-element.21.misc_ref, ...), custom_call_target="tpu_custom_call" | custom-call | tf_op jit(solution)/shard_map/score/pallas_call | solution.py:593
  92.0 8.5 %all_to_all.16 = f32[8,16,256]{2,1,0:T(8,128)S(1)} all-to-all(f32[8,16,256]{2,1,0:T(8,128)} %get-tuple-element.26), channel_id=1, replica_groups=mesh['group'=2,'dp'=4,'mp'=4] {'group','dp'}, dimensions={0} | all-to-all | bytes 262144 | tf_op jit(solution)/shard_map/all_to_all | solution.py:605
  100.5 0.6 pad_maximum_fusion
  (1 shorter events, 0.0 us)
Async XLA Ops:
  34.8 2.7 %collective-permute-start.1 = (bf16[1664,256]{1,0:T(8,128)(2,1)}, bf16[1664,256]{1,0:T(8,128)(2,1)S(1)}, u32[]{:S(2)}, u32[]{:S(2)}) collective-permute-start(bf16[1664,256]{1,0:T(8,128)(2,1)} %get-tuple-element.18), channel_id=1, source_target_pairs={{0,4},{4,0},{8,12},{12,8},{1,5},{5,1},{9,13},{13,9},{2,6},{6,2},{1... | collective-permute-start | bytes 2555912 | tf_op jit(solution)/shard_map/ppermute | solution.py:564
  35.4 6.6 %collective-permute-start = (bf16[1664,256]{1,0:T(8,128)(2,1)}, bf16[1664,256]{1,0:T(8,128)(2,1)S(1)}, u32[]{:S(2)}, u32[]{:S(2)}) collective-permute-start(bf16[1664,256]{1,0:T(8,128)(2,1)} %get-tuple-element.16), channel_id=1, source_target_pairs={{0,4},{4,0},{8,12},{12,8},{1,5},{5,1},{9,13},{13,9},{2,6},{6,2},{1... | collective-permute-start | bytes 2555912 | tf_op jit(solution)/shard_map/ppermute | solution.py:565
  39.0 22.2 %collective-permute-start.2 = (bf16[1664,256]{1,0:T(8,128)(2,1)S(1)}, bf16[1664,256]{1,0:T(8,128)(2,1)S(1)}, u32[]{:S(2)}, u32[]{:S(2)}) collective-permute-start(bf16[1664,256]{1,0:T(8,128)(2,1)S(1)} %add_convert_fusion), channel_id=1, source_target_pairs={{0,8},{4,12},{8,0},{12,4},{1,9},{5,13},{9,1},{13,5},{2,10},{6,14},... | collective-permute-start | bytes 2555912 | tf_op jit(solution)/shard_map/ppermute | solution.py:567
  42.0 19.2 %copy-start = (bf16[1664,256]{1,0:T(8,128)(2,1)}, bf16[1664,256]{1,0:T(8,128)(2,1)S(1)}, u32[]{:S(2)}) copy-start(bf16[1664,256]{1,0:T(8,128)(2,1)S(1)} %collective-permute-done.core_ref) | copy-start | bytes 2555908
  61.2 0.9 copy-start.1
  76.8 10.8 %all-to-all-start.1 = ((f32[4,32,128]{2,1,0:T(8,128)}), f32[4,32,128]{2,1,0:T(8,128)S(1)}, u32[]{:S(2)}, u32[]{:S(2)}) async-start(f32[4,32,128]{2,1,0:T(8,128)} %dots.1), calls=%async_computation.1 | async-start | bytes 131072 | tf_op jit(solution)/shard_map/all_to_all | solution.py:592
  87.6 0.6 copy-start.2

commit v5 on v4

--- a/solution.py
+++ b/solution.py
@@ -116,7 +116,8 @@
 CHUNK = 1 << CHUNK_BITS
 ROWS = 1 << ROW_BITS
 LANES = 128
-PIECES = 1
+STAGES = 4
+PIECES = 4
 NT = (((1,), (1,)), ((), ()))
 VMEM_BYTES = 60 * 1024 * 1024
 
@@ -153,6 +154,7 @@
     weight,
     lower_rows,
     lower,
+    picks,
     gathered,
     values,
     turned,
@@ -177,12 +179,12 @@
     shard = lax.axis_index("dp")
     core, side_y = lax.rem(shard, 2), lax.div(shard, 2)
 
-    def vocab_copy(b, piece):
-        rows = pl.ds(piece * (features // PIECES), features // PIECES)
-        columns = pl.ds(pl.multiple_of(b * IDS_PER_BLOCK, LANES), IDS_PER_BLOCK)
-        return pltpu.make_async_copy(
-            vocab_ref.at[rows, columns], held.at[b, rows], held_sems.at[b, piece]
-        )
+    stage_rows = features // STAGES
+    piece_rows = stage_rows // PIECES
+
+    def vocab_copy(stage, piece):
+        rows = pl.ds(pl.multiple_of((stage * PIECES + piece) * piece_rows, ROWS), piece_rows)
+        return pltpu.make_async_copy(vocab_ref.at[rows], held.at[rows], held_sems.at[stage, piece])
 
     def weight_copy(i, j):
         quarter = (core ^ i) * 2 + (side_y ^ j)
@@ -195,15 +197,14 @@
     lower_copy = pltpu.make_async_copy(
         lower_ref.at[:, pl.ds(pl.multiple_of(shard * features, LANES), features)], lower_rows, lower_sem
     )
-    for piece in range(PIECES):
-        vocab_copy(0, piece).start()
-    lower_copy.start()
-    for i in range(2):
-        for j in range(2):
-            weight_copy(i, j).start()
-    for b in range(1, blocks):
+    for stage in range(STAGES):
         for piece in range(PIECES):
-            vocab_copy(b, piece).start()
+            vocab_copy(stage, piece).start()
+        if stage == 0:
+            lower_copy.start()
+            for i in range(2):
+                for j in range(2):
+                    weight_copy(i, j).start()
 
     ids = ids_ref[...]
     valid = ids != 0
@@ -282,35 +283,49 @@
             outs[q][pl.ds(place_at, ROWS), :] = jnp.zeros((ROWS, width), jnp.bfloat16)
         return carry
 
-    def take(b, done):
-        for piece in range(PIECES):
-            vocab_copy(b, piece).wait()
+    def windows_of(b):
         first, last = bounds[b, 0], bounds[b + 1, 0]
         aligned = lax.shift_left(lax.shift_right_logical(first, ROW_BITS), ROW_BITS)
         windows = lax.shift_right_logical(last - aligned + WINDOW - 1, WINDOW_BITS)
-        windows = jnp.where(last > first, windows, 0)
-
-        def window(w, carry):
-            start = pl.multiple_of(aligned + w * WINDOW, ROWS)
-            wanted = values[pl.ds(start, WINDOW), :].T.astype(jnp.int32)
-            wanted -= b * IDS_PER_BLOCK + iota((LANES, WINDOW), 0)
-            picked = [
-                jnp.where(wanted == j * LANES, 1.0, 0.0).astype(jnp.bfloat16)
-                for j in range(IDS_PER_BLOCK // LANES)
-            ]
-            found = mm(held[b], jnp.concatenate(picked, axis=0))
-            gathered[pl.ds(start, WINDOW), :] += found.T.astype(jnp.bfloat16)
-            return carry
-
-        lax.fori_loop(0, windows, window, 0)
-        full = lax.shift_right_logical(last, CHUNK_BITS)
-        lax.fori_loop(done, full, project, 0)
-        return full
+        return aligned, jnp.where(last > first, windows, 0)
+
+    def over_windows(act):
+        def block(b, slot):
+            aligned, windows = windows_of(b)
+
+            def window(w, slot):
+                act(b, pl.multiple_of(aligned + w * WINDOW, ROWS), slot)
+                return slot + 1
+
+            return lax.fori_loop(0, windows, window, slot)
+
+        lax.fori_loop(0, blocks, block, 0)
+
+    def pick(b, start, slot):
+        wanted = values[pl.ds(start, WINDOW), :].T.astype(jnp.int32)
+        wanted -= b * IDS_PER_BLOCK + iota((LANES, WINDOW), 0)
+        for j in range(IDS_PER_BLOCK // LANES):
+            picks[slot, j * LANES : (j + 1) * LANES, :] = jnp.where(
+                wanted == j * LANES, 1.0, 0.0
+            ).astype(jnp.bfloat16)
 
     bounds_copy.wait()
-    done = lax.fori_loop(0, blocks, take, 0)
+    over_windows(pick)
+
+    for stage in range(STAGES):
+        at = stage * stage_rows
+        for piece in range(PIECES):
+            vocab_copy(stage, piece).wait()
+
+        def take(b, start, slot):
+            ids_at = pl.ds(pl.multiple_of(b * IDS_PER_BLOCK, LANES), IDS_PER_BLOCK)
+            found = mm(held[at : at + stage_rows, ids_at], picks[slot])
+            gathered[pl.ds(start, WINDOW), at : at + stage_rows] += found.T.astype(jnp.bfloat16)
+
+        over_windows(take)
+
     used = lax.shift_right_logical(bounds[blocks, 0] + CHUNK - 1, CHUNK_BITS)
-    lax.fori_loop(done, used, project, 0)
+    lax.fori_loop(0, used, project, 0)
     lax.fori_loop(used, chunks, zero, 0)
 
     hard = turned[...].T[0:ROWS]
@@ -525,6 +540,7 @@
     part_width = layer_weight_matrix.shape[1]
     width = part_width // shards
     rows = tokens + (chunks + 2) * ROWS
+    slots = (tokens + blocks * (WINDOW + ROWS - 2)) // WINDOW + 1
     params = pltpu.CompilerParams(vmem_limit_bytes=VMEM_BYTES)
     half = jax.ShapeDtypeStruct((rows, width), jnp.bfloat16)
     own0, own1, away0, away1, member = pl.pallas_call(
@@ -533,10 +549,11 @@
         in_specs=[vmem_spec()] * 2 + [any_spec()] * 3,
         out_specs=[vmem_spec()] * 5,
         scratch_shapes=[
-            pltpu.VMEM((blocks, features, IDS_PER_BLOCK), jnp.bfloat16),
+            pltpu.VMEM((features, vocab), jnp.bfloat16),
             pltpu.VMEM((4, features, width), jnp.bfloat16),
             pltpu.VMEM((rank, features), jnp.bfloat16),
             pltpu.VMEM((features, LANES), jnp.bfloat16),
+            pltpu.VMEM((slots, IDS_PER_BLOCK, WINDOW), jnp.bfloat16),
             pltpu.VMEM((tokens + WINDOW, features), jnp.bfloat16),
             pltpu.VMEM((tokens + WINDOW, LANES), jnp.float32),
             pltpu.VMEM((LANES, LANES), jnp.float32),
@@ -545,7 +562,7 @@
             pltpu.VMEM((ROWS, features), jnp.float32),
             pltpu.VMEM((block_rows, length), jnp.int32),
             pltpu.SMEM((block_rows, length), jnp.int32),
-            pltpu.SemaphoreType.DMA((blocks, PIECES)),
+            pltpu.SemaphoreType.DMA((STAGES, PIECES)),
             pltpu.SemaphoreType.DMA((4,)),
             pltpu.SemaphoreType.DMA,
             pltpu.SemaphoreType.DMA,

time: 101 us -> 113 us (1.12); the launches traced: 101 us -> 112 us
  Pallas kernels: 42.6 us -> 53.2 us
    pallas_call x1, Pallas kernels: 32.9 us -> 43.5 us  [split_body(): pl.pallas_call(project_kernel, out_shape=[half] * 4 + [jax.ShapeDtypeStru...]
where the time goes in v5:
time: 113 us; the launch traced here: 112 us
  Pallas kernels  53.2 us (47%)
  waiting for transfers between devices  26.5 us (23%)
  blocking collectives  17.3 us (15%)
  starting transfers between devices  8.55 us (8%)
  local copies, waits for them, and re-layouts  2.84 us (3%)
  other arithmetic  2.06 us (2%)
  between operations  1.3 us (1%)
    pallas_call x1, Pallas kernels, split_body(): pl.pallas_call(project_kernel, out_shape=[half] * 4 + [jax.ShapeDtypeStru...  43.5 us
    ppermute x1, waiting for transfers between devices, split_body(): far = lax.ppermute(chip1, 'dp', other_y)  19.2 us
    all_to_all x1, blocking collectives, split_body(): pooled = lax.all_to_all(pooled, sides, 0, 0)  8.89 us
    all_to_all x1, blocking collectives, split_body(): update = lax.all_to_all(update, sides, 0, 0)  8.45 us
    all_to_all x1, waiting for transfers between devices, split_body(): dots = lax.all_to_all(dots, 'mp', 0, 0)  5.09 us
    all_to_all x1, starting transfers between devices, split_body(): dots = lax.all_to_all(dots, 'mp', 0, 0)  5 us
    pallas_call x1, Pallas kernels, split_body(): pl.pallas_call(functools.partial(pool_kernel, model_width=float(features...  4.26 us
    pallas_call x1, Pallas kernels, split_body(): pl.pallas_call(functools.partial(score_kernel, shards=shards, negatives=n...  3.77 us
  transfers between devices with their start and end apart: 4, of which 3 were waited for; matrix products, arithmetic and copies ran while one was open for 1% of the time, Pallas kernels for 0%

profile of v5, /device:TPU:0, one launch (start us, length us, event | category | flops | bytes accessed | tf_op | source)
XLA Modules:
  0.0 111.8 jit_solution(489985767500310209)
XLA Ops:
  0.6 1.3 %copy.12 = s32[1,12,128]{2,1,0:T(8,128)} copy(s32[1,12,128]{2,0,1:T(1,128)} %param.7) | data formatting | bytes 12288
  1.9 43.5 %project.1 = (bf16[1664,256]{1,0:T(8,128)(2,1)}, bf16[1664,256]{1,0:T(8,128)(2,1)}, bf16[1664,256]{1,0:T(8,128)(2,1)}, bf16[1664,256]{1,0:T(8,128)(2,1)}, bf16[1536,128]{1,0:T(8,128)(2,1)}) custom-call(s32[12,128]{1,0:T(8,128)} %bitcast.11, s32[3,7]{1,0:T(4,128)} %hard_ref.1, bf16[1024,16384]{1,0:T(8,128)(2,1)} %vocab_ref.1, bf16[1024,1024]{1,0:T(8,128)(2,1)} %weight_ref.1, ...), custom_call_target="tpu_custom_call" | custom-call | tf_op jit(solution)/shard_map/project/pallas_call | solution.py:546
  45.5 0.5 collective-permute-start.1
  46.0 0.1 collective-permute-start
  46.1 2.1 %collective-permute-done.1 = bf16[1664,256]{1,0:T(8,128)(2,1)S(1)} collective-permute-done((bf16[1664,256]{1,0:T(8,128)(2,1)}, bf16[1664,256]{1,0:T(8,128)(2,1)S(1)}, u32[]{:S(2)}, u32[]{:S(2)}) %collective-permute-start.1) | collective-permute-done | bytes 852000 | tf_op jit(solution)/shard_map/ppermute | solution.py:581
  48.2 1.4 %add_convert_fusion = bf16[1664,256]{1,0:T(8,128)(2,1)S(1)} fusion(bf16[1664,256]{1,0:T(8,128)(2,1)S(1)} %collective-permute-done.1, bf16[1664,256]{1,0:T(8,128)(2,1)} %get-tuple-element.17), kind=kLoop, calls=%fused_computation | loop fusion | flops 1703936 | bytes 2555904 | tf_op jit(solution)/shard_map/convert_element_type | solution.py:583
  49.6 2.9 %collective-permute-start.2 = (bf16[1664,256]{1,0:T(8,128)(2,1)S(1)}, bf16[1664,256]{1,0:T(8,128)(2,1)S(1)}, u32[]{:S(2)}, u32[]{:S(2)}) collective-permute-start(bf16[1664,256]{1,0:T(8,128)(2,1)S(1)} %add_convert_fusion), channel_id=1, source_target_pairs={{0,8},{4,12},{8,0},{12,4},{1,9},{5,13},{9,1},{13,5},{2,10},{6,14},... | collective-permute-start | bytes 2555912 | tf_op jit(solution)/shard_map/ppermute | solution.py:584
  52.6 0.0 collective-permute-done.core_ref
  52.6 0.0 copy-start
  52.6 19.2 %collective-permute-done.2.far_ref = bf16[1664,256]{1,0:T(8,128)(2,1)S(1)} collective-permute-done((bf16[1664,256]{1,0:T(8,128)(2,1)S(1)}, bf16[1664,256]{1,0:T(8,128)(2,1)S(1)}, u32[]{:S(2)}, u32[]{:S(2)}) %collective-permute-start.2) | collective-permute-done | bytes 852000 | tf_op jit(solution)/shard_map/ppermute | solution.py:584
  71.8 0.0 copy-start.1
  71.8 0.0 copy-done
  71.8 0.9 copy-done.1
  72.7 4.3 %pool.1 = (bf16[8,16,256]{2,1,0:T(8,128)(2,1)}, f32[1536,256]{1,0:T(8,128)}, bf16[16,1536]{1,0:T(8,128)(2,1)}, f32[16,256]{1,0:T(8,128)}) custom-call(s32[12,128]{1,0:T(8,128)} %bitcast.12, bf16[1664,256]{1,0:T(8,128)(2,1)} %get-tuple-element.15.own_ref, bf16[1664,256]{1,0:T(8,128)(2,1)} %copy-done, bf16[1664,256]{1,0:T(8,128)(2,1)} %copy-done.1, ...), custom_call_target="tpu_custom_call" | custom-call | tf_op jit(solution)/shard_map/pool/pallas_call | solution.py:585
  77.0 8.9 %all_to_all.15.pooled_ref = bf16[8,16,256]{2,1,0:T(8,128)(2,1)} all-to-all(bf16[8,16,256]{2,1,0:T(8,128)(2,1)} %get-tuple-element.20), channel_id=1, replica_groups=mesh['group'=2,'dp'=4,'mp'=4] {'group','dp'}, dimensions={0} | all-to-all | bytes 131072 | tf_op jit(solution)/shard_map/all_to_all | solution.py:600
  85.9 1.6 %dots.1 = f32[4,32,128]{2,1,0:T(8,128)} custom-call(bf16[8,16,256]{2,1,0:T(8,128)(2,1)} %all_to_all.15.pooled_ref), custom_call_target="tpu_custom_call" | custom-call | tf_op jit(solution)/shard_map/dots/pallas_call | solution.py:601
  87.5 5.0 %all-to-all-start.1 = ((f32[4,32,128]{2,1,0:T(8,128)}), f32[4,32,128]{2,1,0:T(8,128)S(1)}, u32[]{:S(2)}, u32[]{:S(2)}) async-start(f32[4,32,128]{2,1,0:T(8,128)} %dots.1), calls=%async_computation.1 | async-start | bytes 131072 | tf_op jit(solution)/shard_map/all_to_all | solution.py:609
  93.2 5.1 %all-to-all-done.1.dots_ref = f32[4,32,128]{2,1,0:T(8,128)S(1)} async-done(((f32[4,32,128]{2,1,0:T(8,128)}), f32[4,32,128]{2,1,0:T(8,128)S(1)}, u32[]{:S(2)}, u32[]{:S(2)}) %all-to-all-start.1) | async-done | bytes 65568 | tf_op jit(solution)/shard_map/all_to_all | solution.py:609
  98.2 0.0 copy-start.2
  98.2 0.6 copy-done.2
  98.9 3.8 %score.1 = (bf16[1,3,1024]{2,1,0:T(4,128)(2,1)}, f32[1,3]{1,0:T(1,128)}, f32[8,16,256]{2,1,0:T(8,128)}) custom-call(s32[12,128]{1,0:T(8,128)} %bitcast.13, bf16[8,16,256]{2,1,0:T(8,128)(2,1)} %all_to_all.15.pooled_ref, f32[4,32,128]{2,1,0:T(8,128)} %copy-done.2, f32[16,256]{1,0:T(8,128)} %get-tuple-element.21.misc_ref, ...), custom_call_target="tpu_custom_call" | custom-call | tf_op jit(solution)/shard_map/score/pallas_call | solution.py:610
  102.7 8.5 %all_to_all.16 = f32[8,16,256]{2,1,0:T(8,128)S(1)} all-to-all(f32[8,16,256]{2,1,0:T(8,128)} %get-tuple-element.26), channel_id=1, replica_groups=mesh['group'=2,'dp'=4,'mp'=4] {'group','dp'}, dimensions={0} | all-to-all | bytes 262144 | tf_op jit(solution)/shard_map/all_to_all | solution.py:622
  111.1 0.6 pad_maximum_fusion
  (1 shorter events, 0.0 us)
Async XLA Ops:
  45.5 2.7 %collective-permute-start.1 = (bf16[1664,256]{1,0:T(8,128)(2,1)}, bf16[1664,256]{1,0:T(8,128)(2,1)S(1)}, u32[]{:S(2)}, u32[]{:S(2)}) collective-permute-start(bf16[1664,256]{1,0:T(8,128)(2,1)} %get-tuple-element.18), channel_id=1, source_target_pairs={{0,4},{4,0},{8,12},{12,8},{1,5},{5,1},{9,13},{13,9},{2,6},{6,2},{1... | collective-permute-start | bytes 2555912 | tf_op jit(solution)/shard_map/ppermute | solution.py:581
  46.0 6.6 %collective-permute-start = (bf16[1664,256]{1,0:T(8,128)(2,1)}, bf16[1664,256]{1,0:T(8,128)(2,1)S(1)}, u32[]{:S(2)}, u32[]{:S(2)}) collective-permute-start(bf16[1664,256]{1,0:T(8,128)(2,1)} %get-tuple-element.16), channel_id=1, source_target_pairs={{0,4},{4,0},{8,12},{12,8},{1,5},{5,1},{9,13},{13,9},{2,6},{6,2},{1... | collective-permute-start | bytes 2555912 | tf_op jit(solution)/shard_map/ppermute | solution.py:582
  49.6 22.2 %collective-permute-start.2 = (bf16[1664,256]{1,0:T(8,128)(2,1)S(1)}, bf16[1664,256]{1,0:T(8,128)(2,1)S(1)}, u32[]{:S(2)}, u32[]{:S(2)}) collective-permute-start(bf16[1664,256]{1,0:T(8,128)(2,1)S(1)} %add_convert_fusion), channel_id=1, source_target_pairs={{0,8},{4,12},{8,0},{12,4},{1,9},{5,13},{9,1},{13,5},{2,10},{6,14},... | collective-permute-start | bytes 2555912 | tf_op jit(solution)/shard_map/ppermute | solution.py:584
  52.6 19.2 %copy-start = (bf16[1664,256]{1,0:T(8,128)(2,1)}, bf16[1664,256]{1,0:T(8,128)(2,1)S(1)}, u32[]{:S(2)}) copy-start(bf16[1664,256]{1,0:T(8,128)(2,1)S(1)} %collective-permute-done.core_ref) | copy-start | bytes 2555908
  71.8 0.9 copy-start.1
  87.5 10.7 %all-to-all-start.1 = ((f32[4,32,128]{2,1,0:T(8,128)}), f32[4,32,128]{2,1,0:T(8,128)S(1)}, u32[]{:S(2)}, u32[]{:S(2)}) async-start(f32[4,32,128]{2,1,0:T(8,128)} %dots.1), calls=%async_computation.1 | async-start | bytes 131072 | tf_op jit(solution)/shard_map/all_to_all | solution.py:609
  98.2 0.6 copy-start.2

commit v6 on v3

--- a/solution.py
+++ b/solution.py
@@ -110,13 +110,12 @@
     return (embeddings, losses[None], adapter_up_gradient)
 
 
-BLOCK_BITS, WINDOW_BITS, CHUNK_BITS, ROW_BITS = 10, 7, 8, 4
+BLOCK_BITS, WINDOW_BITS, CHUNK_BITS, ROW_BITS = 10, 6, 8, 4
 IDS_PER_BLOCK = 1 << BLOCK_BITS
 WINDOW = 1 << WINDOW_BITS
 CHUNK = 1 << CHUNK_BITS
 ROWS = 1 << ROW_BITS
 LANES = 128
-PIECES = 4
 NT = (((1,), (1,)), ((), ()))
 VMEM_BYTES = 60 * 1024 * 1024
 
@@ -138,84 +137,20 @@
     return (dp_index % cores) * 2 + dp_index // cores
 
 
-def project_kernel(
-    ids_ref,
-    hard_ref,
-    vocab_ref,
-    weight_ref,
-    lower_ref,
-    out00,
-    out01,
-    out10,
-    out11,
-    member_ref,
-    held,
-    weight,
-    lower,
-    gathered,
-    values,
-    turned,
-    ranks,
-    squares,
-    residual,
-    counted,
-    bounds,
-    held_sems,
-    weight_sems,
-    lower_sem,
-    bounds_sem,
-):
+def route_kernel(ids_ref, values_ref, member_ref, bounds_ref, ranks, vocab):
     texts, length = ids_ref.shape
     tokens = texts * length
-    features, vocab = vocab_ref.shape
     blocks = vocab // IDS_PER_BLOCK
-    chunks = tokens // CHUNK
-    per_shard, negatives = hard_ref.shape
-    width = weight.shape[2]
-    outs = (out00, out01, out10, out11)
-    shard = lax.axis_index("dp")
-    core, side_y = lax.rem(shard, 2), lax.div(shard, 2)
-
-    def vocab_copy(b, piece):
-        rows = pl.ds(piece * (features // PIECES), features // PIECES)
-        columns = pl.ds(pl.multiple_of(b * IDS_PER_BLOCK, LANES), IDS_PER_BLOCK)
-        return pltpu.make_async_copy(
-            vocab_ref.at[rows, columns], held.at[b, rows], held_sems.at[b, piece]
-        )
-
-    def weight_copy(i, j):
-        quarter = (core ^ i) * 2 + (side_y ^ j)
-        return pltpu.make_async_copy(
-            weight_ref.at[:, pl.ds(pl.multiple_of(quarter * width, LANES), width)],
-            weight.at[2 * i + j],
-            weight_sems.at[2 * i + j],
-        )
-
-    lower_copy = pltpu.make_async_copy(
-        lower_ref.at[:, pl.ds(pl.multiple_of(shard * features, LANES), features)], lower, lower_sem
-    )
-    for piece in range(PIECES):
-        vocab_copy(0, piece).start()
-    lower_copy.start()
-    for i in range(2):
-        for j in range(2):
-            weight_copy(i, j).start()
-    for b in range(1, blocks):
-        for piece in range(PIECES):
-            vocab_copy(b, piece).start()
-
     ids = ids_ref[...]
     valid = ids != 0
     block_of = jnp.where(valid, lax.shift_right_logical(ids, BLOCK_BITS), blocks)
-    block_rows = counted.shape[0]
+    block_rows = bounds_ref.shape[0]
     block_id = iota((block_rows, length), 0)
     below = jnp.zeros((block_rows, length), jnp.float32)
     for text in range(texts):
         below += jnp.where(block_of[text : text + 1] < block_id, 1.0, 0.0)
     before = jnp.broadcast_to(jnp.sum(below, axis=1, keepdims=True), (block_rows, length))
-    counted[...] = before.astype(jnp.int32)
-    bounds_copy = pltpu.make_async_copy(counted, bounds, bounds_sem)
-    bounds_copy.start()
+    bounds_ref[...] = before.astype(jnp.int32)
     earlier = jnp.where(iota((length, length), 0) < iota((length, length), 1), 1.0, 0.0).astype(
         jnp.bfloat16
     )
@@ -237,58 +172,45 @@
         found = found.astype(jnp.int32)
         token = lax.shift_right_logical(found, ROW_BITS)
         start = pl.multiple_of(p * LANES, LANES)
-        values[pl.ds(start, LANES), :] = jnp.where(token == 0, -vocab, token)
+        values_ref[pl.ds(start, LANES), :] = jnp.where(token == 0, -vocab, token)
         real = (token != 0) & ((found & (ROWS - 1)) == iota((LANES, LANES), 1))
         member_ref[pl.ds(start, LANES), :] = jnp.where(real, 1.0, 0.0).astype(jnp.bfloat16)
-        gathered[pl.ds(start, LANES), :] = jnp.zeros((LANES, features), jnp.bfloat16)
         return carry
 
     lax.fori_loop(0, tokens // LANES, place, 0)
-    values[pl.ds(tokens, WINDOW), :] = jnp.full((WINDOW, LANES), -vocab, jnp.int32)
-    gathered[pl.ds(tokens, WINDOW), :] = jnp.zeros((WINDOW, features), jnp.bfloat16)
-    residual[...] = jnp.zeros_like(residual)
-    squares[...] = jnp.zeros_like(squares)
-    turned[...] = jnp.zeros_like(turned)
-    turned[0:per_shard, chunks : chunks + negatives] = hard_ref[...].astype(jnp.float32)
-    lower_copy.wait()
-    for i in range(2):
-        for j in range(2):
-            weight_copy(i, j).wait()
-
-    def project(k, carry):
-        start = pl.multiple_of(k * CHUNK, CHUNK)
-        x = gathered[pl.ds(start, CHUNK), :]
-        for q in range(4):
-            outs[q][pl.ds(start, CHUNK), :] = mm(x, weight[q]).astype(jnp.bfloat16)
-        reduced = mm(lower[...], x, NT).astype(jnp.bfloat16)
-        place_at = pl.multiple_of(tokens + k * ROWS, ROWS)
-        for q in range(4):
-            outs[q][pl.ds(place_at, ROWS), :] = reduced
-        ones = jnp.ones((ROWS, features), jnp.bfloat16)
-        squares[pl.ds(k, 1), :] = mm(ones, x * x, NT)[0:1]
-        member = member_ref[pl.ds(start, CHUNK), :].astype(jnp.float32).T.astype(jnp.bfloat16)
-        residual[...] += mm(member[0:ROWS], x)
+    values_ref[pl.ds(tokens, WINDOW), :] = jnp.full((WINDOW, LANES), -vocab, jnp.int32)
+
+
+def gather_kernel(bounds, values_ref, vocab_ref, gathered, held, held_sems):
+    features, vocab = vocab_ref.shape
+    blocks = vocab // IDS_PER_BLOCK
+    rows = gathered.shape[0]
+
+    def vocab_copy(b):
+        columns = pl.ds(pl.multiple_of(b * IDS_PER_BLOCK, LANES), IDS_PER_BLOCK)
+        return pltpu.make_async_copy(vocab_ref.at[:, columns], held.at[b], held_sems.at[b])
+
+    for b in range(blocks):
+        vocab_copy(b).start()
+
+    def clear(p, carry):
+        at = pl.multiple_of(p * WINDOW, WINDOW)
+        gathered[pl.ds(at, WINDOW), :] = jnp.zeros((WINDOW, features), jnp.bfloat16)
         return carry
 
-    def zero(k, carry):
-        start = pl.multiple_of(k * CHUNK, CHUNK)
-        place_at = pl.multiple_of(tokens + k * ROWS, ROWS)
-        for q in range(4):
-            outs[q][pl.ds(start, CHUNK), :] = jnp.zeros((CHUNK, width), jnp.bfloat16)
-            outs[q][pl.ds(place_at, ROWS), :] = jnp.zeros((ROWS, width), jnp.bfloat16)
-        return carry
-
-    def take(b, done):
-        for piece in range(PIECES):
-            vocab_copy(b, piece).wait()
+    lax.fori_loop(0, rows // WINDOW, clear, 0)
+
+    def take(b, carry):
         first, last = bounds[b, 0], bounds[b + 1, 0]
         aligned = lax.shift_left(lax.shift_right_logical(first, ROW_BITS), ROW_BITS)
         windows = lax.shift_right_logical(last - aligned + WINDOW - 1, WINDOW_BITS)
         windows = jnp.where(last > first, windows, 0)
+        vocab_copy(b).wait()
 
         def window(w, carry):
             start = pl.multiple_of(aligned + w * WINDOW, ROWS)
-            wanted = values[pl.ds(start, WINDOW), :] - (b * IDS_PER_BLOCK + iota((WINDOW, LANES), 1))
+            wanted = values_ref[pl.ds(start, WINDOW), :]
+            wanted -= b * IDS_PER_BLOCK + iota((WINDOW, LANES), 1)
             picked = [
                 jnp.where(wanted == j * LANES, 1.0, 0.0).astype(jnp.bfloat16)
                 for j in range(IDS_PER_BLOCK // LANES)
@@ -297,39 +219,149 @@
             gathered[pl.ds(start, WINDOW), :] += found.astype(jnp.bfloat16)
             return carry
 
-        lax.fori_loop(0, windows, window, 0)
-        full = lax.shift_right_logical(last, CHUNK_BITS)
-        lax.fori_loop(done, full, project, 0)
-        return full
-
-    bounds_copy.wait()
-    done = lax.fori_loop(0, blocks, take, 0)
+        return lax.fori_loop(0, windows, window, carry)
+
+    lax.fori_loop(0, blocks, take, 0)
+
+
+def split_quarter(i, j, cores=2):
+    shard = lax.axis_index("dp")
+    core, side_y = lax.rem(shard, cores), lax.div(shard, cores)
+    return (core ^ i) * 2 + (side_y ^ j)
+
+
+def weight_copies(weight_ref, weight, sems, i):
+    width = weight.shape[2]
+    return [
+        pltpu.make_async_copy(
+            weight_ref.at[:, pl.ds(pl.multiple_of(split_quarter(i, j) * width, LANES), width)],
+            weight.at[j],
+            sems.at[j],
+        )
+        for j in range(2)
+    ]
+
+
+def away_kernel(
+    bounds,
+    gathered,
+    member_ref,
+    hard_ref,
+    weight_ref,
+    lower_ref,
+    out1,
+    out0,
+    extra_ref,
+    weight,
+    lower,
+    turned,
+    squares,
+    residual,
+    weight_sems,
+    lower_sem,
+    blocks,
+):
+    features = gathered.shape[1]
+    tokens, width = member_ref.shape[0], out0.shape[1]
+    chunks = tokens // CHUNK
+    per_shard, negatives = hard_ref.shape
+    shard = lax.axis_index("dp")
+    copies = weight_copies(weight_ref, weight, weight_sems, 1)
+    lower_copy = pltpu.make_async_copy(
+        lower_ref.at[:, pl.ds(pl.multiple_of(shard * features, LANES), features)], lower, lower_sem
+    )
+    for copy in copies + [lower_copy]:
+        copy.start()
+    residual[...] = jnp.zeros_like(residual)
+    squares[...] = jnp.zeros_like(squares)
+    turned[...] = jnp.zeros_like(turned)
+    turned[0:per_shard, chunks : chunks + negatives] = hard_ref[...].astype(jnp.float32)
+    for copy in copies + [lower_copy]:
+        copy.wait()
+
+    def project(k, carry):
+        start = pl.multiple_of(k * CHUNK, CHUNK)
+        x = gathered[pl.ds(start, CHUNK), :]
+        out1[pl.ds(start, CHUNK), :] = mm(x, weight[1]).astype(jnp.bfloat16)
+        out0[pl.ds(start, CHUNK), :] = mm(x, weight[0]).astype(jnp.bfloat16)
+        reduced = mm(lower[...], x, NT).astype(jnp.bfloat16)
+        extra_ref[pl.ds(pl.multiple_of(k * ROWS, ROWS), ROWS), :] = reduced
+        out1[pl.ds(pl.multiple_of(tokens + k * ROWS, ROWS), ROWS), :] = reduced
+        ones = jnp.ones((ROWS, features), jnp.bfloat16)
+        squares[pl.ds(k, 1), :] = mm(ones, x * x, NT)[0:1]
+        member = member_ref[pl.ds(start, CHUNK), :].astype(jnp.float32).T.astype(jnp.bfloat16)
+        residual[...] += mm(member[0:ROWS], x)
+        return carry
+
+    def zero(k, carry):
+        start = pl.multiple_of(k * CHUNK, CHUNK)
+        out1[pl.ds(start, CHUNK), :] = jnp.zeros((CHUNK, width), jnp.bfloat16)
+        out0[pl.ds(start, CHUNK), :] = jnp.zeros((CHUNK, width), jnp.bfloat16)
+        none = jnp.zeros((ROWS, width), jnp.bfloat16)
+        extra_ref[pl.ds(pl.multiple_of(k * ROWS, ROWS), ROWS), :] = none
+        out1[pl.ds(pl.multiple_of(tokens + k * ROWS, ROWS), ROWS), :] = none
+        return carry
+
     used = lax.shift_right_logical(bounds[blocks, 0] + CHUNK - 1, CHUNK_BITS)
-    lax.fori_loop(done, used, project, 0)
+    lax.fori_loop(0, used, project, 0)
     lax.fori_loop(used, chunks, zero, 0)
-
     hard = turned[...].T[0:ROWS]
     lane = iota((ROWS, width), 1)
     misc = jnp.concatenate([squares[...], jnp.zeros((ROWS - squares.shape[0], width), jnp.float32)])
     for i in range(per_shard):
         misc += jnp.where(lane == shard * per_shard + i, hard[:, i : i + 1], 0.0)
-    misc = misc.astype(jnp.bfloat16)
+    extra_ref[pl.ds(chunks * ROWS, ROWS), :] = misc.astype(jnp.bfloat16)
+    out1[pl.ds(tokens + chunks * ROWS, ROWS), :] = misc.astype(jnp.bfloat16)
+
     mine = lax.axis_index("mp") == shard
-    for i in range(2):
-        for j in range(2):
-            quarter = (core ^ i) * 2 + (side_y ^ j)
-            part = residual[:, pl.ds(pl.multiple_of(quarter * width, LANES), width)]
-            out = outs[2 * i + j]
-            out[pl.ds(tokens + chunks * ROWS, ROWS), :] = misc
-            out[pl.ds(tokens + (chunks + 1) * ROWS, ROWS), :] = jnp.where(mine, part, 0.0).astype(
-                jnp.bfloat16
-            )
+
+    def part(i, j):
+        start = pl.multiple_of(split_quarter(i, j) * width, LANES)
+        return jnp.where(mine, residual[:, pl.ds(start, width)], 0.0).astype(jnp.bfloat16)
+
+    out1[pl.ds(tokens + (chunks + 1) * ROWS, ROWS), :] = part(1, 1)
+    out0[pl.ds(tokens, ROWS), :] = part(1, 0)
+    extra_ref[pl.ds((chunks + 1) * ROWS, ROWS), :] = part(0, 1)
+    extra_ref[pl.ds((chunks + 2) * ROWS, ROWS), :] = part(0, 0)
+
+
+def own_kernel(
+    bounds, gathered, weight_ref, extra_ref, out1, out0, weight, weight_sems, blocks, tokens
+):
+    width = out0.shape[1]
+    chunks = tokens // CHUNK
+    copies = weight_copies(weight_ref, weight, weight_sems, 0)
+    for copy in copies:
+        copy.start()
+    for copy in copies:
+        copy.wait()
+
+    def project(k, carry):
+        start = pl.multiple_of(k * CHUNK, CHUNK)
+        x = gathered[pl.ds(start, CHUNK), :]
+        out1[pl.ds(start, CHUNK), :] = mm(x, weight[1]).astype(jnp.bfloat16)
+        out0[pl.ds(start, CHUNK), :] = mm(x, weight[0]).astype(jnp.bfloat16)
+        return carry
+
+    def zero(k, carry):
+        start = pl.multiple_of(k * CHUNK, CHUNK)
+        out1[pl.ds(start, CHUNK), :] = jnp.zeros((CHUNK, width), jnp.bfloat16)
+        out0[pl.ds(start, CHUNK), :] = jnp.zeros((CHUNK, width), jnp.bfloat16)
+        return carry
+
+    used = lax.shift_right_logical(bounds[blocks, 0] + CHUNK - 1, CHUNK_BITS)
+    lax.fori_loop(0, used, project, 0)
+    lax.fori_loop(used, chunks, zero, 0)
+    size = (chunks + 2) * ROWS
+    out1[pl.ds(tokens, size), :] = extra_ref[0:size, :]
+    out0[pl.ds(tokens, ROWS), :] = extra_ref[size : size + ROWS, :]
 
 
 def pool_kernel(
     ids_ref,
     own_ref,
     core_ref,
+    chip_ref,
     far_ref,
     member_ref,
     raise_ref,
@@ -346,15 +378,13 @@
     width = own_ref.shape[1]
     quarter = quarter_of(lax.axis_index("dp"))
 
-    def summed(start, size):
-        rows = pl.ds(start, size)
-        return (
-            own_ref[rows, :].astype(jnp.float32)
-            + core_ref[rows, :].astype(jnp.float32)
-            + far_ref[rows, :].astype(jnp.float32)
-        )
-
-    misc = summed(tokens + chunks * ROWS, ROWS)
+    def summed(*pieces):
+        return sum(ref[pl.ds(start, size), :].astype(jnp.float32) for ref, start, size in pieces)
+
+    def statistics(row):
+        return summed((chip_ref, tokens + row, ROWS), (far_ref, tokens + row, ROWS))
+
+    misc = statistics(chunks * ROWS)
     misc_ref[...] = misc
     inverse = lax.rsqrt(misc / model_width + 1e-05)
     raised[...] = jnp.zeros_like(raised)
@@ -362,21 +392,27 @@
     total = jnp.zeros((ROWS, width), jnp.float32)
     for k in range(chunks):
         scale = inverse[k : k + 1]
-        reduced = (summed(tokens + k * ROWS, ROWS) * scale).astype(jnp.bfloat16)
+        reduced = (statistics(k * ROWS) * scale).astype(jnp.bfloat16)
         reduced_ref[:, k * CHUNK : (k + 1) * CHUNK] = reduced
         stacked = jnp.concatenate(
             [reduced.astype(jnp.float32), jnp.broadcast_to(scale, (LANES - ROWS, CHUNK))]
         )
         turned = stacked.T
         low = turned.astype(jnp.bfloat16)
-        linear = summed(k * CHUNK, CHUNK) * turned[:, ROWS : ROWS + 1] + mm(low, raised[...])
+        at = k * CHUNK
+        linear = summed((own_ref, at, CHUNK), (core_ref, at, CHUNK), (far_ref, at, CHUNK))
+        linear = linear * turned[:, ROWS : ROWS + 1] + mm(low, raised[...])
         sigma = 1.0 / (1.0 + jnp.exp(-linear))
         slope_ref[pl.ds(k * CHUNK, CHUNK), :] = sigma * (1.0 + linear * (1.0 - sigma))
         member = member_ref[pl.ds(k * CHUNK, CHUNK), :].astype(jnp.float32).T
         member = member[0:ROWS].astype(jnp.bfloat16)
         high, rest = split(linear * sigma)
         total += mm(member, high) + mm(member, rest)
-    total += summed(tokens + (chunks + 1) * ROWS, ROWS)
+    total += summed(
+        (own_ref, tokens, ROWS),
+        (core_ref, tokens, ROWS),
+        (far_ref, tokens + (chunks + 1) * ROWS, ROWS),
+    )
     counts = jnp.sum((ids_ref[...] != 0).astype(jnp.float32), axis=1, keepdims=True)
     pooled = total[0:texts] / counts
     pooled = jnp.concatenate([pooled, jnp.zeros((ROWS - texts, width), jnp.float32)])
@@ -521,35 +557,58 @@
     width = part_width // shards
     rows = tokens + (chunks + 2) * ROWS
     params = pltpu.CompilerParams(vmem_limit_bytes=VMEM_BYTES)
-    half = jax.ShapeDtypeStruct((rows, width), jnp.bfloat16)
-    own0, own1, away0, away1, member = pl.pallas_call(
-        project_kernel,
-        out_shape=[half] * 4 + [jax.ShapeDtypeStruct((tokens, LANES), jnp.bfloat16)],
-        in_specs=[vmem_spec()] * 2 + [any_spec()] * 3,
-        out_specs=[vmem_spec()] * 5,
+    values, member, bounds = pl.pallas_call(
+        functools.partial(route_kernel, vocab=vocab),
+        out_shape=[
+            jax.ShapeDtypeStruct((tokens + WINDOW, LANES), jnp.int32),
+            jax.ShapeDtypeStruct((tokens, LANES), jnp.bfloat16),
+            jax.ShapeDtypeStruct((block_rows, length), jnp.int32),
+        ],
+        in_specs=[vmem_spec()],
+        out_specs=[vmem_spec()] * 3,
+        scratch_shapes=[pltpu.VMEM((texts, length), jnp.float32)],
+        compiler_params=params,
+        name="route",
+    )(ids)
+    gathered = pl.pallas_call(
+        gather_kernel,
+        out_shape=jax.ShapeDtypeStruct((tokens + WINDOW, features), jnp.bfloat16),
+        in_specs=[smem_spec(), vmem_spec(), any_spec()],
+        out_specs=vmem_spec(),
         scratch_shapes=[
             pltpu.VMEM((blocks, features, IDS_PER_BLOCK), jnp.bfloat16),
-            pltpu.VMEM((4, features, width), jnp.bfloat16),
+            pltpu.SemaphoreType.DMA((blocks,)),
+        ],
+        compiler_params=params,
+        name="gather",
+    )(bounds, values, vocabulary_vectors)
+    long = jax.ShapeDtypeStruct((rows, width), jnp.bfloat16)
+    short = jax.ShapeDtypeStruct((tokens + ROWS, width), jnp.bfloat16)
+    away1, away0, extra = pl.pallas_call(
+        functools.partial(away_kernel, blocks=blocks),
+        out_shape=[
+            long,
+            short,
+            jax.ShapeDtypeStruct(((chunks + 3) * ROWS, width), jnp.bfloat16),
+        ],
+        in_specs=[smem_spec()] + [vmem_spec()] * 3 + [any_spec()] * 2,
+        out_specs=[vmem_spec()] * 3,
+        scratch_shapes=[
+            pltpu.VMEM((2, features, width), jnp.bfloat16),
             pltpu.VMEM((rank, features), jnp.bfloat16),
-            pltpu.VMEM((tokens + WINDOW, features), jnp.bfloat16),
-            pltpu.VMEM((tokens + WINDOW, LANES), jnp.int32),
             pltpu.VMEM((LANES, LANES), jnp.float32),
-            pltpu.VMEM((texts, length), jnp.float32),
             pltpu.VMEM((8, width), jnp.float32),
             pltpu.VMEM((ROWS, features), jnp.float32),
-            pltpu.VMEM((block_rows, length), jnp.int32),
-            pltpu.SMEM((block_rows, length), jnp.int32),
-            pltpu.SemaphoreType.DMA((blocks, PIECES)),
-            pltpu.SemaphoreType.DMA((4,)),
-            pltpu.SemaphoreType.DMA,
+            pltpu.SemaphoreType.DMA((2,)),
             pltpu.SemaphoreType.DMA,
         ],
         compiler_params=params,
-        name="project",
+        name="away",
     )(
-        ids,
+        bounds,
+        gathered,
+        member,
         difficult_distractors,
-        vocabulary_vectors,
         layer_weight_matrix,
         lowering_factor_matrix,
     )
@@ -557,6 +616,21 @@
     other_y = [(d, d ^ 2) for d in range(shards)]
     core1 = lax.ppermute(away1, "dp", other_core)
     core0 = lax.ppermute(away0, "dp", other_core)
+    own1, own0 = pl.pallas_call(
+        functools.partial(own_kernel, blocks=blocks, tokens=tokens),
+        out_shape=[long, short],
+        in_specs=[smem_spec(), vmem_spec(), any_spec(), vmem_spec()],
+        out_specs=[vmem_spec()] * 2,
+        scratch_shapes=[
+            pltpu.VMEM((2, features, width), jnp.bfloat16),
+            pltpu.SemaphoreType.DMA((2,)),
+        ],
+        compiler_params=params,
+        cost_estimate=pl.CostEstimate(
+            flops=4 * tokens * features * width, bytes_accessed=8 * 2**20, transcendentals=0
+        ),
+        name="own",
+    )(bounds, gathered, layer_weight_matrix, extra)
     chip1 = (own1.astype(jnp.float32) + core1.astype(jnp.float32)).astype(jnp.bfloat16)
     far = lax.ppermute(chip1, "dp", other_y)
     pooled, slope, reduced, misc = pl.pallas_call(
@@ -567,12 +641,12 @@
             jax.ShapeDtypeStruct((ROWS, tokens), jnp.bfloat16),
             jax.ShapeDtypeStruct((ROWS, width), jnp.float32),
         ],
-        in_specs=[vmem_spec()] * 6,
+        in_specs=[vmem_spec()] * 7,
         out_specs=[vmem_spec()] * 4,
         scratch_shapes=[pltpu.VMEM((LANES, width), jnp.bfloat16)],
         compiler_params=params,
         name="pool",
-    )(ids, own0, core0, far, member, raising_factor_matrix)
+    )(ids, own0, core0, chip1, far, member, raising_factor_matrix)
     sides = ("group", "dp")
     pooled = lax.all_to_all(pooled, sides, 0, 0)
     dots = pl.pallas_call(

time: 102 us -> 108 us (1.059); the launches traced: 101 us -> 106 us
  Pallas kernels: 41.7 us -> 46.6 us
  blocking collectives: 18.3 us -> 20.4 us
  waiting for transfers between devices: 26.5 us -> 24.5 us
    pallas_call x1 -> x4, Pallas kernels: 32 us -> 36.7 us  [the longest x1 19 us: split_body(): pl.pallas_call(gather_kernel, out_shape=jax.ShapeDtypeStruct((tokens + WI...]
    ppermute x1, waiting for transfers between devices: 2.14 us -> 0.01 us  [split_body(): core1 = lax.ppermute(away1, 'dp', other_core)]
    all_to_all x1, blocking collectives: 9.81 us -> 11.9 us  [split_body(): pooled = lax.all_to_all(pooled, sides, 0, 0)]
    ppermute x1, waiting for transfers between devices: 0.01 us -> 2.08 us  [split_body(): core0 = lax.ppermute(away0, 'dp', other_core)]
    ppermute x1, waiting for transfers between devices: 19.2 us -> 17.3 us  [split_body(): far = lax.ppermute(chip1, 'dp', other_y)]
    unnamed x7 -> x11, local copies, waits for them, and re-layouts: 2.84 us -> 2.85 us
  transfers between devices with their start and end apart: 4 -> 4, of which waited for: 3 -> 3; matrix products, arithmetic and copies ran while one was open for 1% -> 0% of each run, Pallas kernels for 0% -> 6%
where the time goes in v6:
time: 108 us; the launch traced here: 106 us
  Pallas kernels  46.6 us (43%)
  waiting for transfers between devices  24.5 us (23%)
  blocking collectives  20.4 us (19%)
  starting transfers between devices  8.19 us (8%)
  local copies, waits for them, and re-layouts  2.85 us (3%)
  other arithmetic  2.09 us (2%)
  between operations  1.34 us (1%)
    pallas_call x1, Pallas kernels, split_body(): pl.pallas_call(gather_kernel, out_shape=jax.ShapeDtypeStruct((tokens + WI...  19 us
    ppermute x1, waiting for transfers between devices, split_body(): far = lax.ppermute(chip1, 'dp', other_y)  17.3 us
    all_to_all x1, blocking collectives, split_body(): pooled = lax.all_to_all(pooled, sides, 0, 0)  11.9 us
    all_to_all x1, blocking collectives, split_body(): update = lax.all_to_all(update, sides, 0, 0)  8.45 us
    pallas_call x1, Pallas kernels, split_body(): pl.pallas_call(functools.partial(away_kernel, blocks=blocks), out_shape=[...  7.5 us
    pallas_call x1, Pallas kernels, split_body(): pl.pallas_call(functools.partial(own_kernel, blocks=blocks, tokens=tokens...  6.18 us
    all_to_all x1, waiting for transfers between devices, split_body(): dots = lax.all_to_all(dots, 'mp', 0, 0)  5.09 us
    all_to_all x1, starting transfers between devices, split_body(): dots = lax.all_to_all(dots, 'mp', 0, 0)  4.87 us
  transfers between devices with their start and end apart: 4, of which 3 were waited for; matrix products, arithmetic and copies ran while one was open for 0% of the time, Pallas kernels for 6%

profile of v6, /device:TPU:0, one launch (start us, length us, event | category | flops | bytes accessed | tf_op | source)
XLA Modules:
  0.0 106.0 jit_solution(18434256127016689162)
XLA Ops:
  0.6 1.3 %copy.12 = s32[1,12,128]{2,1,0:T(8,128)} copy(s32[1,12,128]{2,0,1:T(1,128)} %param.7) | data formatting | bytes 12288
  1.9 4.0 %route.1 = (s32[1600,128]{1,0:T(8,128)}, bf16[1536,128]{1,0:T(8,128)(2,1)}, s32[24,128]{1,0:T(8,128)}) custom-call(s32[12,128]{1,0:T(8,128)} %bitcast.11), custom_call_target="tpu_custom_call" | custom-call | tf_op jit(solution)/shard_map/route/pallas_call | solution.py:560
  5.9 19.0 %gather.1.gathered = bf16[1600,1024]{1,0:T(8,128)(2,1)} custom-call(s32[24,128]{1,0:T(8,128)} %get-tuple-element.18.bounds, s32[1600,128]{1,0:T(8,128)} %get-tuple-element.19.values_ref, bf16[1024,16384]{1,0:T(8,128)(2,1)} %vocab_ref.1), custom_call_target="tpu_custom_call" | custom-call | tf_op jit(solution)/shard_map/gather/pallas_call | solution.py:573
  25.0 7.5 %away.1 = (bf16[1664,256]{1,0:T(8,128)(2,1)}, bf16[1552,256]{1,0:T(8,128)(2,1)}, bf16[144,256]{1,0:T(8,128)(2,1)}) custom-call(s32[24,128]{1,0:T(8,128)} %get-tuple-element.18.bounds, bf16[1600,1024]{1,0:T(8,128)(2,1)} %gather.1.gathered, bf16[1536,128]{1,0:T(8,128)(2,1)} %get-tuple-element.20.member_ref, s32[3,7]{1,0:T(4,128)} %hard_ref.1, ...), custom_call_target="tpu_custom_call" | custom-call | tf_op jit(solution)/shard_map/away/pallas_call | solution.py:587
  32.5 0.5 collective-permute-start.1
  33.0 6.2 %own.1 = (bf16[1664,256]{1,0:T(8,128)(2,1)}, bf16[1552,256]{1,0:T(8,128)(2,1)}) custom-call(s32[24,128]{1,0:T(8,128)} %get-tuple-element.18.bounds, bf16[1600,1024]{1,0:T(8,128)(2,1)} %gather.1.gathered, bf16[1024,1024]{1,0:T(8,128)(2,1)} %weight_ref.3, bf16[144,256]{1,0:T(8,128)(2,1)} %get-tuple-element.21.extra_ref), custom_call_target="tpu_custom_call" | custom-call | flops 1610612736 | bytes 8388608 | tf_op jit(solution)/shard_map/own/pallas_call | solution.py:619
  39.2 0.0 copy-start.4
  39.2 0.0 collective-permute-done.1
  39.2 1.4 %add_convert_fusion.chip_ref = bf16[1664,256]{1,0:T(8,128)(2,1)S(1)} fusion(bf16[1664,256]{1,0:T(8,128)(2,1)S(1)} %collective-permute-done.1, bf16[1664,256]{1,0:T(8,128)(2,1)} %get-tuple-element.24), kind=kLoop, calls=%fused_computation | loop fusion | flops 1703936 | bytes 2555904 | tf_op jit(solution)/shard_map/convert_element_type | solution.py:634
  40.7 0.0 copy-start
  40.7 2.6 %collective-permute-start.2 = (bf16[1664,256]{1,0:T(8,128)(2,1)S(1)}, bf16[1664,256]{1,0:T(8,128)(2,1)S(1)}, u32[]{:S(2)}, u32[]{:S(2)}) collective-permute-start(bf16[1664,256]{1,0:T(8,128)(2,1)S(1)} %add_convert_fusion.chip_ref), channel_id=1, source_target_pairs={{0,8},{4,12},{8,0},{12,4},{1,9},{5,13},{9,1},{13,5},{2,10},{6,14},... | collective-permute-start | bytes 2555912 | tf_op jit(solution)/shard_map/ppermute | solution.py:635
  43.3 0.2 collective-permute-start
  43.5 2.1 %collective-permute-done.core_ref = bf16[1552,256]{1,0:T(8,128)(2,1)S(1)} collective-permute-done((bf16[1552,256]{1,0:T(8,128)(2,1)S(1)}, bf16[1552,256]{1,0:T(8,128)(2,1)S(1)}, u32[]{:S(2)}, u32[]{:S(2)}) %collective-permute-start) | collective-permute-done | bytes 794656 | tf_op jit(solution)/shard_map/ppermute | solution.py:618
  45.6 17.3 %collective-permute-done.2.far_ref = bf16[1664,256]{1,0:T(8,128)(2,1)S(1)} collective-permute-done((bf16[1664,256]{1,0:T(8,128)(2,1)S(1)}, bf16[1664,256]{1,0:T(8,128)(2,1)S(1)}, u32[]{:S(2)}, u32[]{:S(2)}) %collective-permute-start.2) | collective-permute-done | bytes 852000 | tf_op jit(solution)/shard_map/ppermute | solution.py:635
  62.9 0.9 copy-done.1
  63.8 4.5 %pool.1 = (bf16[8,16,256]{2,1,0:T(8,128)(2,1)}, f32[1536,256]{1,0:T(8,128)}, bf16[16,1536]{1,0:T(8,128)(2,1)}, f32[16,256]{1,0:T(8,128)}) custom-call(s32[12,128]{1,0:T(8,128)} %bitcast.12, bf16[1552,256]{1,0:T(8,128)(2,1)} %get-tuple-element.22.own_ref, bf16[1552,256]{1,0:T(8,128)(2,1)} %copy-done.2, bf16[1664,256]{1,0:T(8,128)(2,1)} %copy-done, ...), custom_call_target="tpu_custom_call" | custom-call | tf_op jit(solution)/shard_map/pool/pallas_call | solution.py:636
  68.3 11.9 %all_to_all.15.pooled_ref = bf16[8,16,256]{2,1,0:T(8,128)(2,1)} all-to-all(bf16[8,16,256]{2,1,0:T(8,128)(2,1)} %get-tuple-element.26), channel_id=1, replica_groups=mesh['group'=2,'dp'=4,'mp'=4] {'group','dp'}, dimensions={0} | all-to-all | bytes 131072 | tf_op jit(solution)/shard_map/all_to_all | solution.py:651
  80.2 1.6 %dots.1 = f32[4,32,128]{2,1,0:T(8,128)} custom-call(bf16[8,16,256]{2,1,0:T(8,128)(2,1)} %all_to_all.15.pooled_ref), custom_call_target="tpu_custom_call" | custom-call | tf_op jit(solution)/shard_map/dots/pallas_call | solution.py:652
  81.9 4.9 %all-to-all-start.1 = ((f32[4,32,128]{2,1,0:T(8,128)}), f32[4,32,128]{2,1,0:T(8,128)S(1)}, u32[]{:S(2)}, u32[]{:S(2)}) async-start(f32[4,32,128]{2,1,0:T(8,128)} %dots.1), calls=%async_computation.1 | async-start | bytes 131072 | tf_op jit(solution)/shard_map/all_to_all | solution.py:660
  87.4 5.1 %all-to-all-done.1.dots_ref = f32[4,32,128]{2,1,0:T(8,128)S(1)} async-done(((f32[4,32,128]{2,1,0:T(8,128)}), f32[4,32,128]{2,1,0:T(8,128)S(1)}, u32[]{:S(2)}, u32[]{:S(2)}) %all-to-all-start.1) | async-done | bytes 65568 | tf_op jit(solution)/shard_map/all_to_all | solution.py:660
  92.5 0.6 copy-done.3
  93.1 3.8 %score.1 = (bf16[1,3,1024]{2,1,0:T(4,128)(2,1)}, f32[1,3]{1,0:T(1,128)}, f32[8,16,256]{2,1,0:T(8,128)}) custom-call(s32[12,128]{1,0:T(8,128)} %bitcast.13, bf16[8,16,256]{2,1,0:T(8,128)(2,1)} %all_to_all.15.pooled_ref, f32[4,32,128]{2,1,0:T(8,128)} %copy-done.3, f32[16,256]{1,0:T(8,128)} %get-tuple-element.27.misc_ref, ...), custom_call_target="tpu_custom_call" | custom-call | tf_op jit(solution)/shard_map/score/pallas_call | solution.py:661
  96.9 8.5 %all_to_all.16 = f32[8,16,256]{2,1,0:T(8,128)S(1)} all-to-all(f32[8,16,256]{2,1,0:T(8,128)} %get-tuple-element.32), channel_id=1, replica_groups=mesh['group'=2,'dp'=4,'mp'=4] {'group','dp'}, dimensions={0} | all-to-all | bytes 262144 | tf_op jit(solution)/shard_map/all_to_all | solution.py:673
  105.3 0.6 pad_maximum_fusion
  (7 shorter events, 0.0 us)
Async XLA Ops:
  32.5 6.7 %collective-permute-start.1 = (bf16[1664,256]{1,0:T(8,128)(2,1)}, bf16[1664,256]{1,0:T(8,128)(2,1)S(1)}, u32[]{:S(2)}, u32[]{:S(2)}) collective-permute-start(bf16[1664,256]{1,0:T(8,128)(2,1)} %get-tuple-element.25), channel_id=1, source_target_pairs={{0,4},{4,0},{8,12},{12,8},{1,5},{5,1},{9,13},{13,9},{2,6},{6,2},{1... | collective-permute-start | bytes 2555912 | tf_op jit(solution)/shard_map/ppermute | solution.py:617
  39.2 4.1 %copy-start.4 = (bf16[1552,256]{1,0:T(8,128)(2,1)S(1)}, bf16[1552,256]{1,0:T(8,128)(2,1)}, u32[]{:S(2)}) copy-start(bf16[1552,256]{1,0:T(8,128)(2,1)} %get-tuple-element.23) | copy-start | bytes 2383876
  40.7 22.2 %copy-start = (bf16[1664,256]{1,0:T(8,128)(2,1)}, bf16[1664,256]{1,0:T(8,128)(2,1)S(1)}, u32[]{:S(2)}) copy-start(bf16[1664,256]{1,0:T(8,128)(2,1)S(1)} %add_convert_fusion.chip_ref) | copy-start | bytes 2555908
  40.7 22.2 %collective-permute-start.2 = (bf16[1664,256]{1,0:T(8,128)(2,1)S(1)}, bf16[1664,256]{1,0:T(8,128)(2,1)S(1)}, u32[]{:S(2)}, u32[]{:S(2)}) collective-permute-start(bf16[1664,256]{1,0:T(8,128)(2,1)S(1)} %add_convert_fusion.chip_ref), channel_id=1, source_target_pairs={{0,8},{4,12},{8,0},{12,4},{1,9},{5,13},{9,1},{13,5},{2,10},{6,14},... | collective-permute-start | bytes 2555912 | tf_op jit(solution)/shard_map/ppermute | solution.py:635
  43.3 2.3 %collective-permute-start = (bf16[1552,256]{1,0:T(8,128)(2,1)S(1)}, bf16[1552,256]{1,0:T(8,128)(2,1)S(1)}, u32[]{:S(2)}, u32[]{:S(2)}) collective-permute-start(bf16[1552,256]{1,0:T(8,128)(2,1)S(1)} %copy-done.4), channel_id=1, source_target_pairs={{0,4},{4,0},{8,12},{12,8},{1,5},{5,1},{9,13},{13,9},{2,6},{6,2},{1... | collective-permute-start | bytes 2383880 | tf_op jit(solution)/shard_map/ppermute | solution.py:618
  45.6 17.3 %copy-start.2 = (bf16[1552,256]{1,0:T(8,128)(2,1)}, bf16[1552,256]{1,0:T(8,128)(2,1)S(1)}, u32[]{:S(2)}) copy-start(bf16[1552,256]{1,0:T(8,128)(2,1)S(1)} %collective-permute-done.core_ref) | copy-start | bytes 2383876
  62.9 0.9 copy-start.1
  81.9 10.6 %all-to-all-start.1 = ((f32[4,32,128]{2,1,0:T(8,128)}), f32[4,32,128]{2,1,0:T(8,128)S(1)}, u32[]{:S(2)}, u32[]{:S(2)}) async-start(f32[4,32,128]{2,1,0:T(8,128)} %dots.1), calls=%async_computation.1 | async-start | bytes 131072 | tf_op jit(solution)/shard_map/all_to_all | solution.py:660
  92.5 0.6 copy-start.3

commit v7 on v6

--- a/solution.py
+++ b/solution.py
@@ -191,7 +191,7 @@
         return pltpu.make_async_copy(vocab_ref.at[:, columns], held.at[b], held_sems.at[b])
 
     for b in range(blocks):
-        vocab_copy(b).start()
+        vocab_copy(b).start(priority=b % 2)
 
     def clear(p, carry):
         at = pl.multiple_of(p * WINDOW, WINDOW)

time: 108 us -> 117 us (1.083)
  Pallas kernels: 46.6 us -> 55.3 us
    pallas_call x1, Pallas kernels: 19 us -> 27.8 us  [split_body(): pl.pallas_call(gather_kernel, out_shape=jax.ShapeDtypeStruct((tokens + WI...]
  transfers between devices with their start and end apart: 4 -> 4, of which waited for: 3 -> 3; matrix products, arithmetic and copies ran while one was open for 0% -> 0% of each run, Pallas kernels for 6% -> 5%
where the time goes in v7:
time: 117 us; the launch traced here: 116 us
  Pallas kernels  55.3 us (47%)
  waiting for transfers between devices  24.5 us (21%)
  blocking collectives  21.5 us (18%)
  starting transfers between devices  8.2 us (7%)
  local copies, waits for them, and re-layouts  2.85 us (2%)
  other arithmetic  2.09 us (2%)
  between operations  1.34 us (1%)
    pallas_call x1, Pallas kernels, split_body(): pl.pallas_call(gather_kernel, out_shape=jax.ShapeDtypeStruct((tokens + WI...  27.8 us
    ppermute x1, waiting for transfers between devices, split_body(): far = lax.ppermute(chip1, 'dp', other_y)  17.3 us
    all_to_all x1, blocking collectives, split_body(): pooled = lax.all_to_all(pooled, sides, 0, 0)  13.1 us
    all_to_all x1, blocking collectives, split_body(): update = lax.all_to_all(update, sides, 0, 0)  8.45 us
    pallas_call x1, Pallas kernels, split_body(): pl.pallas_call(functools.partial(away_kernel, blocks=blocks), out_shape=[...  7.5 us
    pallas_call x1, Pallas kernels, split_body(): pl.pallas_call(functools.partial(own_kernel, blocks=blocks, tokens=tokens...  6.18 us
    all_to_all x1, waiting for transfers between devices, split_body(): dots = lax.all_to_all(dots, 'mp', 0, 0)  5.09 us
    all_to_all x1, starting transfers between devices, split_body(): dots = lax.all_to_all(dots, 'mp', 0, 0)  4.87 us
  transfers between devices with their start and end apart: 4, of which 3 were waited for; matrix products, arithmetic and copies ran while one was open for 0% of the time, Pallas kernels for 5%

profile of v7, /device:TPU:0, one launch (start us, length us, event | category | flops | bytes accessed | tf_op | source)
XLA Modules:
  0.0 115.8 jit_solution(12543455947791535171)
XLA Ops:
  0.6 1.3 %copy.12 = s32[1,12,128]{2,1,0:T(8,128)} copy(s32[1,12,128]{2,0,1:T(1,128)} %param.7) | data formatting | bytes 12288
  1.9 4.0 %route.1 = (s32[1600,128]{1,0:T(8,128)}, bf16[1536,128]{1,0:T(8,128)(2,1)}, s32[24,128]{1,0:T(8,128)}) custom-call(s32[12,128]{1,0:T(8,128)} %bitcast.11), custom_call_target="tpu_custom_call" | custom-call | tf_op jit(solution)/shard_map/route/pallas_call | solution.py:560
  5.9 27.8 %gather.1.gathered = bf16[1600,1024]{1,0:T(8,128)(2,1)} custom-call(s32[24,128]{1,0:T(8,128)} %get-tuple-element.18.bounds, s32[1600,128]{1,0:T(8,128)} %get-tuple-element.19.values_ref, bf16[1024,16384]{1,0:T(8,128)(2,1)} %vocab_ref.1), custom_call_target="tpu_custom_call" | custom-call | tf_op jit(solution)/shard_map/gather/pallas_call | solution.py:573
  33.7 7.5 %away.1 = (bf16[1664,256]{1,0:T(8,128)(2,1)}, bf16[1552,256]{1,0:T(8,128)(2,1)}, bf16[144,256]{1,0:T(8,128)(2,1)}) custom-call(s32[24,128]{1,0:T(8,128)} %get-tuple-element.18.bounds, bf16[1600,1024]{1,0:T(8,128)(2,1)} %gather.1.gathered, bf16[1536,128]{1,0:T(8,128)(2,1)} %get-tuple-element.20.member_ref, s32[3,7]{1,0:T(4,128)} %hard_ref.1, ...), custom_call_target="tpu_custom_call" | custom-call | tf_op jit(solution)/shard_map/away/pallas_call | solution.py:587
  41.2 0.5 collective-permute-start.1
  41.7 6.2 %own.1 = (bf16[1664,256]{1,0:T(8,128)(2,1)}, bf16[1552,256]{1,0:T(8,128)(2,1)}) custom-call(s32[24,128]{1,0:T(8,128)} %get-tuple-element.18.bounds, bf16[1600,1024]{1,0:T(8,128)(2,1)} %gather.1.gathered, bf16[1024,1024]{1,0:T(8,128)(2,1)} %weight_ref.3, bf16[144,256]{1,0:T(8,128)(2,1)} %get-tuple-element.21.extra_ref), custom_call_target="tpu_custom_call" | custom-call | flops 1610612736 | bytes 8388608 | tf_op jit(solution)/shard_map/own/pallas_call | solution.py:619
  47.9 0.0 copy-start.4
  47.9 0.0 collective-permute-done.1
  47.9 1.4 %add_convert_fusion.chip_ref = bf16[1664,256]{1,0:T(8,128)(2,1)S(1)} fusion(bf16[1664,256]{1,0:T(8,128)(2,1)S(1)} %collective-permute-done.1, bf16[1664,256]{1,0:T(8,128)(2,1)} %get-tuple-element.24), kind=kLoop, calls=%fused_computation | loop fusion | flops 1703936 | bytes 2555904 | tf_op jit(solution)/shard_map/convert_element_type | solution.py:634
  49.4 2.6 %collective-permute-start.2 = (bf16[1664,256]{1,0:T(8,128)(2,1)S(1)}, bf16[1664,256]{1,0:T(8,128)(2,1)S(1)}, u32[]{:S(2)}, u32[]{:S(2)}) collective-permute-start(bf16[1664,256]{1,0:T(8,128)(2,1)S(1)} %add_convert_fusion.chip_ref), channel_id=1, source_target_pairs={{0,8},{4,12},{8,0},{12,4},{1,9},{5,13},{9,1},{13,5},{2,10},{6,14},... | collective-permute-start | bytes 2555912 | tf_op jit(solution)/shard_map/ppermute | solution.py:635
  52.0 0.0 copy-done.4
  52.0 0.2 collective-permute-start
  52.2 2.1 %collective-permute-done.core_ref = bf16[1552,256]{1,0:T(8,128)(2,1)S(1)} collective-permute-done((bf16[1552,256]{1,0:T(8,128)(2,1)S(1)}, bf16[1552,256]{1,0:T(8,128)(2,1)S(1)}, u32[]{:S(2)}, u32[]{:S(2)}) %collective-permute-start) | collective-permute-done | bytes 794656 | tf_op jit(solution)/shard_map/ppermute | solution.py:618
  54.3 17.3 %collective-permute-done.2.far_ref = bf16[1664,256]{1,0:T(8,128)(2,1)S(1)} collective-permute-done((bf16[1664,256]{1,0:T(8,128)(2,1)S(1)}, bf16[1664,256]{1,0:T(8,128)(2,1)S(1)}, u32[]{:S(2)}, u32[]{:S(2)}) %collective-permute-start.2) | collective-permute-done | bytes 852000 | tf_op jit(solution)/shard_map/ppermute | solution.py:635
  71.6 0.9 copy-done.1
  72.5 4.5 %pool.1 = (bf16[8,16,256]{2,1,0:T(8,128)(2,1)}, f32[1536,256]{1,0:T(8,128)}, bf16[16,1536]{1,0:T(8,128)(2,1)}, f32[16,256]{1,0:T(8,128)}) custom-call(s32[12,128]{1,0:T(8,128)} %bitcast.12, bf16[1552,256]{1,0:T(8,128)(2,1)} %get-tuple-element.22.own_ref, bf16[1552,256]{1,0:T(8,128)(2,1)} %copy-done.2, bf16[1664,256]{1,0:T(8,128)(2,1)} %copy-done, ...), custom_call_target="tpu_custom_call" | custom-call | tf_op jit(solution)/shard_map/pool/pallas_call | solution.py:636
  77.0 13.1 %all_to_all.15.pooled_ref = bf16[8,16,256]{2,1,0:T(8,128)(2,1)} all-to-all(bf16[8,16,256]{2,1,0:T(8,128)(2,1)} %get-tuple-element.26), channel_id=1, replica_groups=mesh['group'=2,'dp'=4,'mp'=4] {'group','dp'}, dimensions={0} | all-to-all | bytes 131072 | tf_op jit(solution)/shard_map/all_to_all | solution.py:651
  90.1 1.6 %dots.1 = f32[4,32,128]{2,1,0:T(8,128)} custom-call(bf16[8,16,256]{2,1,0:T(8,128)(2,1)} %all_to_all.15.pooled_ref), custom_call_target="tpu_custom_call" | custom-call | tf_op jit(solution)/shard_map/dots/pallas_call | solution.py:652
  91.7 4.9 %all-to-all-start.1 = ((f32[4,32,128]{2,1,0:T(8,128)}), f32[4,32,128]{2,1,0:T(8,128)S(1)}, u32[]{:S(2)}, u32[]{:S(2)}) async-start(f32[4,32,128]{2,1,0:T(8,128)} %dots.1), calls=%async_computation.1 | async-start | bytes 131072 | tf_op jit(solution)/shard_map/all_to_all | solution.py:660
  97.2 5.1 %all-to-all-done.1.dots_ref = f32[4,32,128]{2,1,0:T(8,128)S(1)} async-done(((f32[4,32,128]{2,1,0:T(8,128)}), f32[4,32,128]{2,1,0:T(8,128)S(1)}, u32[]{:S(2)}, u32[]{:S(2)}) %all-to-all-start.1) | async-done | bytes 65568 | tf_op jit(solution)/shard_map/all_to_all | solution.py:660
  102.3 0.6 copy-done.3
  103.0 3.8 %score.1 = (bf16[1,3,1024]{2,1,0:T(4,128)(2,1)}, f32[1,3]{1,0:T(1,128)}, f32[8,16,256]{2,1,0:T(8,128)}) custom-call(s32[12,128]{1,0:T(8,128)} %bitcast.13, bf16[8,16,256]{2,1,0:T(8,128)(2,1)} %all_to_all.15.pooled_ref, f32[4,32,128]{2,1,0:T(8,128)} %copy-done.3, f32[16,256]{1,0:T(8,128)} %get-tuple-element.27.misc_ref, ...), custom_call_target="tpu_custom_call" | custom-call | tf_op jit(solution)/shard_map/score/pallas_call | solution.py:661
  106.7 8.5 %all_to_all.16 = f32[8,16,256]{2,1,0:T(8,128)S(1)} all-to-all(f32[8,16,256]{2,1,0:T(8,128)} %get-tuple-element.32), channel_id=1, replica_groups=mesh['group'=2,'dp'=4,'mp'=4] {'group','dp'}, dimensions={0} | all-to-all | bytes 262144 | tf_op jit(solution)/shard_map/all_to_all | solution.py:673
  115.2 0.6 pad_maximum_fusion
  (7 shorter events, 0.0 us)
Async XLA Ops:
  41.2 6.7 %collective-permute-start.1 = (bf16[1664,256]{1,0:T(8,128)(2,1)}, bf16[1664,256]{1,0:T(8,128)(2,1)S(1)}, u32[]{:S(2)}, u32[]{:S(2)}) collective-permute-start(bf16[1664,256]{1,0:T(8,128)(2,1)} %get-tuple-element.25), channel_id=1, source_target_pairs={{0,4},{4,0},{8,12},{12,8},{1,5},{5,1},{9,13},{13,9},{2,6},{6,2},{1... | collective-permute-start | bytes 2555912 | tf_op jit(solution)/shard_map/ppermute | solution.py:617
  47.9 4.1 %copy-start.4 = (bf16[1552,256]{1,0:T(8,128)(2,1)S(1)}, bf16[1552,256]{1,0:T(8,128)(2,1)}, u32[]{:S(2)}) copy-start(bf16[1552,256]{1,0:T(8,128)(2,1)} %get-tuple-element.23) | copy-start | bytes 2383876
  49.4 22.2 %copy-start = (bf16[1664,256]{1,0:T(8,128)(2,1)}, bf16[1664,256]{1,0:T(8,128)(2,1)S(1)}, u32[]{:S(2)}) copy-start(bf16[1664,256]{1,0:T(8,128)(2,1)S(1)} %add_convert_fusion.chip_ref) | copy-start | bytes 2555908
  49.4 22.2 %collective-permute-start.2 = (bf16[1664,256]{1,0:T(8,128)(2,1)S(1)}, bf16[1664,256]{1,0:T(8,128)(2,1)S(1)}, u32[]{:S(2)}, u32[]{:S(2)}) collective-permute-start(bf16[1664,256]{1,0:T(8,128)(2,1)S(1)} %add_convert_fusion.chip_ref), channel_id=1, source_target_pairs={{0,8},{4,12},{8,0},{12,4},{1,9},{5,13},{9,1},{13,5},{2,10},{6,14},... | collective-permute-start | bytes 2555912 | tf_op jit(solution)/shard_map/ppermute | solution.py:635
  52.0 2.3 %collective-permute-start = (bf16[1552,256]{1,0:T(8,128)(2,1)S(1)}, bf16[1552,256]{1,0:T(8,128)(2,1)S(1)}, u32[]{:S(2)}, u32[]{:S(2)}) collective-permute-start(bf16[1552,256]{1,0:T(8,128)(2,1)S(1)} %copy-done.4), channel_id=1, source_target_pairs={{0,4},{4,0},{8,12},{12,8},{1,5},{5,1},{9,13},{13,9},{2,6},{6,2},{1... | collective-permute-start | bytes 2383880 | tf_op jit(solution)/shard_map/ppermute | solution.py:618
  54.3 17.3 %copy-start.2 = (bf16[1552,256]{1,0:T(8,128)(2,1)}, bf16[1552,256]{1,0:T(8,128)(2,1)S(1)}, u32[]{:S(2)}) copy-start(bf16[1552,256]{1,0:T(8,128)(2,1)S(1)} %collective-permute-done.core_ref) | copy-start | bytes 2383876
  71.6 0.9 copy-start.1
  91.7 10.6 %all-to-all-start.1 = ((f32[4,32,128]{2,1,0:T(8,128)}), f32[4,32,128]{2,1,0:T(8,128)S(1)}, u32[]{:S(2)}, u32[]{:S(2)}) async-start(f32[4,32,128]{2,1,0:T(8,128)} %dots.1), calls=%async_computation.1 | async-start | bytes 131072 | tf_op jit(solution)/shard_map/all_to_all | solution.py:660
  102.3 0.6 copy-start.3

commit v8 on v6

--- a/solution.py
+++ b/solution.py
@@ -110,12 +110,12 @@
     return (embeddings, losses[None], adapter_up_gradient)
 
 
-BLOCK_BITS, WINDOW_BITS, CHUNK_BITS, ROW_BITS = 10, 6, 8, 4
+BLOCK_BITS, CHUNK_BITS, LANE_BITS, ROW_BITS = 10, 8, 7, 4
 IDS_PER_BLOCK = 1 << BLOCK_BITS
-WINDOW = 1 << WINDOW_BITS
 CHUNK = 1 << CHUNK_BITS
 ROWS = 1 << ROW_BITS
-LANES = 128
+LANES = 1 << LANE_BITS
+FEATURE_ROWS = 256
 NT = (((1,), (1,)), ((), ()))
 VMEM_BYTES = 60 * 1024 * 1024
 
@@ -137,7 +137,7 @@
     return (dp_index % cores) * 2 + dp_index // cores
 
 
-def route_kernel(ids_ref, values_ref, member_ref, bounds_ref, ranks, vocab):
+def route_kernel(ids_ref, token_ref, member_ref, bounds_ref, ranks, vocab):
     texts, length = ids_ref.shape
     tokens = texts * length
     blocks = vocab // IDS_PER_BLOCK
@@ -172,19 +172,31 @@
         found = found.astype(jnp.int32)
         token = lax.shift_right_logical(found, ROW_BITS)
         start = pl.multiple_of(p * LANES, LANES)
-        values_ref[pl.ds(start, LANES), :] = jnp.where(token == 0, -vocab, token)
+        flat = jnp.where(token == 0, -vocab, token).astype(jnp.float32).T
+        token_ref[pl.ds(p, 1), :] = flat[0:1].astype(jnp.int32)
         real = (token != 0) & ((found & (ROWS - 1)) == iota((LANES, LANES), 1))
         member_ref[pl.ds(start, LANES), :] = jnp.where(real, 1.0, 0.0).astype(jnp.bfloat16)
         return carry
 
     lax.fori_loop(0, tokens // LANES, place, 0)
-    values_ref[pl.ds(tokens, WINDOW), :] = jnp.full((WINDOW, LANES), -vocab, jnp.int32)
-
-
-def gather_kernel(bounds, values_ref, vocab_ref, gathered, held, held_sems):
+
+
+def take_lanes(x, lanes):
+    numbers = lax.GatherDimensionNumbers(
+        offset_dims=(),
+        collapsed_slice_dims=(1,),
+        start_index_map=(1,),
+        operand_batching_dims=(0,),
+        start_indices_batching_dims=(0,),
+    )
+    mode = lax.GatherScatterMode.PROMISE_IN_BOUNDS
+    return lax.gather(x, lanes[..., None], numbers, slice_sizes=(1, 1), mode=mode)
+
+
+def gather_kernel(bounds, token_ref, vocab_ref, gathered, held, turned, held_sems):
     features, vocab = vocab_ref.shape
     blocks = vocab // IDS_PER_BLOCK
-    rows = gathered.shape[0]
+    windows = gathered.shape[0] // LANES
 
     def vocab_copy(b):
         columns = pl.ds(pl.multiple_of(b * IDS_PER_BLOCK, LANES), IDS_PER_BLOCK)
@@ -194,34 +206,43 @@
         vocab_copy(b).start()
 
     def clear(p, carry):
-        at = pl.multiple_of(p * WINDOW, WINDOW)
-        gathered[pl.ds(at, WINDOW), :] = jnp.zeros((WINDOW, features), jnp.bfloat16)
+        at = pl.multiple_of(p * LANES, LANES)
+        turned[:, pl.ds(at, LANES)] = jnp.zeros((features, LANES), jnp.bfloat16)
         return carry
 
-    lax.fori_loop(0, rows // WINDOW, clear, 0)
+    lax.fori_loop(0, windows, clear, 0)
 
     def take(b, carry):
         first, last = bounds[b, 0], bounds[b + 1, 0]
-        aligned = lax.shift_left(lax.shift_right_logical(first, ROW_BITS), ROW_BITS)
-        windows = lax.shift_right_logical(last - aligned + WINDOW - 1, WINDOW_BITS)
-        windows = jnp.where(last > first, windows, 0)
+        begin = lax.shift_right_logical(first, LANE_BITS)
+        end = lax.shift_right_logical(last + LANES - 1, LANE_BITS)
         vocab_copy(b).wait()
 
-        def window(w, carry):
-            start = pl.multiple_of(aligned + w * WINDOW, ROWS)
-            wanted = values_ref[pl.ds(start, WINDOW), :]
-            wanted -= b * IDS_PER_BLOCK + iota((WINDOW, LANES), 1)
-            picked = [
-                jnp.where(wanted == j * LANES, 1.0, 0.0).astype(jnp.bfloat16)
-                for j in range(IDS_PER_BLOCK // LANES)
-            ]
-            found = mm(jnp.concatenate(picked, axis=1), held[b], NT)
-            gathered[pl.ds(start, WINDOW), :] += found.astype(jnp.bfloat16)
+        def window(p, carry):
+            at = pl.ds(pl.multiple_of(p * LANES, LANES), LANES)
+            token = token_ref[pl.ds(p, 1), :] - b * IDS_PER_BLOCK
+            token = jnp.broadcast_to(token, (FEATURE_ROWS, LANES))
+            lane = (token & (LANES - 1)).astype(jnp.int16)
+            tile = lax.shift_right_arithmetic(token, LANE_BITS).astype(jnp.int16)
+            for f in range(features // FEATURE_ROWS):
+                rows = pl.ds(f * FEATURE_ROWS, FEATURE_ROWS)
+                total = turned[rows, at]
+                for j in range(IDS_PER_BLOCK // LANES):
+                    found = take_lanes(held[b, rows, j * LANES : (j + 1) * LANES], lane)
+                    total = jnp.where(tile == j, found, total)
+                turned[rows, at] = total
             return carry
 
-        return lax.fori_loop(0, windows, window, carry)
+        return lax.fori_loop(begin, jnp.where(last > first, end, begin), window, carry)
 
     lax.fori_loop(0, blocks, take, 0)
+
+    def turn(p, carry):
+        at = pl.ds(pl.multiple_of(p * LANES, LANES), LANES)
+        gathered[at, :] = turned[:, at].astype(jnp.float32).T.astype(jnp.bfloat16)
+        return carry
+
+    lax.fori_loop(0, windows, turn, 0)
 
 
 def split_quarter(i, j, cores=2):
@@ -557,10 +578,10 @@
     width = part_width // shards
     rows = tokens + (chunks + 2) * ROWS
     params = pltpu.CompilerParams(vmem_limit_bytes=VMEM_BYTES)
-    values, member, bounds = pl.pallas_call(
+    token, member, bounds = pl.pallas_call(
         functools.partial(route_kernel, vocab=vocab),
         out_shape=[
-            jax.ShapeDtypeStruct((tokens + WINDOW, LANES), jnp.int32),
+            jax.ShapeDtypeStruct((tokens // LANES, LANES), jnp.int32),
             jax.ShapeDtypeStruct((tokens, LANES), jnp.bfloat16),
             jax.ShapeDtypeStruct((block_rows, length), jnp.int32),
         ],
@@ -572,16 +593,17 @@
     )(ids)
     gathered = pl.pallas_call(
         gather_kernel,
-        out_shape=jax.ShapeDtypeStruct((tokens + WINDOW, features), jnp.bfloat16),
+        out_shape=jax.ShapeDtypeStruct((tokens, features), jnp.bfloat16),
         in_specs=[smem_spec(), vmem_spec(), any_spec()],
         out_specs=vmem_spec(),
         scratch_shapes=[
             pltpu.VMEM((blocks, features, IDS_PER_BLOCK), jnp.bfloat16),
+            pltpu.VMEM((features, tokens), jnp.bfloat16),
             pltpu.SemaphoreType.DMA((blocks,)),
         ],
         compiler_params=params,
         name="gather",
-    )(bounds, values, vocabulary_vectors)
+    )(bounds, token, vocabulary_vectors)
     long = jax.ShapeDtypeStruct((rows, width), jnp.bfloat16)
     short = jax.ShapeDtypeStruct((tokens + ROWS, width), jnp.bfloat16)
     away1, away0, extra = pl.pallas_call(

time: 108 us -> 105 us (0.972); the launches traced: 106 us -> 104 us
  blocking collectives: 20.4 us -> 17.3 us
  Pallas kernels: 46.6 us -> 48 us
    all_to_all x1, blocking collectives: 11.9 us -> 8.89 us  [split_body(): pooled = lax.all_to_all(pooled, sides, 0, 0)]
    pallas_call x1, Pallas kernels: 19 us -> 20.4 us  [split_body(): pl.pallas_call(gather_kernel, out_shape=jax.ShapeDtypeStruct((tokens, fea...]
where the time goes in v8:
time: 105 us; the launch traced here: 104 us
  Pallas kernels  48 us (46%)
  waiting for transfers between devices  24.5 us (23%)
  blocking collectives  17.3 us (16%)
  starting transfers between devices  8.32 us (8%)
  local copies, waits for them, and re-layouts  2.85 us (3%)
  other arithmetic  2.09 us (2%)
  between operations  1.34 us (1%)
    pallas_call x1, Pallas kernels, split_body(): pl.pallas_call(gather_kernel, out_shape=jax.ShapeDtypeStruct((tokens, fea...  20.4 us
    ppermute x1, waiting for transfers between devices, split_body(): far = lax.ppermute(chip1, 'dp', other_y)  17.3 us
    all_to_all x1, blocking collectives, split_body(): pooled = lax.all_to_all(pooled, sides, 0, 0)  8.89 us
    all_to_all x1, blocking collectives, split_body(): update = lax.all_to_all(update, sides, 0, 0)  8.45 us
    pallas_call x1, Pallas kernels, split_body(): pl.pallas_call(functools.partial(away_kernel, blocks=blocks), out_shape=[...  7.45 us
    pallas_call x1, Pallas kernels, split_body(): pl.pallas_call(functools.partial(own_kernel, blocks=blocks, tokens=tokens...  6.13 us
    all_to_all x1, waiting for transfers between devices, split_body(): dots = lax.all_to_all(dots, 'mp', 0, 0)  5.09 us
    all_to_all x1, starting transfers between devices, split_body(): dots = lax.all_to_all(dots, 'mp', 0, 0)  4.99 us
  transfers between devices with their start and end apart: 4, of which 3 were waited for; matrix products, arithmetic and copies ran while one was open for 0% of the time, Pallas kernels for 6%

profile of v8, /device:TPU:0, one launch (start us, length us, event | category | flops | bytes accessed | tf_op | source)
XLA Modules:
  0.0 104.5 jit_solution(16584684456647840740)
XLA Ops:
  0.6 1.3 %copy.12 = s32[1,12,128]{2,1,0:T(8,128)} copy(s32[1,12,128]{2,0,1:T(1,128)} %param.7) | data formatting | bytes 12288
  1.9 4.2 %route.1 = (s32[12,128]{1,0:T(8,128)}, bf16[1536,128]{1,0:T(8,128)(2,1)}, s32[24,128]{1,0:T(8,128)}) custom-call(s32[12,128]{1,0:T(8,128)} %bitcast.11), custom_call_target="tpu_custom_call" | custom-call | tf_op jit(solution)/shard_map/route/pallas_call | solution.py:581
  6.1 20.4 %gather.1.gathered = bf16[1536,1024]{1,0:T(8,128)(2,1)} custom-call(s32[24,128]{1,0:T(8,128)} %get-tuple-element.18.bounds, s32[12,128]{1,0:T(8,128)} %get-tuple-element.19.token_ref, bf16[1024,16384]{1,0:T(8,128)(2,1)} %vocab_ref.1), custom_call_target="tpu_custom_call" | custom-call | tf_op jit(solution)/shard_map/gather/pallas_call | solution.py:594
  26.5 7.5 %away.1 = (bf16[1664,256]{1,0:T(8,128)(2,1)}, bf16[1552,256]{1,0:T(8,128)(2,1)}, bf16[144,256]{1,0:T(8,128)(2,1)}) custom-call(s32[24,128]{1,0:T(8,128)} %get-tuple-element.18.bounds, bf16[1536,1024]{1,0:T(8,128)(2,1)} %gather.1.gathered, bf16[1536,128]{1,0:T(8,128)(2,1)} %get-tuple-element.20.member_ref, s32[3,7]{1,0:T(4,128)} %hard_ref.1, ...), custom_call_target="tpu_custom_call" | custom-call | tf_op jit(solution)/shard_map/away/pallas_call | solution.py:609
  34.0 0.5 collective-permute-start.1
  34.5 6.1 %own.1 = (bf16[1664,256]{1,0:T(8,128)(2,1)}, bf16[1552,256]{1,0:T(8,128)(2,1)}) custom-call(s32[24,128]{1,0:T(8,128)} %get-tuple-element.18.bounds, bf16[1536,1024]{1,0:T(8,128)(2,1)} %gather.1.gathered, bf16[1024,1024]{1,0:T(8,128)(2,1)} %weight_ref.3, bf16[144,256]{1,0:T(8,128)(2,1)} %get-tuple-element.21.extra_ref), custom_call_target="tpu_custom_call" | custom-call | flops 1610612736 | bytes 8388608 | tf_op jit(solution)/shard_map/own/pallas_call | solution.py:641
  40.6 0.0 copy-start.4
  40.6 0.0 collective-permute-done.1
  40.7 1.4 %add_convert_fusion.chip_ref = bf16[1664,256]{1,0:T(8,128)(2,1)S(1)} fusion(bf16[1664,256]{1,0:T(8,128)(2,1)S(1)} %collective-permute-done.1, bf16[1664,256]{1,0:T(8,128)(2,1)} %get-tuple-element.24), kind=kLoop, calls=%fused_computation | loop fusion | flops 1703936 | bytes 2555904 | tf_op jit(solution)/shard_map/convert_element_type | solution.py:656
  42.1 2.6 %collective-permute-start.2 = (bf16[1664,256]{1,0:T(8,128)(2,1)S(1)}, bf16[1664,256]{1,0:T(8,128)(2,1)S(1)}, u32[]{:S(2)}, u32[]{:S(2)}) collective-permute-start(bf16[1664,256]{1,0:T(8,128)(2,1)S(1)} %add_convert_fusion.chip_ref), channel_id=1, source_target_pairs={{0,8},{4,12},{8,0},{12,4},{1,9},{5,13},{9,1},{13,5},{2,10},{6,14},... | collective-permute-start | bytes 2555912 | tf_op jit(solution)/shard_map/ppermute | solution.py:657
  44.7 0.2 collective-permute-start
  44.9 2.1 %collective-permute-done.core_ref = bf16[1552,256]{1,0:T(8,128)(2,1)S(1)} collective-permute-done((bf16[1552,256]{1,0:T(8,128)(2,1)S(1)}, bf16[1552,256]{1,0:T(8,128)(2,1)S(1)}, u32[]{:S(2)}, u32[]{:S(2)}) %collective-permute-start) | collective-permute-done | bytes 794656 | tf_op jit(solution)/shard_map/ppermute | solution.py:640
  47.0 17.3 %collective-permute-done.2.far_ref = bf16[1664,256]{1,0:T(8,128)(2,1)S(1)} collective-permute-done((bf16[1664,256]{1,0:T(8,128)(2,1)S(1)}, bf16[1664,256]{1,0:T(8,128)(2,1)S(1)}, u32[]{:S(2)}, u32[]{:S(2)}) %collective-permute-start.2) | collective-permute-done | bytes 852000 | tf_op jit(solution)/shard_map/ppermute | solution.py:657
  64.3 0.0 copy-done.2
  64.3 0.9 copy-done.1
  65.2 4.5 %pool.1 = (bf16[8,16,256]{2,1,0:T(8,128)(2,1)}, f32[1536,256]{1,0:T(8,128)}, bf16[16,1536]{1,0:T(8,128)(2,1)}, f32[16,256]{1,0:T(8,128)}) custom-call(s32[12,128]{1,0:T(8,128)} %bitcast.12, bf16[1552,256]{1,0:T(8,128)(2,1)} %get-tuple-element.22.own_ref, bf16[1552,256]{1,0:T(8,128)(2,1)} %copy-done.2, bf16[1664,256]{1,0:T(8,128)(2,1)} %copy-done, ...), custom_call_target="tpu_custom_call" | custom-call | tf_op jit(solution)/shard_map/pool/pallas_call | solution.py:658
  69.7 8.9 %all_to_all.15.pooled_ref = bf16[8,16,256]{2,1,0:T(8,128)(2,1)} all-to-all(bf16[8,16,256]{2,1,0:T(8,128)(2,1)} %get-tuple-element.26), channel_id=1, replica_groups=mesh['group'=2,'dp'=4,'mp'=4] {'group','dp'}, dimensions={0} | all-to-all | bytes 131072 | tf_op jit(solution)/shard_map/all_to_all | solution.py:673
  78.6 1.6 %dots.1 = f32[4,32,128]{2,1,0:T(8,128)} custom-call(bf16[8,16,256]{2,1,0:T(8,128)(2,1)} %all_to_all.15.pooled_ref), custom_call_target="tpu_custom_call" | custom-call | tf_op jit(solution)/shard_map/dots/pallas_call | solution.py:674
  80.2 5.0 %all-to-all-start.1 = ((f32[4,32,128]{2,1,0:T(8,128)}), f32[4,32,128]{2,1,0:T(8,128)S(1)}, u32[]{:S(2)}, u32[]{:S(2)}) async-start(f32[4,32,128]{2,1,0:T(8,128)} %dots.1), calls=%async_computation.1 | async-start | bytes 131072 | tf_op jit(solution)/shard_map/all_to_all | solution.py:682
  85.9 5.1 %all-to-all-done.1.dots_ref = f32[4,32,128]{2,1,0:T(8,128)S(1)} async-done(((f32[4,32,128]{2,1,0:T(8,128)}), f32[4,32,128]{2,1,0:T(8,128)S(1)}, u32[]{:S(2)}, u32[]{:S(2)}) %all-to-all-start.1) | async-done | bytes 65568 | tf_op jit(solution)/shard_map/all_to_all | solution.py:682
  91.0 0.6 copy-done.3
  91.6 3.8 %score.1 = (bf16[1,3,1024]{2,1,0:T(4,128)(2,1)}, f32[1,3]{1,0:T(1,128)}, f32[8,16,256]{2,1,0:T(8,128)}) custom-call(s32[12,128]{1,0:T(8,128)} %bitcast.13, bf16[8,16,256]{2,1,0:T(8,128)(2,1)} %all_to_all.15.pooled_ref, f32[4,32,128]{2,1,0:T(8,128)} %copy-done.3, f32[16,256]{1,0:T(8,128)} %get-tuple-element.27.misc_ref, ...), custom_call_target="tpu_custom_call" | custom-call | tf_op jit(solution)/shard_map/score/pallas_call | solution.py:683
  95.4 8.5 %all_to_all.16 = f32[8,16,256]{2,1,0:T(8,128)S(1)} all-to-all(f32[8,16,256]{2,1,0:T(8,128)} %get-tuple-element.32), channel_id=1, replica_groups=mesh['group'=2,'dp'=4,'mp'=4] {'group','dp'}, dimensions={0} | all-to-all | bytes 262144 | tf_op jit(solution)/shard_map/all_to_all | solution.py:695
  103.8 0.6 pad_maximum_fusion
  (7 shorter events, 0.0 us)
Async XLA Ops:
  34.0 6.7 %collective-permute-start.1 = (bf16[1664,256]{1,0:T(8,128)(2,1)}, bf16[1664,256]{1,0:T(8,128)(2,1)S(1)}, u32[]{:S(2)}, u32[]{:S(2)}) collective-permute-start(bf16[1664,256]{1,0:T(8,128)(2,1)} %get-tuple-element.25), channel_id=1, source_target_pairs={{0,4},{4,0},{8,12},{12,8},{1,5},{5,1},{9,13},{13,9},{2,6},{6,2},{1... | collective-permute-start | bytes 2555912 | tf_op jit(solution)/shard_map/ppermute | solution.py:639
  40.6 4.1 %copy-start.4 = (bf16[1552,256]{1,0:T(8,128)(2,1)S(1)}, bf16[1552,256]{1,0:T(8,128)(2,1)}, u32[]{:S(2)}) copy-start(bf16[1552,256]{1,0:T(8,128)(2,1)} %get-tuple-element.23) | copy-start | bytes 2383876
  42.1 22.2 %copy-start = (bf16[1664,256]{1,0:T(8,128)(2,1)}, bf16[1664,256]{1,0:T(8,128)(2,1)S(1)}, u32[]{:S(2)}) copy-start(bf16[1664,256]{1,0:T(8,128)(2,1)S(1)} %add_convert_fusion.chip_ref) | copy-start | bytes 2555908
  42.1 22.2 %collective-permute-start.2 = (bf16[1664,256]{1,0:T(8,128)(2,1)S(1)}, bf16[1664,256]{1,0:T(8,128)(2,1)S(1)}, u32[]{:S(2)}, u32[]{:S(2)}) collective-permute-start(bf16[1664,256]{1,0:T(8,128)(2,1)S(1)} %add_convert_fusion.chip_ref), channel_id=1, source_target_pairs={{0,8},{4,12},{8,0},{12,4},{1,9},{5,13},{9,1},{13,5},{2,10},{6,14},... | collective-permute-start | bytes 2555912 | tf_op jit(solution)/shard_map/ppermute | solution.py:657
  44.7 2.3 %collective-permute-start = (bf16[1552,256]{1,0:T(8,128)(2,1)S(1)}, bf16[1552,256]{1,0:T(8,128)(2,1)S(1)}, u32[]{:S(2)}, u32[]{:S(2)}) collective-permute-start(bf16[1552,256]{1,0:T(8,128)(2,1)S(1)} %copy-done.4), channel_id=1, source_target_pairs={{0,4},{4,0},{8,12},{12,8},{1,5},{5,1},{9,13},{13,9},{2,6},{6,2},{1... | collective-permute-start | bytes 2383880 | tf_op jit(solution)/shard_map/ppermute | solution.py:640
  47.0 17.3 %copy-start.2 = (bf16[1552,256]{1,0:T(8,128)(2,1)}, bf16[1552,256]{1,0:T(8,128)(2,1)S(1)}, u32[]{:S(2)}) copy-start(bf16[1552,256]{1,0:T(8,128)(2,1)S(1)} %collective-permute-done.core_ref) | copy-start | bytes 2383876
  64.3 0.9 copy-start.1
  80.2 10.7 %all-to-all-start.1 = ((f32[4,32,128]{2,1,0:T(8,128)}), f32[4,32,128]{2,1,0:T(8,128)S(1)}, u32[]{:S(2)}, u32[]{:S(2)}) async-start(f32[4,32,128]{2,1,0:T(8,128)} %dots.1), calls=%async_computation.1 | async-start | bytes 131072 | tf_op jit(solution)/shard_map/all_to_all | solution.py:682
  91.0 0.6 copy-start.3
